TPU v7x, 32 devices: a whole 2x2x4 slice. The times are simulated.
32 devices in a mesh: band: 4 (over x, core), mesh: 8 (over z, y).
Axes of the slice: x: 2, y: 2, z: 4, core: 2. Of those that a mesh axis runs over, the one named last changes fastest.
Arguments:
- grid_vars: bfloat16 [32768, 227], P(('band', 'mesh')), may hold values from -6 to 6
- mesh_latent: bfloat16 [10240, 512], P(('band', 'mesh')), may hold values from -6 to 6
- cotangent: bfloat16 [10240, 512], P(('band', 'mesh')), may hold values from -6 to 6
- edge_grid: int32 [131072], P(('band', 'mesh')), may hold values from 0 to 32767, as said below
- edge_mesh: int32 [131072], P(('band', 'mesh')), may hold values from 0 to 10239, as said below
- w_in: bfloat16 [227, 512], replicated, may hold values from -0.375 to 0.375
- b_in: float32 [512], replicated, may hold values from -4 to 4
- w_out: bfloat16 [512, 512], replicated, may hold values from -0.25 to 0.25
- norm_gain: float32 [512], replicated, may hold values from 0.1 to 1.9
- u_grid: bfloat16 [512, 512], replicated, may hold values from -0.25 to 0.25
- u_mesh: bfloat16 [512, 512], replicated, may hold values from -0.25 to 0.25
- b_edge: float32 [512], replicated, may hold values from -4 to 4
- w_edge: bfloat16 [512, 512], replicated, may hold values from -0.25 to 0.25
- w_self: bfloat16 [512, 512], replicated, may hold values from -0.25 to 0.25
- w_agg: bfloat16 [512, 512], replicated, may hold values from -0.1875 to 0.1875
- b_node: float32 [512], replicated, may hold values from -4 to 4
- w_node_out: bfloat16 [512, 512], replicated, may hold values from -0.25 to 0.25
Outputs:
- mesh_out: bfloat16 [10240, 512], P(('band', 'mesh'))
- grad_mesh: bfloat16 [10240, 512], P(('band', 'mesh'))
- grad_edge: float32 [512, 512], replicated
- grad_ugrid: float32 [512, 512], replicated
- grad_umesh: float32 [512, 512], replicated
Inputs may be any that keep to these rules, and one draw needn't show every extreme that they name: `edge_grid`: the edges of one device (aligned blocks of 4096) have grid nodes among that device's 1024 grid nodes. `edge_mesh`: the edges of one device have mesh nodes among the 2560 mesh nodes of the device's band (the nodes of the 8 devices of that band), in nondecreasing order within the device's block. One device's edges reach at most 48 distinct mesh nodes owned by any one device (blocks of 320 mesh nodes); this most is reached in every draw.
All inputs are finite; a program needn't handle non-finite values.
Results may differ from a plain program's by a relative error of at most 0.013.
The roundings to bfloat16 on the way count: a program that leaves them out, or rounds other values in their place, can miss the bound.
Values may be sent and summed in bfloat16 or wider, within the bound.
No kernel may reach another device: no remote copies, remote signals or barrier semaphores. Data moves between devices by JAX's collectives and lax.ppermute only.
A program may use at most 192 MiB of HBM per device.

v0:
```python
import jax
import jax.numpy as jnp
from jax import lax
from jax.sharding import PartitionSpec as P

CAP = 48


def swish(v):
    return v * jax.nn.sigmoid(v)


def swish_grad(v):
    s = jax.nn.sigmoid(v)
    return s * (1.0 + v * (1.0 - s))


def layer_norm(v, gain):
    mean = jnp.mean(v, axis=-1, keepdims=True)
    centred = v - mean
    var = jnp.mean(centred * centred, axis=-1, keepdims=True)
    return centred * lax.rsqrt(var + 1e-05) * gain


def matmul(a, b):
    return jnp.dot(a, b, preferred_element_type=jnp.float32)


def window_take(table, ranks, block):
    width = table.shape[1]
    padded = jnp.concatenate([table, jnp.zeros((block, width), table.dtype)], axis=0)
    blocks = ranks.reshape(-1, block)
    columns = jnp.arange(block, dtype=jnp.int32)[None, :]

    def one_block(rank_block):
        base = rank_block[0]
        window = lax.dynamic_slice_in_dim(padded, base, block, 0)
        onehot = ((rank_block - base)[:, None] == columns).astype(table.dtype)
        return matmul(onehot, window).astype(table.dtype)

    return lax.map(one_block, blocks).reshape(-1, width)


def window_add(values, ranks, block, rows):
    width = values.shape[1]
    blocks = ranks.reshape(-1, block)
    value_blocks = values.reshape(-1, block, width)
    columns = jnp.arange(block, dtype=jnp.int32)[None, :]

    def one_block(index, total):
        rank_block = blocks[index]
        base = rank_block[0]
        onehot = ((rank_block - base)[:, None] == columns).astype(values.dtype)
        contrib = lax.dot_general(
            onehot,
            value_blocks[index],
            (((0,), (0,)), ((), ())),
            preferred_element_type=jnp.float32,
        )
        current = lax.dynamic_slice_in_dim(total, base, block, 0)
        return lax.dynamic_update_slice_in_dim(total, current + contrib, base, 0)

    total = lax.fori_loop(
        0, blocks.shape[0], one_block, jnp.zeros((rows + block, width), jnp.float32)
    )
    return total[:rows]


def grid_take(table, local_ids, block):
    blocks = local_ids.reshape(-1, block)
    columns = jnp.arange(table.shape[0], dtype=jnp.int32)[None, :]

    def one_block(id_block):
        onehot = (id_block[:, None] == columns).astype(table.dtype)
        return matmul(onehot, table).astype(table.dtype)

    return lax.map(one_block, blocks).reshape(-1, table.shape[1])


def grid_add(values, local_ids, block, rows):
    width = values.shape[1]
    blocks = local_ids.reshape(-1, block)
    value_blocks = values.reshape(-1, block, width)
    columns = jnp.arange(rows, dtype=jnp.int32)[None, :]

    def one_block(index, total):
        onehot = (blocks[index][:, None] == columns).astype(values.dtype)
        return total + lax.dot_general(
            onehot,
            value_blocks[index],
            (((0,), (0,)), ((), ())),
            preferred_element_type=jnp.float32,
        )

    return lax.fori_loop(0, blocks.shape[0], one_block, jnp.zeros((rows, width), jnp.float32))


def shards(
    grid_vars,
    mesh_latent,
    cotangent,
    edge_grid,
    edge_mesh,
    w_in,
    b_in,
    w_out,
    norm_gain,
    u_grid,
    u_mesh,
    b_edge,
    w_edge,
    w_self,
    w_agg,
    b_node,
    w_node_out,
):
    grid_dev = grid_vars.shape[0]
    mesh_dev = mesh_latent.shape[0]
    edge_dev = edge_grid.shape[0]
    width = mesh_latent.shape[1]
    owners = lax.axis_size("mesh")
    band_rows_count = owners * mesh_dev
    compact = owners * CAP
    block = min(512, edge_dev)
    device = lax.axis_index("band") * owners + lax.axis_index("mesh")
    grid_local = edge_grid - device * grid_dev
    mesh_local = edge_mesh - lax.axis_index("band") * band_rows_count
    fresh = jnp.concatenate(
        [jnp.ones((1,), jnp.int32), (mesh_local[1:] != mesh_local[:-1]).astype(jnp.int32)]
    )
    rank = jnp.cumsum(fresh) - 1
    node_of = jnp.full((compact,), band_rows_count, jnp.int32).at[rank].min(mesh_local, mode="drop")
    hidden = swish(matmul(grid_vars, w_in) + b_in).astype(jnp.bfloat16)
    latent = layer_norm(matmul(hidden, w_out), norm_gain).astype(jnp.bfloat16)
    proj_grid = matmul(latent, u_grid).astype(jnp.bfloat16)
    proj_mesh = matmul(mesh_latent, u_mesh).astype(jnp.bfloat16)
    edge_pgrid = grid_take(proj_grid, grid_local, block)
    owner = mesh_local // mesh_dev
    owner_ids = jnp.arange(owners, dtype=jnp.int32)[:, None]
    starts = jnp.sum(jnp.where(owner[None, :] < owner_ids, fresh[None, :], 0), axis=1)
    first = jnp.sum(jnp.where(owner[None, :] == owner_ids, starts[:, None], 0), axis=0)
    slot = owner * CAP + rank - first
    slot_of = jnp.full((compact,), compact, jnp.int32).at[rank].min(slot, mode="drop")
    ids = jnp.zeros((compact,), jnp.int32).at[slot_of].add(node_of % mesh_dev, mode="drop")
    incoming = lax.all_to_all(
        ids.reshape(owners, CAP), "mesh", split_axis=0, concat_axis=0, tiled=True
    ).reshape(-1)
    asked = proj_mesh[incoming].reshape(owners, CAP, width)
    answered = lax.all_to_all(asked, "mesh", split_axis=0, concat_axis=0, tiled=True).reshape(
        compact, width
    )
    compact_pmesh = answered.at[slot_of].get(mode="fill", fill_value=0)
    edge_pmesh = window_take(compact_pmesh, rank, block)
    pre = edge_pgrid.astype(jnp.float32) + edge_pmesh.astype(jnp.float32) + b_edge
    act = swish(pre).astype(jnp.bfloat16)
    message = matmul(act, w_edge).astype(jnp.bfloat16)
    compact_sums = window_add(message, rank, block, compact)
    partial_value = (
        jnp.zeros((compact, width), jnp.float32).at[slot_of].add(compact_sums, mode="drop")
    )
    received = lax.all_to_all(
        partial_value.reshape(owners, CAP, width), "mesh", split_axis=0, concat_axis=0, tiled=True
    ).reshape(compact, width)
    agg = jax.ops.segment_sum(received, incoming, num_segments=mesh_dev)
    agg = agg.astype(jnp.bfloat16)
    node_pre = matmul(mesh_latent, w_self) + matmul(agg, w_agg) + b_node
    node_act = swish(node_pre).astype(jnp.bfloat16)
    mesh_out = (mesh_latent.astype(jnp.float32) + matmul(node_act, w_node_out)).astype(jnp.bfloat16)
    g_node = (matmul(cotangent, w_node_out.T) * swish_grad(node_pre)).astype(jnp.bfloat16)
    g_agg = matmul(g_node, w_agg.T).astype(jnp.bfloat16)
    grad_asked = g_agg[incoming].reshape(owners, CAP, width)
    grad_answered = lax.all_to_all(
        grad_asked, "mesh", split_axis=0, concat_axis=0, tiled=True
    ).reshape(compact, width)
    compact_grads = grad_answered.at[slot_of].get(mode="fill", fill_value=0)
    g_msg = window_take(compact_grads, rank, block)
    local_edge = matmul(act.T, g_msg)
    g_edge = (matmul(g_msg, w_edge.T) * swish_grad(pre)).astype(jnp.bfloat16)
    g_pgrid = grid_add(g_edge, grid_local, block, grid_dev).astype(jnp.bfloat16)
    compact_gsums = window_add(g_edge, rank, block, compact)
    grad_partial = (
        jnp.zeros((compact, width), jnp.float32).at[slot_of].add(compact_gsums, mode="drop")
    )
    grad_received = lax.all_to_all(
        grad_partial.reshape(owners, CAP, width), "mesh", split_axis=0, concat_axis=0, tiled=True
    ).reshape(compact, width)
    g_pmesh = jax.ops.segment_sum(grad_received, incoming, num_segments=mesh_dev)
    g_pmesh = g_pmesh.astype(jnp.bfloat16)
    local_ugrid = matmul(latent.T, g_pgrid)
    local_umesh = matmul(mesh_latent.T, g_pmesh)
    summed_edge, summed_ugrid, summed_umesh = lax.psum(
        (local_edge, local_ugrid, local_umesh), ("band", "mesh")
    )
    scale = (edge_dev * lax.axis_size("band") * owners) ** (-0.5)
    grad_mesh = (
        cotangent.astype(jnp.float32) + matmul(g_node, w_self.T) + matmul(g_pmesh, u_mesh.T)
    ).astype(jnp.bfloat16)
    return (mesh_out, grad_mesh, summed_edge * scale, summed_ugrid * scale, summed_umesh * scale)


def solution(mesh):
    return jax.shard_map(
        shards,
        mesh=mesh,
        in_specs=(
            P(("band", "mesh"), None),
            P(("band", "mesh"), None),
            P(("band", "mesh"), None),
            P(("band", "mesh")),
            P(("band", "mesh")),
            P(),
            P(),
            P(),
            P(),
            P(),
            P(),
            P(),
            P(),
            P(),
            P(),
            P(),
            P(),
        ),
        out_specs=(P(("band", "mesh"), None), P(("band", "mesh"), None), P(), P(), P()),
        check_vma=False,
    )
```

profile of v0, /device:TPU:0, one launch (start us, length us, event | category | flops | bytes accessed | tf_op | source)
XLA Modules:
  0.0 568.9 jit_solution(7292715392566975957)
XLA Ops:
  9.1 28.8 %scatter_custom_fusion.1 = s32[384]{0:T(512)S(1)} fusion(s32[4096]{0:T(1024)S(1)} %bitcast.140, s32[4096]{0:T(1024)S(1)} %get-tuple-element.495, s32[]{:T(128)} %constant.172.clone.1), kind=kCustom, calls=%fused_computation.147 | custom fusion | flops 4096 | bytes 1540 | tf_op jit(solution)/shard_map/scatter-min | solution.py:132
  37.9 28.8 %scatter_custom_fusion = s32[384]{0:T(512)S(1)} fusion(s32[4096]{0:T(1024)S(1)} %bitcast.141, s32[4096]{0:T(1024)S(1)} %get-tuple-element.492, s32[]{:T(128)} %constant.169.clone.1), kind=kCustom, calls=%fused_computation.149 | custom fusion | flops 4096 | bytes 1540 | tf_op jit(solution)/shard_map/scatter-min | solution.py:143
  66.7 3.9 scatter_custom_fusion.2
  71.3 7.3 %all-to-all-start = ((s32[8,1,48]{2,1,0:T(1,128)}), s32[8,1,48]{2,1,0:T(1,128)S(1)}, u32[]{:S(2)}, u32[]{:S(2)}) async-start(s32[8,1,48]{2,1,0:T(1,128)} %all_to_all.18), calls=%async_computation | async-start | bytes 8192 | tf_op jit(solution)/shard_map/all_to_all | solution.py:145
  88.9 6.3 %all-to-all-start.1 = ((bf16[8,48,512]{2,1,0:T(8,128)(2,1)}), bf16[8,48,512]{2,1,0:T(8,128)(2,1)S(1)}, u32[]{:S(2)}, u32[]{:S(2)}) async-start(bf16[8,48,512]{2,1,0:T(8,128)(2,1)} %bitcast.6), calls=%async_computation.1 | async-start | bytes 786432 | tf_op jit(solution)/shard_map/all_to_all | solution.py:149
  97.6 12.5 %while.75 = (s32[]{:T(128)}, bf16[8,512,512]{2,1,0:T(8,128)(2,1)}, s32[8,512]{1,0:T(8,128)S(1)}, bf16[1024,512]{1,0:T(8,128)(2,1)S(1)}, s32[]{:T(128)}) while((s32[]{:T(128)}, bf16[8,512,512]{2,1,0:T(8,128)(2,1)}, s32[8,512]{1,0:T(8,128)S(1)}, bf16[1024,512]{1,0:T(8,128)(2,1)S(1)}, s32[]{:T(128)}) %tuple.170), condition=%wide.region_10.11_spmd.clone, body=%wide.region_9.10_spmd.clone.sunk | while | flops 537657344 | bytes 1579585 | solution.py:77
  114.9 35.4 %while.76 = (s32[]{:T(128)}, bf16[8,512,512]{2,1,0:T(8,128)(2,1)}, s32[8,512]{1,0:T(8,128)S(1)}, bf16[896,512]{1,0:T(8,128)(2,1)S(1)}, s32[]{:T(128)}, /*index=5*/s32[]{:T(128)}, s32[]{:T(128)}) while((s32[]{:T(128)}, bf16[8,512,512]{2,1,0:T(8,128)(2,1)}, s32[8,512]{1,0:T(8,128)S(1)}, bf16[896,512]{1,0:T(8,128)(2,1)S(1)}, ...), condition=%wide.region_12.13_spmd.clone, body=%wide.region_11.12_spmd.clone.sunk | while | flops 268960256 | bytes 1055367 | solution.py:41
  150.3 4.8 convert_add_fusion
  158.6 4.3 convolution_convert_fusion.2
  163.1 45.7 %while.77 = (s32[]{:T(128)}, f32[896,512]{1,0:T(8,128)S(1)}, s32[8,512]{1,0:T(8,128)S(1)}, bf16[8,512,512]{2,1,0:T(8,128)(2,1)}, s32[]{:T(128)}, /*index=5*/s32[]{:T(128)}, s32[]{:T(128)}) while((s32[]{:T(128)}, f32[896,512]{1,0:T(8,128)S(1)}, s32[8,512]{1,0:T(8,128)S(1)}, bf16[8,512,512]{2,1,0:T(8,128)(2,1)}, s32[]{:T(128)}, ...), condition=%wide.region_14.15_spmd.clone, body=%wide.region_13.14_spmd.clone.sunk | while | flops 268960256 | bytes 4725387 | solution.py:63
  208.8 3.8 scatter_custom_fusion.3
  212.6 6.2 %all-to-all-start.2 = ((f32[8,48,512]{2,1,0:T(8,128)}), f32[8,48,512]{2,1,0:T(8,128)S(1)}, u32[]{:S(2)}, u32[]{:S(2)}) async-start(f32[8,48,512]{2,1,0:T(8,128)} %bitcast.10), calls=%async_computation.2 | async-start | bytes 1572864 | tf_op jit(solution)/shard_map/all_to_all | solution.py:161
  221.5 16.4 %all-to-all-done.2 = f32[8,48,512]{2,1,0:T(8,128)S(1)} async-done(((f32[8,48,512]{2,1,0:T(8,128)}), f32[8,48,512]{2,1,0:T(8,128)S(1)}, u32[]{:S(2)}, u32[]{:S(2)}) %all-to-all-start.2) | async-done | bytes 786464 | tf_op jit(solution)/shard_map/all_to_all | solution.py:161
  238.8 3.6 scatter_custom_fusion.4
  251.6 11.6 %all-to-all-done.3 = bf16[8,48,512]{2,1,0:T(8,128)(2,1)S(1)} async-done(((bf16[8,48,512]{2,1,0:T(8,128)(2,1)}), bf16[8,48,512]{2,1,0:T(8,128)(2,1)S(1)}, u32[]{:S(2)}, u32[]{:S(2)}) %all-to-all-start.3) | async-done | bytes 393248 | tf_op jit(solution)/shard_map/all_to_all | solution.py:172
  268.7 35.4 %while.78 = (s32[]{:T(128)}, bf16[8,512,512]{2,1,0:T(8,128)(2,1)}, s32[8,512]{1,0:T(8,128)S(1)}, bf16[896,512]{1,0:T(8,128)(2,1)S(1)}, s32[]{:T(128)}, /*index=5*/s32[]{:T(128)}, s32[]{:T(128)}) while((s32[]{:T(128)}, bf16[8,512,512]{2,1,0:T(8,128)(2,1)}, s32[8,512]{1,0:T(8,128)S(1)}, bf16[896,512]{1,0:T(8,128)(2,1)S(1)}, ...), condition=%wide.region_18.19_spmd.clone, body=%wide.region_17.18_spmd.clone.sunk | while | flops 268960256 | bytes 1055367 | solution.py:41
  304.1 8.4 %multiply_convert_fusion.1 = bf16[4096,512]{1,0:T(8,128)(2,1)} fusion(f32[8,512,512]{2,1,0:T(8,128)} %copy-done.2, bf16[4096,512]{1,0:T(8,128)(2,1)} %bitcast.127, bf16[512,512]{1,0:T(8,128)(2,1)S(1)} %copy-done, f32[512]{0:T(512)} %param.40), kind=kOutput, calls=%fused_computation.68 | convolution fusion | flops 2168455168 | bytes 17303552 | tf_op jit(solution)/shard_map/dot_general | solution.py:26
  312.5 24.6 %while.80 = (s32[]{:T(128)}, f32[1024,512]{1,0:T(8,128)S(1)}, s32[8,512]{1,0:T(8,128)}, bf16[8,512,512]{2,1,0:T(8,128)(2,1)}, s32[]{:T(128)}, /*index=5*/s32[]{:T(128)}) while((s32[]{:T(128)}, f32[1024,512]{1,0:T(8,128)S(1)}, s32[8,512]{1,0:T(8,128)}, bf16[8,512,512]{2,1,0:T(8,128)(2,1)}, s32[]{:T(128)}, ...), condition=%wide.region_25.26_spmd.clone, body=%wide.region_24.25_spmd.clone.sunk | while | flops 538443776 | bytes 4725331 | solution.py:95
  340.7 45.7 %while.79 = (s32[]{:T(128)}, f32[896,512]{1,0:T(8,128)S(1)}, s32[8,512]{1,0:T(8,128)S(1)}, bf16[8,512,512]{2,1,0:T(8,128)(2,1)}, s32[]{:T(128)}, /*index=5*/s32[]{:T(128)}, s32[]{:T(128)}) while((s32[]{:T(128)}, f32[896,512]{1,0:T(8,128)S(1)}, s32[8,512]{1,0:T(8,128)S(1)}, bf16[8,512,512]{2,1,0:T(8,128)(2,1)}, s32[]{:T(128)}, ...), condition=%wide.region_20.21_spmd.clone, body=%wide.region_19.20_spmd.clone.sunk | while | flops 268960256 | bytes 4725387 | solution.py:63
  386.4 3.9 scatter_custom_fusion.5
  390.3 3.6 all-to-all-start.4
  394.2 8.8 %fusion.41 = f32[512,512]{1,0:T(8,128)} fusion(bf16[8,512,512]{2,1,0:T(8,128)(2,1)} %get-tuple-element.371, f32[512]{0:T(512)S(1)} %copy-done.29, bf16[8,512,512]{2,1,0:T(8,128)(2,1)} %get-tuple-element.369, bf16[8,512,512]{2,1,0:T(8,128)(2,1)} %get-tuple-element.368), kind=kOutput, calls=%fused_computation.79 | convolution fusion | flops 2166358016 | bytes 13633536 | tf_op jit(solution)/shard_map/dot_general | solution.py:26
  402.9 10.6 %all-to-all-done.4 = f32[8,48,512]{2,1,0:T(8,128)S(1)} async-done(((f32[8,48,512]{2,1,0:T(8,128)}), f32[8,48,512]{2,1,0:T(8,128)S(1)}, u32[]{:S(2)}, u32[]{:S(2)}) %all-to-all-start.4) | async-done | bytes 786464 | tf_op jit(solution)/shard_map/all_to_all | solution.py:184
  422.1 133.7 %all-reduce.5.cloned.1.call-done = (f32[512,512]{1,0:T(8,128)}, f32[512,512]{1,0:T(8,128)}, f32[512,512]{1,0:T(8,128)}) async-done(((f32[512,512]{1,0:T(8,128)}, f32[512,512]{1,0:T(8,128)}, f32[512,512]{1,0:T(8,128)}), (f32[512,512]{1,0:T(8,128)}, f32[512,512]{1,0:T(8,128)}, f32[512,512]{1,0:T(8,128)})) %all-reduce.5.cloned.1.call-update) | async-done | bytes 3145744 | tf_op jit(solution)/shard_map/psum | solution.py:191
  (273 shorter events, 196.1 us)
Async XLA Ops:
  7.2 151.4 %copy-start = (bf16[512,512]{1,0:T(8,128)(2,1)S(1)}, bf16[512,512]{1,0:T(8,128)(2,1)}, u32[]{:S(2)}) copy-start(bf16[512,512]{1,0:T(8,128)(2,1)} %param.41) | copy-start | bytes 1572868
  66.7 142.1 %copy-start.23 = (s32[384]{0:T(512)}, s32[384]{0:T(512)S(1)}, u32[]{:S(2)}) copy-start(s32[384]{0:T(512)S(1)} %get-tuple-element.500) | copy-start | bytes 4612
  71.3 14.9 %all-to-all-start = ((s32[8,1,48]{2,1,0:T(1,128)}), s32[8,1,48]{2,1,0:T(1,128)S(1)}, u32[]{:S(2)}, u32[]{:S(2)}) async-start(s32[8,1,48]{2,1,0:T(1,128)} %all_to_all.18), calls=%async_computation | async-start | bytes 8192 | tf_op jit(solution)/shard_map/all_to_all | solution.py:145
  81.2 7.7 %copy-start.3 = (f32[1024,512]{0,1:T(8,128)}, f32[1024,512]{0,1:T(8,128)S(1)}, u32[]{:S(2)}) copy-start(f32[1024,512]{0,1:T(8,128)S(1)} %get-tuple-element.499) | copy-start | bytes 6291460
  81.2 7.7 %copy-start.18 = (f32[1024]{0:T(1024)}, f32[1024]{0:T(1024)S(1)}, u32[]{:S(2)}) copy-start(f32[1024]{0:T(1024)S(1)} %broadcast_multiply_fusion.3) | copy-start | bytes 12292
  88.9 8.6 %copy-start.30 = (bf16[1024,512]{1,0:T(8,128)(2,1)S(1)}, bf16[1024,512]{1,0:T(8,128)(2,1)}, u32[]{:S(2)}) copy-start(bf16[1024,512]{1,0:T(8,128)(2,1)} %convolution_convert_fusion.3) | copy-start | bytes 3145732
  88.9 21.4 %all-to-all-start.1 = ((bf16[8,48,512]{2,1,0:T(8,128)(2,1)}), bf16[8,48,512]{2,1,0:T(8,128)(2,1)S(1)}, u32[]{:S(2)}, u32[]{:S(2)}) async-start(bf16[8,48,512]{2,1,0:T(8,128)(2,1)} %bitcast.6), calls=%async_computation.1 | async-start | bytes 786432 | tf_op jit(solution)/shard_map/all_to_all | solution.py:149
  208.8 33.6 %copy-start.7 = (bf16[512,512]{1,0:T(8,128)(2,1)S(1)}, bf16[512,512]{1,0:T(8,128)(2,1)}, u32[]{:S(2)}) copy-start(bf16[512,512]{1,0:T(8,128)(2,1)} %param.43) | copy-start | bytes 1572868
  208.8 33.6 %copy-start.27 = (f32[512]{0:T(512)S(1)}, f32[512]{0:T(512)}, u32[]{:S(2)}) copy-start(f32[512]{0:T(512)} %param.44) | copy-start | bytes 6148
  208.8 34.8 %copy-start.15 = (bf16[320,512]{1,0:T(8,128)(2,1)S(1)}, bf16[320,512]{1,0:T(8,128)(2,1)}, u32[]{:S(2)}) copy-start(bf16[320,512]{1,0:T(8,128)(2,1)} %param.31) | copy-start | bytes 983044
  212.6 25.3 %all-to-all-start.2 = ((f32[8,48,512]{2,1,0:T(8,128)}), f32[8,48,512]{2,1,0:T(8,128)S(1)}, u32[]{:S(2)}, u32[]{:S(2)}) async-start(f32[8,48,512]{2,1,0:T(8,128)} %bitcast.10), calls=%async_computation.2 | async-start | bytes 1572864 | tf_op jit(solution)/shard_map/all_to_all | solution.py:161
  221.5 43.9 %copy-start.26 = (s32[384]{0:T(512)}, s32[384]{0:T(512)S(1)}, u32[]{:S(2)}) copy-start(s32[384]{0:T(512)S(1)} %reshape.308) | copy-start | bytes 4612
  248.1 15.1 %all-to-all-start.3 = ((bf16[8,48,512]{2,1,0:T(8,128)(2,1)}), bf16[8,48,512]{2,1,0:T(8,128)(2,1)S(1)}, u32[]{:S(2)}, u32[]{:S(2)}) async-start(bf16[8,48,512]{2,1,0:T(8,128)(2,1)} %bitcast.12), calls=%async_computation.3 | async-start | bytes 786432 | tf_op jit(solution)/shard_map/all_to_all | solution.py:172
  312.5 24.6 %copy-start.19 = (f32[1024]{0:T(1024)S(1)}, f32[1024]{0:T(1024)}, u32[]{:S(2)}) copy-start(f32[1024]{0:T(1024)} %copy-done.18) | copy-start | bytes 12292
  312.5 24.6 %copy-start.21 = (f32[1024]{0:T(1024)S(1)}, f32[1024]{0:T(1024)}, u32[]{:S(2)}) copy-start(f32[1024]{0:T(1024)} %copy-done.20) | copy-start | bytes 12292
  312.5 24.6 %copy-start.25 = (f32[512]{0:T(512)S(1)}, f32[512]{0:T(512)}, u32[]{:S(2)}) copy-start(f32[512]{0:T(512)} %param.37) | copy-start | bytes 6148
  340.7 53.5 %copy-start.29 = (f32[512]{0:T(512)S(1)}, f32[512]{0:T(512)}, u32[]{:S(2)}) copy-start(f32[512]{0:T(512)} %param.40) | copy-start | bytes 6148
  390.3 23.3 %all-to-all-start.4 = ((f32[8,48,512]{2,1,0:T(8,128)}), f32[8,48,512]{2,1,0:T(8,128)S(1)}, u32[]{:S(2)}, u32[]{:S(2)}) async-start(f32[8,48,512]{2,1,0:T(8,128)} %bitcast.16), calls=%async_computation.4 | async-start | bytes 1572864 | tf_op jit(solution)/shard_map/all_to_all | solution.py:184
  393.8 22.9 %copy-start.5 = (bf16[320,512]{1,0:T(8,128)(2,1)S(1)}, bf16[320,512]{1,0:T(8,128)(2,1)}, u32[]{:S(2)}) copy-start(bf16[320,512]{1,0:T(8,128)(2,1)} %param.30) | copy-start | bytes 983044
  393.9 161.9 %all-reduce.5.cloned.1.call-start = ((), (), s32[]{:S(2)}) async-start(), calls=%async_computation.5 | async-start | bytes 6291456 | tf_op jit(solution)/shard_map/psum | solution.py:191
  402.9 15.3 %copy-start.6 = (bf16[512,512]{1,0:T(8,128)(2,1)S(1)}, bf16[512,512]{1,0:T(8,128)(2,1)}, u32[]{:S(2)}) copy-start(bf16[512,512]{1,0:T(8,128)(2,1)} %param.42) | copy-start | bytes 1572868
  402.9 15.3 %copy-start.10 = (bf16[320,512]{1,0:T(8,128)(2,1)S(1)}, bf16[320,512]{1,0:T(8,128)(2,1)}, u32[]{:S(2)}) copy-start(bf16[320,512]{1,0:T(8,128)(2,1)} %copy-done.9) | copy-start | bytes 983044
  402.9 15.3 %copy-start.16 = (bf16[320,512]{1,0:T(8,128)(2,1)S(1)}, bf16[320,512]{1,0:T(8,128)(2,1)}, u32[]{:S(2)}) copy-start(bf16[320,512]{1,0:T(8,128)(2,1)} %param.31) | copy-start | bytes 983044
  418.6 143.0 %copy-start.1 = (bf16[512,512]{1,0:T(8,128)(2,1)S(1)}, bf16[512,512]{1,0:T(8,128)(2,1)}, u32[]{:S(2)}) copy-start(bf16[512,512]{1,0:T(8,128)(2,1)} %param.41) | copy-start | bytes 1572868
  (13 other events, 51.3 us)
Sparse Core Ops, SparseCore 0:
  418.3 137.4 all-reduce.4
where the time goes:
time: 578 us; the launch traced here: 569 us
  waiting for transfers between devices  172 us (30%)
  matrix products  119 us (21%)
  other arithmetic  114 us (20%)
  loops' own time  63.1 us (11%)
  local copies, waits for them, and re-layouts  58.7 us (10%)
  starting transfers between devices  27.2 us (5%)
  between operations  15.1 us (3%)
    psum x1, waiting for transfers between devices, shards(): lax.psum((local_edge, local_ugrid, local_umesh), ('band', 'mesh'))  134 us
    dot_general x39, matrix products, matmul(): return jnp.dot(a, b, preferred_element_type=jnp.float32)  74.3 us
    dot_general x24, matrix products, one_block(): lax.dot_general(onehot, value_blocks[index], (((0,), (0,)), ((), ())), pr...  44.4 us
    another operation x2, loops' own time, window_add(): lax.fori_loop(0, blocks.shape[0], one_block, jnp.zeros((rows + block, wid...  31.7 us
    another operation x2, loops' own time, window_take(): return lax.map(one_block, blocks).reshape(-1, width)  31.2 us
    another operation x1, other arithmetic, shards(): jnp.full((compact,), band_rows_count, jnp.int32).at[rank]  28.8 us
    another operation x1, other arithmetic, shards(): jnp.full((compact,), compact, jnp.int32).at[rank].min(slot, mode='drop')  28.8 us
    slice x32, local copies, waits for them, and re-layouts, one_block(): base = rank_block[0]  16.5 us
  transfers between devices with their start and end apart: 6, of which 4 were waited for; matrix products, arithmetic and copies ran while one was open for 7% of the time, Pallas kernels for 0%

commit v1 on v0

v1 whole, which is shorter than its diff:
```python
import functools

import jax
import jax.numpy as jnp
from jax import lax
from jax.experimental import pallas as pl
from jax.experimental.pallas import tpu as pltpu
from jax.sharding import Mesh
from jax.sharding import PartitionSpec as P

CAP = 48
LANES = 128
ROWS = 8
BF16 = jnp.bfloat16
F32 = jnp.float32


def dot(a, b):
    return jnp.dot(a, b, preferred_element_type=F32)


def dot_nt(a, b):
    return lax.dot_general(a, b, (((1,), (1,)), ((), ())), preferred_element_type=F32)


def dot_tn(a, b):
    return lax.dot_general(a, b, (((0,), (0,)), ((), ())), preferred_element_type=F32)


def sigmoid(v):
    return 0.5 + 0.5 * jnp.tanh(0.5 * v)


def as_bf16(mask):
    return jnp.where(mask, 1.0, 0.0).astype(BF16)


def edges_by_ids(ids, count):
    columns = jnp.transpose(ids)
    lanes = lax.broadcasted_iota(jnp.int32, (LANES, count), 1)
    return jnp.concatenate(
        [as_bf16(columns[:, j : j + 1] == lanes) for j in range(ids.shape[0])], axis=0
    )


def ids_by_edges(ids, count):
    places = lax.broadcasted_iota(jnp.int32, (count, LANES), 0)
    return jnp.concatenate(
        [as_bf16(ids[j : j + 1, :] == places) for j in range(ids.shape[0])], axis=1
    )


def call(kernel, name, out, args, flops, grid=None, in_specs=None, out_specs=None, scratch=(), vmem=24):
    moved = sum(a.size * a.dtype.itemsize for a in args)
    moved += sum(o.size * o.dtype.itemsize for o in out)
    extra = {}
    if grid is not None:
        extra = dict(grid=grid, in_specs=in_specs, out_specs=out_specs)
    return pl.pallas_call(
        kernel,
        out_shape=out,
        scratch_shapes=scratch,
        name=name,
        cost_estimate=pl.CostEstimate(flops=int(flops), bytes_accessed=int(moved), transcendentals=0),
        compiler_params=pltpu.CompilerParams(vmem_limit_bytes=vmem << 20),
        **extra,
    )(*args)


def whole(shape):
    return pl.BlockSpec(shape, lambda i: (0,) * len(shape))


def prep_kernel(owners, mesh_dev, em_ref, slot_ref, ids_ref):
    m = em_ref[...]
    rows = m.shape[0]
    lane = lax.broadcasted_iota(jnp.int32, m.shape, 1)
    row = lax.broadcasted_iota(jnp.int32, m.shape, 0)
    turned = pltpu.roll(m, 1, axis=1)
    before = jnp.where(lane == 0, pltpu.roll(turned, 1, axis=0), turned)
    fresh = (m != before) | ((lane == 0) & (row == 0))
    fresh_b = as_bf16(fresh)
    upto = lax.broadcasted_iota(jnp.int32, (LANES, LANES), 0) <= lax.broadcasted_iota(
        jnp.int32, (LANES, LANES), 1
    )
    inside = dot(fresh_b, as_bf16(upto))
    totals = jnp.broadcast_to(inside[:, LANES - 1 :], inside.shape).astype(BF16)
    above = lax.broadcasted_iota(jnp.int32, (rows, rows), 1) < lax.broadcasted_iota(
        jnp.int32, (rows, rows), 0
    )
    rank = (inside + dot(as_bf16(above), totals)).astype(jnp.int32) - 1
    slot = rank
    local = m
    fresh_i = fresh.astype(jnp.int32)
    for o in range(1, owners):
        past = m >= o * mesh_dev
        start = jnp.sum(
            jnp.sum(jnp.where(past, 0, fresh_i), axis=0, keepdims=True), axis=1, keepdims=True
        )
        slot = jnp.where(past, rank + (o * CAP - start), slot)
        local = jnp.where(past, m - o * mesh_dev, local)
    slot_ref[...] = slot
    value = jnp.where(fresh, local + 1, 0)
    found = []
    for o in range(owners):
        places = o * CAP + lax.broadcasted_iota(jnp.int32, (CAP, LANES), 0)
        total = jnp.zeros((CAP, LANES), jnp.int32)
        for r in range(rows):
            total = total + jnp.where(slot[r : r + 1, :] == places, value[r : r + 1, :], 0)
        found.append(total)
    pad = jnp.zeros((LANES - CAP, LANES), jnp.int32)
    for o in range(owners):
        square = jnp.transpose(jnp.concatenate([found[o], pad], axis=0))
        ids_ref[o : o + 1, :] = jnp.sum(square, axis=0, keepdims=True) - 1


def node_pre_kernel(ml_ref, cot_ref, um_ref, ws_ref, bn_ref, wno_ref, pm_ref, self_ref, cw_ref):
    ml = ml_ref[...]
    pm_ref[...] = dot(ml, um_ref[...]).astype(BF16)
    self_ref[...] = dot(ml, ws_ref[...]) + bn_ref[...]
    cw_ref[...] = dot_nt(cot_ref[...], wno_ref[...])


def embed_kernel(gv_ref, win_ref, bin_ref, wout_ref, gain_ref, ug_ref, lat_t_ref, pg_ref):
    v = dot(gv_ref[...], win_ref[...]) + bin_ref[...]
    hidden = (v * sigmoid(v)).astype(BF16)
    out = dot(hidden, wout_ref[...])
    mean = jnp.mean(out, axis=-1, keepdims=True)
    centred = out - mean
    var = jnp.mean(centred * centred, axis=-1, keepdims=True)
    latent = centred * lax.rsqrt(var + 1e-05) * gain_ref[...]
    pg_ref[...] = dot(latent.astype(BF16), ug_ref[...]).astype(BF16)
    lat_t_ref[...] = jnp.transpose(latent).astype(BF16)


def take_grid_kernel(ids_ref, pg_ref, out_ref):
    onehot = edges_by_ids(ids_ref[...], pg_ref.shape[0])
    out_ref[...] = dot(onehot, pg_ref[...]).astype(BF16)


def take_latent_kernel(ids_ref, lat_t_ref, out_ref):
    onehot = ids_by_edges(ids_ref[...], lat_t_ref.shape[1])
    out_ref[...] = dot(lat_t_ref[...], onehot).astype(BF16)


def ask_kernel(ids_ref, pm_ref, asked_ref, onehot_ref):
    owners = ids_ref.shape[0]
    nodes = pm_ref.shape[0]
    columns = jnp.transpose(ids_ref[...])
    lanes = lax.broadcasted_iota(jnp.int32, (CAP, nodes), 1)
    onehot = jnp.concatenate(
        [as_bf16(columns[:CAP, o : o + 1] == lanes) for o in range(owners)], axis=0
    )
    onehot_ref[...] = onehot
    asked_ref[...] = dot(onehot, pm_ref[...]).astype(BF16)


def pre_act(slot, pg, pm, bias):
    onehot = edges_by_ids(slot, pm.shape[0])
    return dot(onehot, pm) + pg.astype(F32) + bias


def edge_kernel(steps, slot_ref, pg_ref, pm_ref, be_ref, sum_ref, total):
    step = pl.program_id(0)

    @pl.when(step == 0)
    def _():
        total[...] = jnp.zeros_like(total)

    slot = slot_ref[...]
    pre = pre_act(slot, pg_ref[...], pm_ref[...], be_ref[...])
    act = (pre * sigmoid(pre)).astype(BF16)
    total[...] += dot(ids_by_edges(slot, total.shape[0]), act)

    @pl.when(step == steps - 1)
    def _():
        sum_ref[...] = total[...].astype(BF16)


def slope_kernel(steps, slot_ref, pg_ref, pm_ref, be_ref, slope_ref, sum_ref, total):
    step = pl.program_id(0)

    @pl.when(step == 0)
    def _():
        total[...] = jnp.zeros_like(total)

    slot = slot_ref[...]
    pre = pre_act(slot, pg_ref[...], pm_ref[...], be_ref[...])
    s = sigmoid(pre)
    slope = s * (1.0 + pre * (1.0 - s))
    slope_ref[...] = slope
    total[...] += dot(ids_by_edges(slot, total.shape[0]), slope.astype(BF16))

    @pl.when(step == steps - 1)
    def _():
        sum_ref[...] = total[...].astype(BF16)


def node_kernel(
    rec_ref, row_ref, oh_ref, self_ref, cw_ref, we_ref, wa_ref,
    hask_ref, act_ref, h_ref, gagg_ref, gnode_ref, nact_ref,
):
    nodes = self_ref.shape[0]
    onehot_t = as_bf16(lax.broadcasted_iota(jnp.int32, (nodes, row_ref.shape[1]), 0) == row_ref[...])
    act = dot(onehot_t, rec_ref[...]).astype(BF16)
    agg = dot(act, we_ref[...]).astype(BF16)
    pre = self_ref[...] + dot(agg, wa_ref[...])
    s = sigmoid(pre)
    g_node = (cw_ref[...] * (s * (1.0 + pre * (1.0 - s)))).astype(BF16)
    g_agg = dot_nt(g_node, wa_ref[...]).astype(BF16)
    h = dot_nt(g_agg, we_ref[...])
    hask_ref[...] = dot(oh_ref[...], h.astype(BF16)).astype(BF16)
    act_ref[...] = act
    h_ref[...] = h
    gagg_ref[...] = g_agg
    gnode_ref[...] = g_node
    nact_ref[...] = (pre * s).astype(BF16)


def node_post_kernel(
    rec_ref, row_ref, act_ref, h_ref, gagg_ref, gnode_ref, nact_ref, ml_ref, cot_ref,
    wno_ref, ws_ref, um_ref, mo_ref, gm_ref, grads_ref,
):
    nodes, width = h_ref.shape
    ml = ml_ref[...]
    onehot_t = as_bf16(lax.broadcasted_iota(jnp.int32, (nodes, row_ref.shape[1]), 0) == row_ref[...])
    slopes = dot(onehot_t, rec_ref[...])
    g_pmesh = (h_ref[...] * slopes).astype(BF16)
    grads_ref[:width, :] = dot_tn(act_ref[...], gagg_ref[...]).astype(BF16)
    grads_ref[width:, :] = dot_tn(ml, g_pmesh).astype(BF16)
    mo_ref[...] = (ml.astype(F32) + dot(nact_ref[...], wno_ref[...])).astype(BF16)
    gm_ref[...] = (
        cot_ref[...].astype(F32) + dot_nt(gnode_ref[...], ws_ref[...]) + dot_nt(g_pmesh, um_ref[...])
    ).astype(BF16)


def edge_back_kernel(steps, slot_ref, slope_ref, lat_t_ref, h_ref, out_ref, total):
    step = pl.program_id(0)

    @pl.when(step == 0)
    def _():
        total[...] = jnp.zeros_like(total)

    onehot = edges_by_ids(slot_ref[...], h_ref.shape[0])
    g_edge = (dot(onehot, h_ref[...]) * slope_ref[...]).astype(BF16)
    total[...] += dot(lat_t_ref[...], g_edge)

    @pl.when(step == steps - 1)
    def _():
        out_ref[...] = total[...].astype(BF16)


def all_sum(value, scale):
    rows, width = value.shape
    half = rows // 2
    core = lax.axis_index("core")
    pairs = [(0, 1), (1, 0)]
    others = ("x", "mesh")
    count = lax.axis_size("x") * lax.axis_size("mesh")
    keep = lax.dynamic_slice_in_dim(value, core * half, half, 0)
    give = lax.dynamic_slice_in_dim(value, (1 - core) * half, half, 0)
    got = lax.ppermute(give, "core", pairs)
    part = (keep.astype(F32) + got.astype(F32)).astype(BF16)
    pieces = lax.all_to_all(part, others, 0, 0, tiled=True).reshape(count, half // count, width)
    total = (jnp.sum(pieces.astype(F32), axis=0) * scale).astype(BF16)
    copies = jnp.broadcast_to(total[None], pieces.shape).reshape(half, width)
    mine = lax.all_to_all(copies, others, 0, 0, tiled=True)
    other = lax.ppermute(mine, "core", pairs)
    first = jnp.where(core == 0, mine, other)
    second = jnp.where(core == 0, other, mine)
    return jnp.concatenate([first, second], axis=0).astype(F32)


def shards(
    grid_vars,
    mesh_latent,
    cotangent,
    edge_grid,
    edge_mesh,
    w_in,
    b_in,
    w_out,
    norm_gain,
    u_grid,
    u_mesh,
    b_edge,
    w_edge,
    w_self,
    w_agg,
    b_node,
    w_node_out,
):
    grid_dev, variables = grid_vars.shape
    mesh_dev, width = mesh_latent.shape
    edge_dev = edge_grid.shape[0]
    owners = lax.axis_size("mesh")
    slots = owners * CAP
    rows = edge_dev // LANES
    block = ROWS * LANES
    steps = edge_dev // block
    band = lax.axis_index("x") * lax.axis_size("core") + lax.axis_index("core")
    device = band * owners + lax.axis_index("mesh")
    scale = (edge_dev * lax.axis_size("x") * lax.axis_size("core") * owners) ** (-0.5)
    sds = jax.ShapeDtypeStruct

    def exchange(value):
        return lax.all_to_all(value, "mesh", 0, 0, tiled=True)

    mesh_local = (edge_mesh - band * (owners * mesh_dev)).reshape(rows, LANES)
    grid_local = (edge_grid - device * grid_dev).reshape(rows, LANES)

    slot, ids = call(
        functools.partial(prep_kernel, owners, mesh_dev),
        "prep",
        [sds((rows, LANES), jnp.int32), sds((owners, LANES), jnp.int32)],
        [mesh_local],
        1e9,
    )
    incoming = exchange(ids)

    proj_mesh, self_part, cot_part = call(
        node_pre_kernel,
        "node_pre",
        [sds((mesh_dev, width), BF16), sds((mesh_dev, width), F32), sds((mesh_dev, width), F32)],
        [mesh_latent, cotangent, u_mesh, w_self, b_node.reshape(1, width), w_node_out],
        6 * mesh_dev * width * width,
    )

    tile = min(256, grid_dev)
    latent_t, proj_grid = call(
        embed_kernel,
        "embed",
        [sds((width, grid_dev), BF16), sds((grid_dev, width), BF16)],
        [grid_vars, w_in, b_in.reshape(1, width), w_out, norm_gain.reshape(1, width), u_grid],
        2 * grid_dev * width * (variables + 2 * width),
        grid=(grid_dev // tile,),
        in_specs=[
            pl.BlockSpec((tile, variables), lambda i: (i, 0)),
            whole((variables, width)),
            whole((1, width)),
            whole((width, width)),
            whole((1, width)),
            whole((width, width)),
        ],
        out_specs=[
            pl.BlockSpec((width, tile), lambda i: (0, i)),
            pl.BlockSpec((tile, width), lambda i: (i, 0)),
        ],
    )

    id_spec = pl.BlockSpec((ROWS, LANES), lambda i: (i, 0))
    edge_spec = pl.BlockSpec((block, width), lambda i: (i, 0))
    edge_t_spec = pl.BlockSpec((width, block), lambda i: (0, i))
    (edge_pgrid,) = call(
        take_grid_kernel,
        "take_grid",
        [sds((edge_dev, width), BF16)],
        [grid_local, proj_grid],
        2 * edge_dev * grid_dev * width,
        grid=(steps,),
        in_specs=[id_spec, whole((grid_dev, width))],
        out_specs=[edge_spec],
    )
    (edge_latent_t,) = call(
        take_latent_kernel,
        "take_latent",
        [sds((width, edge_dev), BF16)],
        [grid_local, latent_t],
        2 * edge_dev * grid_dev * width,
        grid=(steps,),
        in_specs=[id_spec, whole((width, grid_dev))],
        out_specs=[edge_t_spec],
    )

    asked, onehot_in = call(
        ask_kernel,
        "ask",
        [sds((slots, width), BF16), sds((slots, mesh_dev), BF16)],
        [incoming, proj_mesh],
        2 * slots * mesh_dev * width,
    )
    incoming_row = incoming[:, :CAP].reshape(1, slots)
    slot_pmesh = exchange(asked)

    bias = b_edge.reshape(1, width)
    forward_specs = [id_spec, edge_spec, whole((slots, width)), whole((1, width))]
    total = [pltpu.VMEM((slots, width), F32)]
    (act_sums,) = call(
        functools.partial(edge_kernel, steps),
        "edge",
        [sds((slots, width), BF16)],
        [slot, edge_pgrid, slot_pmesh, bias],
        4 * edge_dev * slots * width,
        grid=(steps,),
        in_specs=forward_specs,
        out_specs=[whole((slots, width))],
        scratch=total,
    )
    act_received = exchange(act_sums)
    slope, slope_sums = call(
        functools.partial(slope_kernel, steps),
        "slope",
        [sds((edge_dev, width), F32), sds((slots, width), BF16)],
        [slot, edge_pgrid, slot_pmesh, bias],
        4 * edge_dev * slots * width,
        grid=(steps,),
        in_specs=forward_specs,
        out_specs=[edge_spec, whole((slots, width))],
        scratch=total,
    )
    slope_received = exchange(slope_sums)

    node_b = sds((mesh_dev, width), BF16)
    h_asked, act_total, h, g_agg, g_node, node_act = call(
        node_kernel,
        "node",
        [sds((slots, width), BF16), node_b, sds((mesh_dev, width), F32), node_b, node_b, node_b],
        [act_received, incoming_row, onehot_in, self_part, cot_part, w_edge, w_agg],
        8 * mesh_dev * width * width + 4 * mesh_dev * slots * width,
    )
    slot_h = exchange(h_asked)

    mesh_out, grad_mesh, owner_grads = call(
        node_post_kernel,
        "node_post",
        [node_b, node_b, sds((2 * width, width), BF16)],
        [
            slope_received, incoming_row, act_total, h, g_agg, g_node, node_act,
            mesh_latent, cotangent, w_node_out, w_self, u_mesh,
        ],
        10 * mesh_dev * width * width + 2 * mesh_dev * slots * width,
    )
    owner_total = all_sum(owner_grads, scale)

    (local_ugrid,) = call(
        functools.partial(edge_back_kernel, steps),
        "edge_back",
        [sds((width, width), BF16)],
        [slot, slope, edge_latent_t, slot_h],
        2 * edge_dev * (slots + width) * width,
        grid=(steps,),
        in_specs=[id_spec, edge_spec, edge_t_spec, whole((slots, width))],
        out_specs=[whole((width, width))],
        scratch=[pltpu.VMEM((width, width), F32)],
    )
    grad_ugrid = all_sum(local_ugrid, scale)
    return mesh_out, grad_mesh, owner_total[:width], grad_ugrid, owner_total[width:]


def solution(mesh):
    bands, owners = mesh.shape["band"], mesh.shape["mesh"]
    cores = 2
    fine = Mesh(mesh.devices.reshape(bands // cores, cores, owners), ("x", "core", "mesh"))
    split = ("x", "core", "mesh")
    return jax.shard_map(
        shards,
        mesh=fine,
        in_specs=(P(split, None),) * 3 + (P(split),) * 2 + (P(),) * 12,
        out_specs=(P(split, None), P(split, None), P(), P(), P()),
        check_vma=False,
    )
```

time: 578 us -> 196 us (0.34); the launches traced: 569 us -> 194 us
  matrix products: 119 us -> 0 us
  waiting for transfers between devices: 172 us -> 58.1 us
  other arithmetic: 114 us -> 6.31 us
  loops' own time: 63.1 us -> 0 us
  Pallas kernels: 0 us -> 43.1 us
  local copies, waits for them, and re-layouts: 58.7 us -> 40.1 us
  starting transfers between devices: 27.2 us -> 45.1 us
  between operations: 15.1 us -> 1.09 us
    psum x1 -> x0, waiting for transfers between devices: 134 us -> none  [shards(): lax.psum((local_edge, local_ugrid, local_umesh), ('band', 'mesh'))]
    dot_general x63 -> x0, matrix products: 119 us -> none  [the longest x39 74.3 us: matmul(): return jnp.dot(a, b, preferred_element_type=jnp.float32)]
    another operation x6 -> x0, loops' own time: 63.1 us -> none  [the longest x2 31.7 us: window_add(): lax.fori_loop(0, blocks.shape[0], one_block, jnp.zeros((rows + block, wid...]
    another operation x4 -> x0, other arithmetic: 57.9 us -> none  [the longest x1 28.8 us: shards(): jnp.full((compact,), band_rows_count, jnp.int32).at[rank]]
    pallas_call x0 -> x11, Pallas kernels: none -> 43.1 us  [call(): pl.pallas_call(kernel, out_shape=out, scratch_shapes=scratch, name=name,...]
    unnamed x62 -> x89, local copies, waits for them, and re-layouts: 1.86 us -> 36.1 us
    sub x35 -> x0, other arithmetic: 21.1 us -> none  [the longest x16 10.5 us: one_block(): onehot = ((rank_block - base)[:, None] == columns).astype(table.dtype)]
    all_to_all x5 -> x9, waiting for transfers between devices: 38.6 us -> 57.4 us  [the longest x2 22.5 us: all_sum(): lax.all_to_all(part, others, 0, 0, tiled=True)]
  transfers between devices with their start and end apart: 6 -> 13, of which waited for: 4 -> 7; matrix products, arithmetic and copies ran while one was open for 7% -> 4% of each run, Pallas kernels for 0% -> 16%
where the time goes in v1:
time: 196 us; the launch traced here: 194 us
  waiting for transfers between devices  58.1 us (30%)
  starting transfers between devices  45.1 us (23%)
  Pallas kernels  43.1 us (22%)
  local copies, waits for them, and re-layouts  40.1 us (20%)
  other arithmetic  6.31 us (3%)
    pallas_call x11, Pallas kernels, call(): pl.pallas_call(kernel, out_shape=out, scratch_shapes=scratch, name=name,...  43.1 us
    unnamed x89, local copies, waits for them, and re-layouts  36.1 us
    all_to_all x5, starting transfers between devices, exchange(): return lax.all_to_all(value, 'mesh', 0, 0, tiled=True)  26.7 us
    all_to_all x2, waiting for transfers between devices, all_sum(): lax.all_to_all(part, others, 0, 0, tiled=True)  22.5 us
    all_to_all x2, waiting for transfers between devices, all_sum(): mine = lax.all_to_all(copies, others, 0, 0, tiled=True)  21.8 us
    all_to_all x5, waiting for transfers between devices, exchange(): return lax.all_to_all(value, 'mesh', 0, 0, tiled=True)  13.1 us
    all_to_all x2, starting transfers between devices, all_sum(): lax.all_to_all(part, others, 0, 0, tiled=True)  10.6 us
    all_to_all x2, starting transfers between devices, all_sum(): mine = lax.all_to_all(copies, others, 0, 0, tiled=True)  7.13 us
  transfers between devices with their start and end apart: 13, of which 7 were waited for; matrix products, arithmetic and copies ran while one was open for 4% of the time, Pallas kernels for 16%

profile of v1, /device:TPU:0, one launch (start us, length us, event | category | flops | bytes accessed | tf_op | source)
XLA Modules:
  0.0 193.8 jit_solution(13684847358158687385)
XLA Ops:
  3.3 7.3 %all-to-all-start = ((s32[8,1,128]{2,1,0:T(1,128)}), s32[8,1,128]{2,1,0:T(1,128)S(1)}, u32[]{:S(2)}, u32[]{:S(2)}) async-start(s32[8,1,128]{2,1,0:T(1,128)} %bitcast.5), calls=%async_computation | async-start | bytes 8192 | tf_op jit(solution)/shard_map/all_to_all | solution.py:307
  14.3 2.7 %all-to-all-done = s32[8,1,128]{2,1,0:T(1,128)S(1)} async-done(((s32[8,1,128]{2,1,0:T(1,128)}), s32[8,1,128]{2,1,0:T(1,128)S(1)}, u32[]{:S(2)}, u32[]{:S(2)}) %all-to-all-start) | async-done | bytes 4128 | tf_op jit(solution)/shard_map/all_to_all | solution.py:307
  19.0 3.5 %all-to-all-start.1 = ((bf16[8,48,512]{2,1,0:T(8,128)(2,1)}), bf16[8,48,512]{2,1,0:T(8,128)(2,1)S(1)}, u32[]{:S(2)}, u32[]{:S(2)}) async-start(bf16[8,48,512]{2,1,0:T(8,128)(2,1)} %bitcast.8), calls=%async_computation.1 | async-start | bytes 786432 | tf_op jit(solution)/shard_map/all_to_all | solution.py:307
  24.5 3.7 %embed.1 = (bf16[512,1024]{1,0:T(8,128)(2,1)S(1)}, bf16[1024,512]{1,0:T(8,128)(2,1)S(1)}) custom-call(bf16[1024,227]{1,0:T(8,128)(2,1)S(1)} %copy.23.gv_ref, bf16[227,512]{1,0:T(8,128)(2,1)S(1)} %copy-done.28, f32[1,512]{1,0:T(1,128)S(1)} %bitcast.38, bf16[512,512]{1,0:T(8,128)(2,1)S(1)} %copy-done.24, f32[1,512]{1,0:T(1,128)S(1)} %bitcast.39, ...), custom_call_target="tpu_custom_call" | custom-call | flops 1311768576 | bytes 3847168 | tf_op jit(solution)/shard_map/embed/pallas_call | solution.py:59
  31.4 5.5 %take_grid.1.pg_ref = bf16[4096,512]{1,0:T(8,128)(2,1)S(1)} custom-call(s32[32,128]{1,0:T(8,128)S(1)} %subtract_bitcast_fusion.ids_ref, bf16[1024,512]{1,0:T(8,128)(2,1)S(1)} %copy-done.39), custom_call_target="tpu_custom_call" | custom-call | flops 4294967296 | bytes 5259264 | tf_op jit(solution)/shard_map/take_grid/pallas_call | solution.py:59
  38.9 2.2 %copy-done.41 = bf16[4096,512]{1,0:T(8,128)(2,1)S(1)} copy-done((bf16[4096,512]{1,0:T(8,128)(2,1)S(1)}, bf16[4096,512]{1,0:T(8,128)(2,1)}, u32[]{:S(2)}) %copy-start.41) | copy-done | bytes 4194328
  41.1 7.1 %edge.1 = bf16[384,512]{1,0:T(8,128)(2,1)} custom-call(s32[32,128]{1,0:T(8,128)S(1)} %get-tuple-element.25.slot_ref, bf16[4096,512]{1,0:T(8,128)(2,1)S(1)} %copy-done.41, bf16[384,512]{1,0:T(8,128)(2,1)S(1)} %bitcast.30, f32[1,512]{1,0:T(1,128)S(1)} %bitcast.40), custom_call_target="tpu_custom_call" | custom-call | flops 3221225472 | bytes 4999168 | tf_op jit(solution)/shard_map/edge/pallas_call | solution.py:59
  48.2 5.9 %all-to-all-start.3 = ((bf16[8,48,512]{2,1,0:T(8,128)(2,1)}), bf16[8,48,512]{2,1,0:T(8,128)(2,1)S(1)}, u32[]{:S(2)}, u32[]{:S(2)}) async-start(bf16[8,48,512]{2,1,0:T(8,128)(2,1)} %bitcast.13), calls=%async_computation.3 | async-start | bytes 786432 | tf_op jit(solution)/shard_map/all_to_all | solution.py:307
  54.2 10.4 %all-to-all-done.3 = bf16[8,48,512]{2,1,0:T(8,128)(2,1)S(1)} async-done(((bf16[8,48,512]{2,1,0:T(8,128)(2,1)}), bf16[8,48,512]{2,1,0:T(8,128)(2,1)S(1)}, u32[]{:S(2)}, u32[]{:S(2)}) %all-to-all-start.3) | async-done | bytes 393248 | tf_op jit(solution)/shard_map/all_to_all | solution.py:307
  76.9 4.1 %all-to-all-start.6 = ((bf16[8,48,512]{2,1,0:T(8,128)(2,1)}), bf16[8,48,512]{2,1,0:T(8,128)(2,1)}, u32[]{:S(2)}, u32[]{:S(2)}) async-start(bf16[8,48,512]{2,1,0:T(8,128)(2,1)} %bitcast.32), calls=%async_computation.6 | async-start | bytes 786432 | tf_op jit(solution)/shard_map/all_to_all | solution.py:307
  81.1 2.2 %copy-done.42 = bf16[4096,512]{1,0:T(8,128)(2,1)S(1)} copy-done((bf16[4096,512]{1,0:T(8,128)(2,1)S(1)}, bf16[4096,512]{1,0:T(8,128)(2,1)}, u32[]{:S(2)}) %copy-start.42) | copy-done | bytes 4194328
  83.2 7.2 %slope.1 = (f32[4096,512]{1,0:T(8,128)S(1)}, bf16[384,512]{1,0:T(8,128)(2,1)S(1)}) custom-call(s32[32,128]{1,0:T(8,128)S(1)} %get-tuple-element.25.slot_ref, bf16[4096,512]{1,0:T(8,128)(2,1)S(1)} %copy-done.42, bf16[384,512]{1,0:T(8,128)(2,1)S(1)} %bitcast.31, f32[1,512]{1,0:T(1,128)S(1)} %bitcast.41), custom_call_target="tpu_custom_call" | custom-call | flops 3221225472 | bytes 13387776 | tf_op jit(solution)/shard_map/slope/pallas_call | solution.py:59
  91.2 3.3 %copy-done.32 = f32[4096,512]{1,0:T(8,128)} copy-done((f32[4096,512]{1,0:T(8,128)}, f32[4096,512]{1,0:T(8,128)S(1)}, u32[]{:S(2)}) %copy-start.32) | copy-done | bytes 8388632
  94.5 5.9 %all-to-all-start.2 = ((bf16[8,48,512]{2,1,0:T(8,128)(2,1)}), bf16[8,48,512]{2,1,0:T(8,128)(2,1)S(1)}, u32[]{:S(2)}, u32[]{:S(2)}) async-start(bf16[8,48,512]{2,1,0:T(8,128)(2,1)} %bitcast.33), calls=%async_computation.2 | async-start | bytes 786432 | tf_op jit(solution)/shard_map/all_to_all | solution.py:307
  101.6 5.3 %take_latent.1.lat_t_ref = bf16[512,4096]{1,0:T(8,128)(2,1)S(1)} custom-call(s32[32,128]{1,0:T(8,128)S(1)} %subtract_bitcast_fusion.ids_ref, bf16[512,1024]{1,0:T(8,128)(2,1)S(1)} %copy-done.37), custom_call_target="tpu_custom_call" | custom-call | flops 4294967296 | bytes 5259264 | tf_op jit(solution)/shard_map/take_latent/pallas_call | solution.py:59
  106.9 6.9 %edge_back.1 = bf16[512,512]{1,0:T(8,128)(2,1)S(1)} custom-call(s32[32,128]{1,0:T(8,128)S(1)} %get-tuple-element.25.slot_ref, f32[4096,512]{1,0:T(8,128)S(1)} %copy-done.33, bf16[512,4096]{1,0:T(8,128)(2,1)S(1)} %take_latent.1.lat_t_ref, bf16[384,512]{1,0:T(8,128)(2,1)} %bitcast.18.h_ref), custom_call_target="tpu_custom_call" | custom-call | flops 3758096384 | bytes 13516800 | tf_op jit(solution)/shard_map/edge_back/pallas_call | solution.py:59
  124.1 7.1 %all-to-all-start.7 = ((bf16[16,16,512]{2,1,0:T(8,128)(2,1)}), bf16[16,16,512]{2,1,0:T(8,128)(2,1)S(1)}, u32[]{:S(2)}, u32[]{:S(2)}) async-start(bf16[16,16,512]{2,1,0:T(8,128)(2,1)} %bitcast.19), calls=%async_computation.7 | async-start | bytes 524288 | tf_op jit(solution)/shard_map/all_to_all | solution.py:264
  133.2 8.1 %all-to-all-done.7 = bf16[16,16,512]{2,1,0:T(8,128)(2,1)S(1)} async-done(((bf16[16,16,512]{2,1,0:T(8,128)(2,1)}), bf16[16,16,512]{2,1,0:T(8,128)(2,1)S(1)}, u32[]{:S(2)}, u32[]{:S(2)}) %all-to-all-start.7) | async-done | bytes 262176 | tf_op jit(solution)/shard_map/all_to_all | solution.py:264
  141.2 3.6 %all-to-all-start.4 = ((bf16[16,32,512]{2,1,0:T(8,128)(2,1)}), bf16[16,32,512]{2,1,0:T(8,128)(2,1)S(1)}, u32[]{:S(2)}, u32[]{:S(2)}) async-start(bf16[16,32,512]{2,1,0:T(8,128)(2,1)} %bitcast.15), calls=%async_computation.4 | async-start | bytes 1048576 | tf_op jit(solution)/shard_map/all_to_all | solution.py:264
  144.9 14.4 %all-to-all-done.4 = bf16[16,32,512]{2,1,0:T(8,128)(2,1)S(1)} async-done(((bf16[16,32,512]{2,1,0:T(8,128)(2,1)}), bf16[16,32,512]{2,1,0:T(8,128)(2,1)S(1)}, u32[]{:S(2)}, u32[]{:S(2)}) %all-to-all-start.4) | async-done | bytes 524320 | tf_op jit(solution)/shard_map/all_to_all | solution.py:264
  160.1 3.5 %all-to-all-start.8 = ((bf16[16,16,512]{2,1,0:T(8,128)(2,1)}), bf16[16,16,512]{2,1,0:T(8,128)(2,1)S(1)}, u32[]{:S(2)}, u32[]{:S(2)}) async-start(bf16[16,16,512]{2,1,0:T(8,128)(2,1)} %broadcast_in_dim.5), calls=%async_computation.8 | async-start | bytes 524288 | tf_op jit(solution)/shard_map/all_to_all | solution.py:267
  163.7 8.3 %all-to-all-done.8 = bf16[16,16,512]{2,1,0:T(8,128)(2,1)S(1)} async-done(((bf16[16,16,512]{2,1,0:T(8,128)(2,1)}), bf16[16,16,512]{2,1,0:T(8,128)(2,1)S(1)}, u32[]{:S(2)}, u32[]{:S(2)}) %all-to-all-start.8) | async-done | bytes 262176 | tf_op jit(solution)/shard_map/all_to_all | solution.py:267
  172.9 3.6 %all-to-all-start.5 = ((bf16[16,32,512]{2,1,0:T(8,128)(2,1)}), bf16[16,32,512]{2,1,0:T(8,128)(2,1)S(1)}, u32[]{:S(2)}, u32[]{:S(2)}) async-start(bf16[16,32,512]{2,1,0:T(8,128)(2,1)} %broadcast_in_dim.4), calls=%async_computation.5 | async-start | bytes 1048576 | tf_op jit(solution)/shard_map/all_to_all | solution.py:267
  176.6 13.4 %all-to-all-done.5 = bf16[16,32,512]{2,1,0:T(8,128)(2,1)S(1)} async-done(((bf16[16,32,512]{2,1,0:T(8,128)(2,1)}), bf16[16,32,512]{2,1,0:T(8,128)(2,1)S(1)}, u32[]{:S(2)}, u32[]{:S(2)}) %all-to-all-start.5) | async-done | bytes 524320 | tf_op jit(solution)/shard_map/all_to_all | solution.py:267
  (120 shorter events, 47.6 us)
Async XLA Ops:
  0.6 10.0 %copy-start.3 = (bf16[320,512]{1,0:T(8,128)(2,1)S(1)}, bf16[320,512]{1,0:T(8,128)(2,1)}, u32[]{:S(2)}) copy-start(bf16[320,512]{1,0:T(8,128)(2,1)} %ml_ref.3) | copy-start | bytes 983044
  0.6 10.0 %copy-start.4 = (bf16[320,512]{1,0:T(8,128)(2,1)S(1)}, bf16[320,512]{1,0:T(8,128)(2,1)}, u32[]{:S(2)}) copy-start(bf16[320,512]{1,0:T(8,128)(2,1)} %cot_ref.3) | copy-start | bytes 983044
  0.7 10.0 %copy-start = (bf16[512,512]{1,0:T(8,128)(2,1)S(1)}, bf16[512,512]{1,0:T(8,128)(2,1)}, u32[]{:S(2)}) copy-start(bf16[512,512]{1,0:T(8,128)(2,1)} %um_ref.3) | copy-start | bytes 1572868
  0.7 10.0 %copy-start.1 = (bf16[512,512]{1,0:T(8,128)(2,1)S(1)}, bf16[512,512]{1,0:T(8,128)(2,1)}, u32[]{:S(2)}) copy-start(bf16[512,512]{1,0:T(8,128)(2,1)} %ws_ref.3) | copy-start | bytes 1572868
  0.7 10.0 %copy-start.19 = (f32[512]{0:T(512)S(1)}, f32[512]{0:T(512)}, u32[]{:S(2)}) copy-start(f32[512]{0:T(512)} %param.32) | copy-start | bytes 6148
  0.7 10.0 %copy-start.2 = (bf16[512,512]{1,0:T(8,128)(2,1)S(1)}, bf16[512,512]{1,0:T(8,128)(2,1)}, u32[]{:S(2)}) copy-start(bf16[512,512]{1,0:T(8,128)(2,1)} %wno_ref.3) | copy-start | bytes 1572868
  3.3 13.7 %all-to-all-start = ((s32[8,1,128]{2,1,0:T(1,128)}), s32[8,1,128]{2,1,0:T(1,128)S(1)}, u32[]{:S(2)}, u32[]{:S(2)}) async-start(s32[8,1,128]{2,1,0:T(1,128)} %bitcast.5), calls=%async_computation | async-start | bytes 8192 | tf_op jit(solution)/shard_map/all_to_all | solution.py:307
  10.7 11.7 %copy-start.28 = (bf16[227,512]{1,0:T(8,128)(2,1)S(1)}, bf16[227,512]{1,0:T(8,128)(2,1)}, u32[]{:S(2)}) copy-start(bf16[227,512]{1,0:T(8,128)(2,1)} %win_ref.1) | copy-start | bytes 697348
  10.7 11.7 %copy-start.29 = (f32[512]{0:T(512)S(1)}, f32[512]{0:T(512)}, u32[]{:S(2)}) copy-start(f32[512]{0:T(512)} %param.23) | copy-start | bytes 6148
  10.7 11.7 %copy-start.30 = (f32[512]{0:T(512)S(1)}, f32[512]{0:T(512)}, u32[]{:S(2)}) copy-start(f32[512]{0:T(512)} %param.25) | copy-start | bytes 6148
  19.0 19.9 %all-to-all-start.1 = ((bf16[8,48,512]{2,1,0:T(8,128)(2,1)}), bf16[8,48,512]{2,1,0:T(8,128)(2,1)S(1)}, u32[]{:S(2)}, u32[]{:S(2)}) async-start(bf16[8,48,512]{2,1,0:T(8,128)(2,1)} %bitcast.8), calls=%async_computation.1 | async-start | bytes 786432 | tf_op jit(solution)/shard_map/all_to_all | solution.py:307
  24.5 5.6 %copy-start.43 = (s32[4096]{0:T(1024)S(1)}, s32[4096]{0:T(1024)}, u32[]{:S(2)}) copy-start(s32[4096]{0:T(1024)} %param.20) | copy-start | bytes 49156
  31.4 7.5 %copy-start.31 = (f32[512]{0:T(512)S(1)}, f32[512]{0:T(512)}, u32[]{:S(2)}) copy-start(f32[512]{0:T(512)} %param.28) | copy-start | bytes 6148
  48.2 16.4 %all-to-all-start.3 = ((bf16[8,48,512]{2,1,0:T(8,128)(2,1)}), bf16[8,48,512]{2,1,0:T(8,128)(2,1)S(1)}, u32[]{:S(2)}, u32[]{:S(2)}) async-start(bf16[8,48,512]{2,1,0:T(8,128)(2,1)} %bitcast.13), calls=%async_computation.3 | async-start | bytes 786432 | tf_op jit(solution)/shard_map/all_to_all | solution.py:307
  76.9 17.6 %all-to-all-start.6 = ((bf16[8,48,512]{2,1,0:T(8,128)(2,1)}), bf16[8,48,512]{2,1,0:T(8,128)(2,1)}, u32[]{:S(2)}, u32[]{:S(2)}) async-start(bf16[8,48,512]{2,1,0:T(8,128)(2,1)} %bitcast.32), calls=%async_computation.6 | async-start | bytes 786432 | tf_op jit(solution)/shard_map/all_to_all | solution.py:307
  94.5 20.2 %all-to-all-start.2 = ((bf16[8,48,512]{2,1,0:T(8,128)(2,1)}), bf16[8,48,512]{2,1,0:T(8,128)(2,1)S(1)}, u32[]{:S(2)}, u32[]{:S(2)}) async-start(bf16[8,48,512]{2,1,0:T(8,128)(2,1)} %bitcast.33), calls=%async_computation.2 | async-start | bytes 786432 | tf_op jit(solution)/shard_map/all_to_all | solution.py:307
  114.7 7.6 %collective-permute-start.2 = (bf16[256,512]{1,0:T(8,128)(2,1)}, bf16[256,512]{1,0:T(8,128)(2,1)}, u32[]{:S(2)}, u32[]{:S(2)}) collective-permute-start(bf16[256,512]{1,0:T(8,128)(2,1)} %constant_dynamic-slice_fusion), channel_id=1, source_target_pairs={{0,8},{8,0},{1,9},{9,1},{2,10},{10,2},{3,11},{11,3},{4,12},{12,4},... | collective-permute-start | bytes 786440 | tf_op jit(solution)/shard_map/ppermute | solution.py:262
  121.7 9.4 %collective-permute-start = (bf16[512,512]{1,0:T(8,128)(2,1)S(1)}, bf16[512,512]{1,0:T(8,128)(2,1)S(1)}, u32[]{:S(2)}, u32[]{:S(2)}) collective-permute-start(bf16[512,512]{1,0:T(8,128)(2,1)S(1)} %constant_dynamic-slice_fusion.1), channel_id=1, source_target_pairs={{0,8},{8,0},{1,9},{9,1},{2,10},{10,2},{3,11},{11,3},{4,12},{12,4},... | collective-permute-start | bytes 1572872 | tf_op jit(solution)/shard_map/ppermute | solution.py:262
  124.1 17.1 %all-to-all-start.7 = ((bf16[16,16,512]{2,1,0:T(8,128)(2,1)}), bf16[16,16,512]{2,1,0:T(8,128)(2,1)S(1)}, u32[]{:S(2)}, u32[]{:S(2)}) async-start(bf16[16,16,512]{2,1,0:T(8,128)(2,1)} %bitcast.19), calls=%async_computation.7 | async-start | bytes 524288 | tf_op jit(solution)/shard_map/all_to_all | solution.py:264
  141.2 18.1 %all-to-all-start.4 = ((bf16[16,32,512]{2,1,0:T(8,128)(2,1)}), bf16[16,32,512]{2,1,0:T(8,128)(2,1)S(1)}, u32[]{:S(2)}, u32[]{:S(2)}) async-start(bf16[16,32,512]{2,1,0:T(8,128)(2,1)} %bitcast.15), calls=%async_computation.4 | async-start | bytes 1048576 | tf_op jit(solution)/shard_map/all_to_all | solution.py:264
  160.1 12.0 %all-to-all-start.8 = ((bf16[16,16,512]{2,1,0:T(8,128)(2,1)}), bf16[16,16,512]{2,1,0:T(8,128)(2,1)S(1)}, u32[]{:S(2)}, u32[]{:S(2)}) async-start(bf16[16,16,512]{2,1,0:T(8,128)(2,1)} %broadcast_in_dim.5), calls=%async_computation.8 | async-start | bytes 524288 | tf_op jit(solution)/shard_map/all_to_all | solution.py:267
  172.9 17.1 %all-to-all-start.5 = ((bf16[16,32,512]{2,1,0:T(8,128)(2,1)}), bf16[16,32,512]{2,1,0:T(8,128)(2,1)S(1)}, u32[]{:S(2)}, u32[]{:S(2)}) async-start(bf16[16,32,512]{2,1,0:T(8,128)(2,1)} %broadcast_in_dim.4), calls=%async_computation.5 | async-start | bytes 1048576 | tf_op jit(solution)/shard_map/all_to_all | solution.py:267
  176.5 13.5 %collective-permute-start.3 = (bf16[256,512]{1,0:T(8,128)(2,1)S(1)}, bf16[256,512]{1,0:T(8,128)(2,1)S(1)}, u32[]{:S(2)}, u32[]{:S(2)}) collective-permute-start(bf16[256,512]{1,0:T(8,128)(2,1)S(1)} %bitcast.43), channel_id=1, source_target_pairs={{0,8},{8,0},{1,9},{9,1},{2,10},{10,2},{3,11},{11,3},{4,12},{12,4},... | collective-permute-start | bytes 786440 | tf_op jit(solution)/shard_map/ppermute | solution.py:268
  190.0 1.9 collective-permute-start.1
  (33 other events, 41.0 us)

commit v2 on v1

--- a/solution.py
+++ b/solution.py
@@ -50,7 +50,7 @@
     )
 
 
-def call(kernel, name, out, args, flops, grid=None, in_specs=None, out_specs=None, scratch=(), vmem=24):
+def call(kernel, name, out, args, flops, grid=None, in_specs=None, out_specs=None, scratch=(), vmem=60):
     moved = sum(a.size * a.dtype.itemsize for a in args)
     moved += sum(o.size * o.dtype.itemsize for o in out)
     extra = {}
@@ -155,120 +155,139 @@
     asked_ref[...] = dot(onehot, pm_ref[...]).astype(BF16)
 
 
-def pre_act(slot, pg, pm, bias):
-    onehot = edges_by_ids(slot, pm.shape[0])
-    return dot(onehot, pm) + pg.astype(F32) + bias
-
-
-def edge_kernel(steps, slot_ref, pg_ref, pm_ref, be_ref, sum_ref, total):
+def edge_kernel(steps, slot_ref, pg_ref, pm_ref, be_ref, we_ref, slope_ref, sums_ref, act_ref, acts, slopes):
     step = pl.program_id(0)
 
     @pl.when(step == 0)
     def _():
-        total[...] = jnp.zeros_like(total)
+        acts[...] = jnp.zeros_like(acts)
+        slopes[...] = jnp.zeros_like(slopes)
 
     slot = slot_ref[...]
-    pre = pre_act(slot, pg_ref[...], pm_ref[...], be_ref[...])
-    act = (pre * sigmoid(pre)).astype(BF16)
-    total[...] += dot(ids_by_edges(slot, total.shape[0]), act)
+    slots, width = acts.shape
+    pre = dot(edges_by_ids(slot, slots), pm_ref[...]) + pg_ref[...].astype(F32) + be_ref[...]
+    s = sigmoid(pre)
+    act = pre * s
+    slope = s * (1.0 + pre - act)
+    slope_ref[...] = slope
+    onehot_t = ids_by_edges(slot, slots)
+    acts[...] += dot(onehot_t, act.astype(BF16))
+    slopes[...] += dot(onehot_t, slope.astype(BF16))
 
     @pl.when(step == steps - 1)
     def _():
-        sum_ref[...] = total[...].astype(BF16)
-
-
-def slope_kernel(steps, slot_ref, pg_ref, pm_ref, be_ref, slope_ref, sum_ref, total):
-    step = pl.program_id(0)
-
-    @pl.when(step == 0)
-    def _():
-        total[...] = jnp.zeros_like(total)
-
-    slot = slot_ref[...]
-    pre = pre_act(slot, pg_ref[...], pm_ref[...], be_ref[...])
-    s = sigmoid(pre)
-    slope = s * (1.0 + pre * (1.0 - s))
-    slope_ref[...] = slope
-    total[...] += dot(ids_by_edges(slot, total.shape[0]), slope.astype(BF16))
-
-    @pl.when(step == steps - 1)
-    def _():
-        sum_ref[...] = total[...].astype(BF16)
-
-
-def node_kernel(
-    rec_ref, row_ref, oh_ref, self_ref, cw_ref, we_ref, wa_ref,
-    hask_ref, act_ref, h_ref, gagg_ref, gnode_ref, nact_ref,
-):
-    nodes = self_ref.shape[0]
+        total = acts[...]
+        high = total.astype(BF16)
+        low = (total - high.astype(F32)).astype(BF16)
+        act_ref[...] = high
+        sums_ref[:, :width] = (dot(high, we_ref[...]) + dot(low, we_ref[...])).astype(BF16)
+        sums_ref[:, width:] = slopes[...].astype(BF16)
+
+
+def node_kernel(rec_ref, row_ref, oh_ref, self_ref, cw_ref, wa_ref, gask_ref, gagg_ref, gnode_ref, nact_ref):
+    nodes, width = self_ref.shape
     onehot_t = as_bf16(lax.broadcasted_iota(jnp.int32, (nodes, row_ref.shape[1]), 0) == row_ref[...])
-    act = dot(onehot_t, rec_ref[...]).astype(BF16)
-    agg = dot(act, we_ref[...]).astype(BF16)
+    agg = dot(onehot_t, rec_ref[:, :width]).astype(BF16)
     pre = self_ref[...] + dot(agg, wa_ref[...])
     s = sigmoid(pre)
-    g_node = (cw_ref[...] * (s * (1.0 + pre * (1.0 - s)))).astype(BF16)
+    act = pre * s
+    g_node = (cw_ref[...] * (s * (1.0 + pre - act))).astype(BF16)
     g_agg = dot_nt(g_node, wa_ref[...]).astype(BF16)
-    h = dot_nt(g_agg, we_ref[...])
-    hask_ref[...] = dot(oh_ref[...], h.astype(BF16)).astype(BF16)
-    act_ref[...] = act
-    h_ref[...] = h
+    gask_ref[...] = dot(oh_ref[...], g_agg).astype(BF16)
     gagg_ref[...] = g_agg
     gnode_ref[...] = g_node
-    nact_ref[...] = (pre * s).astype(BF16)
+    nact_ref[...] = act.astype(BF16)
 
 
 def node_post_kernel(
-    rec_ref, row_ref, act_ref, h_ref, gagg_ref, gnode_ref, nact_ref, ml_ref, cot_ref,
-    wno_ref, ws_ref, um_ref, mo_ref, gm_ref, grads_ref,
+    rec_ref, row_ref, gagg_ref, gnode_ref, nact_ref, ml_ref, cot_ref,
+    we_ref, wno_ref, ws_ref, um_ref, mo_ref, gm_ref, keep_ref, give_ref,
 ):
-    nodes, width = h_ref.shape
+    nodes, width = gagg_ref.shape
+    half = width // 2
     ml = ml_ref[...]
     onehot_t = as_bf16(lax.broadcasted_iota(jnp.int32, (nodes, row_ref.shape[1]), 0) == row_ref[...])
-    slopes = dot(onehot_t, rec_ref[...])
-    g_pmesh = (h_ref[...] * slopes).astype(BF16)
-    grads_ref[:width, :] = dot_tn(act_ref[...], gagg_ref[...]).astype(BF16)
-    grads_ref[width:, :] = dot_tn(ml, g_pmesh).astype(BF16)
+    slopes = dot(onehot_t, rec_ref[:, width:])
+    g_pmesh = (dot_nt(gagg_ref[...], we_ref[...]) * slopes).astype(BF16)
+    grad = dot_tn(ml, g_pmesh).astype(BF16)
+    put_halves(grad[:half], grad[half:], keep_ref, give_ref)
     mo_ref[...] = (ml.astype(F32) + dot(nact_ref[...], wno_ref[...])).astype(BF16)
     gm_ref[...] = (
         cot_ref[...].astype(F32) + dot_nt(gnode_ref[...], ws_ref[...]) + dot_nt(g_pmesh, um_ref[...])
     ).astype(BF16)
 
 
-def edge_back_kernel(steps, slot_ref, slope_ref, lat_t_ref, h_ref, out_ref, total):
+def put_halves(first, second, keep_ref, give_ref):
+    core = lax.axis_index("core")
+
+    @pl.when(core == 0)
+    def _():
+        keep_ref[...] = first
+        give_ref[...] = second
+
+    @pl.when(core != 0)
+    def _():
+        keep_ref[...] = second
+        give_ref[...] = first
+
+
+def edge_back_kernel(
+    steps, slot_ref, slope_ref, lat_t_ref, gc_ref, act_ref, we_ref, keep_ref, give_ref, total, h
+):
     step = pl.program_id(0)
 
     @pl.when(step == 0)
     def _():
         total[...] = jnp.zeros_like(total)
-
-    onehot = edges_by_ids(slot_ref[...], h_ref.shape[0])
-    g_edge = (dot(onehot, h_ref[...]) * slope_ref[...]).astype(BF16)
+        h[...] = dot_nt(gc_ref[...], we_ref[...]).astype(BF16)
+
+    onehot = edges_by_ids(slot_ref[...], h.shape[0])
+    g_edge = (dot(onehot, h[...]) * slope_ref[...]).astype(BF16)
     total[...] += dot(lat_t_ref[...], g_edge)
 
     @pl.when(step == steps - 1)
     def _():
-        out_ref[...] = total[...].astype(BF16)
-
-
-def all_sum(value, scale):
-    rows, width = value.shape
-    half = rows // 2
+        grad_edge = dot_tn(act_ref[...], gc_ref[...]).astype(BF16)
+        put_halves(total[...].astype(BF16), grad_edge, keep_ref, give_ref)
+
+
+def add_kernel(keep_ref, got_ref, out_ref):
+    out_ref[...] = (keep_ref[...].astype(F32) + got_ref[...].astype(F32)).astype(BF16)
+
+
+def spread_kernel(scale, umesh_ref, pair_ref, out_ref):
+    low, high = umesh_ref.shape[1], pair_ref.shape[1]
+    umesh = jnp.sum(umesh_ref[...].astype(F32), axis=0) * scale
+    pair = jnp.sum(pair_ref[...].astype(F32), axis=0) * scale
+    total = jnp.concatenate([umesh, pair], axis=0).astype(BF16)
+    out_ref[...] = jnp.broadcast_to(total[None], out_ref.shape)
+
+
+def finish_kernel(mine_ref, other_ref, edge_ref, ugrid_ref, umesh_ref):
+    count, _, width = mine_ref.shape
+    low = umesh_ref.shape[0] // 2 // count
     core = lax.axis_index("core")
-    pairs = [(0, 1), (1, 0)]
-    others = ("x", "mesh")
-    count = lax.axis_size("x") * lax.axis_size("mesh")
-    keep = lax.dynamic_slice_in_dim(value, core * half, half, 0)
-    give = lax.dynamic_slice_in_dim(value, (1 - core) * half, half, 0)
-    got = lax.ppermute(give, "core", pairs)
-    part = (keep.astype(F32) + got.astype(F32)).astype(BF16)
-    pieces = lax.all_to_all(part, others, 0, 0, tiled=True).reshape(count, half // count, width)
-    total = (jnp.sum(pieces.astype(F32), axis=0) * scale).astype(BF16)
-    copies = jnp.broadcast_to(total[None], pieces.shape).reshape(half, width)
-    mine = lax.all_to_all(copies, others, 0, 0, tiled=True)
-    other = lax.ppermute(mine, "core", pairs)
-    first = jnp.where(core == 0, mine, other)
-    second = jnp.where(core == 0, other, mine)
-    return jnp.concatenate([first, second], axis=0).astype(F32)
+
+    def put(first_ref, second_ref):
+        half = count * low
+        umesh_ref[:half] = first_ref[:, :low].astype(F32).reshape(half, width)
+        umesh_ref[half:] = second_ref[:, :low].astype(F32).reshape(half, width)
+        ugrid_ref[...] = first_ref[:, low:].astype(F32).reshape(2 * half, width)
+        edge_ref[...] = second_ref[:, low:].astype(F32).reshape(2 * half, width)
+
+    @pl.when(core == 0)
+    def _():
+        put(mine_ref, other_ref)
+
+    @pl.when(core != 0)
+    def _():
+        put(other_ref, mine_ref)
+
+
+def pair_sum(keep, give, name):
+    got = lax.ppermute(give, "core", [(0, 1), (1, 0)])
+    (out,) = call(add_kernel, name, [jax.ShapeDtypeStruct(keep.shape, BF16)], [keep, got], keep.size)
+    return out
 
 
 def shards(
@@ -382,69 +401,77 @@
     incoming_row = incoming[:, :CAP].reshape(1, slots)
     slot_pmesh = exchange(asked)
 
-    bias = b_edge.reshape(1, width)
-    forward_specs = [id_spec, edge_spec, whole((slots, width)), whole((1, width))]
-    total = [pltpu.VMEM((slots, width), F32)]
-    (act_sums,) = call(
+    sums_b = sds((slots, width), BF16)
+    slope, sums, act_sums = call(
         functools.partial(edge_kernel, steps),
         "edge",
-        [sds((slots, width), BF16)],
-        [slot, edge_pgrid, slot_pmesh, bias],
-        4 * edge_dev * slots * width,
+        [sds((edge_dev, width), F32), sds((slots, 2 * width), BF16), sums_b],
+        [slot, edge_pgrid, slot_pmesh, b_edge.reshape(1, width), w_edge],
+        6 * edge_dev * slots * width,
         grid=(steps,),
-        in_specs=forward_specs,
-        out_specs=[whole((slots, width))],
-        scratch=total,
-    )
-    act_received = exchange(act_sums)
-    slope, slope_sums = call(
-        functools.partial(slope_kernel, steps),
-        "slope",
-        [sds((edge_dev, width), F32), sds((slots, width), BF16)],
-        [slot, edge_pgrid, slot_pmesh, bias],
-        4 * edge_dev * slots * width,
-        grid=(steps,),
-        in_specs=forward_specs,
-        out_specs=[edge_spec, whole((slots, width))],
-        scratch=total,
-    )
-    slope_received = exchange(slope_sums)
+        in_specs=[id_spec, edge_spec, whole((slots, width)), whole((1, width)), whole((width, width))],
+        out_specs=[edge_spec, whole((slots, 2 * width)), whole((slots, width))],
+        scratch=[pltpu.VMEM((slots, width), F32), pltpu.VMEM((slots, width), F32)],
+    )
+    received = exchange(sums)
 
     node_b = sds((mesh_dev, width), BF16)
-    h_asked, act_total, h, g_agg, g_node, node_act = call(
+    g_asked, g_agg, g_node, node_act = call(
         node_kernel,
         "node",
-        [sds((slots, width), BF16), node_b, sds((mesh_dev, width), F32), node_b, node_b, node_b],
-        [act_received, incoming_row, onehot_in, self_part, cot_part, w_edge, w_agg],
-        8 * mesh_dev * width * width + 4 * mesh_dev * slots * width,
-    )
-    slot_h = exchange(h_asked)
-
-    mesh_out, grad_mesh, owner_grads = call(
+        [sums_b, node_b, node_b, node_b],
+        [received, incoming_row, onehot_in, self_part, cot_part, w_agg],
+        4 * mesh_dev * width * width + 4 * mesh_dev * slots * width,
+    )
+    slot_g = exchange(g_asked)
+
+    half = sds((width // 2, width), BF16)
+    mesh_out, grad_mesh, keep, give = call(
         node_post_kernel,
         "node_post",
-        [node_b, node_b, sds((2 * width, width), BF16)],
+        [node_b, node_b, half, half],
         [
-            slope_received, incoming_row, act_total, h, g_agg, g_node, node_act,
-            mesh_latent, cotangent, w_node_out, w_self, u_mesh,
+            received, incoming_row, g_agg, g_node, node_act, mesh_latent, cotangent,
+            w_edge, w_node_out, w_self, u_mesh,
         ],
         10 * mesh_dev * width * width + 2 * mesh_dev * slots * width,
     )
-    owner_total = all_sum(owner_grads, scale)
-
-    (local_ugrid,) = call(
+    others = ("x", "mesh")
+    count = lax.axis_size("x") * owners
+    umesh_parts = lax.all_to_all(pair_sum(keep, give, "add_umesh"), others, 0, 0, tiled=True)
+
+    full = sds((width, width), BF16)
+    keep, give = call(
         functools.partial(edge_back_kernel, steps),
         "edge_back",
-        [sds((width, width), BF16)],
-        [slot, slope, edge_latent_t, slot_h],
+        [full, full],
+        [slot, slope, edge_latent_t, slot_g, act_sums, w_edge],
         2 * edge_dev * (slots + width) * width,
         grid=(steps,),
-        in_specs=[id_spec, edge_spec, edge_t_spec, whole((slots, width))],
-        out_specs=[whole((width, width))],
-        scratch=[pltpu.VMEM((width, width), F32)],
-    )
-    grad_ugrid = all_sum(local_ugrid, scale)
-    return mesh_out, grad_mesh, owner_total[:width], grad_ugrid, owner_total[width:]
+        in_specs=[
+            id_spec, edge_spec, edge_t_spec, whole((slots, width)), whole((slots, width)),
+            whole((width, width)),
+        ],
+        out_specs=[whole((width, width)), whole((width, width))],
+        scratch=[pltpu.VMEM((width, width), F32), pltpu.VMEM((slots, width), BF16)],
+    )
+    pair_parts = lax.all_to_all(pair_sum(keep, give, "add_pair"), others, 0, 0, tiled=True)
+
+    low = width // 2 // count
+    (copies,) = call(
+        functools.partial(spread_kernel, scale),
+        "spread",
+        [sds((count, 3 * low, width), BF16)],
+        [umesh_parts.reshape(count, low, width), pair_parts.reshape(count, 2 * low, width)],
+        3 * count * low * width,
+    )
+    mine = lax.all_to_all(copies, others, 0, 0, tiled=True)
+    other = lax.ppermute(mine, "core", [(0, 1), (1, 0)])
+    weight = sds((width, width), F32)
+    grad_edge, grad_ugrid, grad_umesh = call(
+        finish_kernel, "finish", [weight, weight, weight], [mine, other], 3 * width * width
+    )
+    return mesh_out, grad_mesh, grad_edge, grad_ugrid, grad_umesh
 
 
 def solution(mesh):

time: 196 us -> 181 us (0.923)
  blocking collectives: 0 us -> 41.7 us
  local copies, waits for them, and re-layouts: 40.1 us -> 6.99 us
  waiting for transfers between devices: 58.1 us -> 30.1 us
  Pallas kernels: 43.1 us -> 70.4 us
  starting transfers between devices: 45.1 us -> 28.1 us
  other arithmetic: 6.31 us -> 1.99 us
    all_to_all x0 -> x2, blocking collectives: none -> 41.7 us  [the longest x1 23.5 us: shards(): mine = lax.all_to_all(copies, others, 0, 0, tiled=True)]
    all_to_all x4 -> x1, waiting for transfers between devices: 44.3 us -> 7.12 us  [shards(): lax.all_to_all(pair_sum(keep, give, 'add_umesh'), others, 0, 0, tiled=True)]
    unnamed x89 -> x25, local copies, waits for them, and re-layouts: 36.1 us -> 6.37 us
    pallas_call x11 -> x14, Pallas kernels: 43.1 us -> 70.4 us  [call(): pl.pallas_call(kernel, out_shape=out, scratch_shapes=scratch, name=name,...]
    all_to_all x4 -> x1, starting transfers between devices: 17.8 us -> 7.04 us  [shards(): lax.all_to_all(pair_sum(keep, give, 'add_umesh'), others, 0, 0, tiled=True)]
    all_to_all x5 -> x4, waiting for transfers between devices: 13.1 us -> 20.7 us  [exchange(): return lax.all_to_all(value, 'mesh', 0, 0, tiled=True)]
    all_to_all x5 -> x4, starting transfers between devices: 26.7 us -> 20.6 us  [exchange(): return lax.all_to_all(value, 'mesh', 0, 0, tiled=True)]
    convert_element_type x6 -> x0, other arithmetic: 5.16 us -> none  [the longest x2 3.77 us: all_sum(): part = (keep.astype(F32) + got.astype(F32)).astype(BF16)]
  transfers between devices with their start and end apart: 13 -> 8, of which waited for: 7 -> 4; matrix products, arithmetic and copies ran while one was open for 4% -> 1% of each run, Pallas kernels for 16% -> 24%
where the time goes in v2:
time: 181 us; the launch traced here: 180 us
  Pallas kernels  70.4 us (39%)
  blocking collectives  41.7 us (23%)
  waiting for transfers between devices  30.1 us (17%)
  starting transfers between devices  28.1 us (16%)
  local copies, waits for them, and re-layouts  6.99 us (4%)
  other arithmetic  1.99 us (1%)
    pallas_call x14, Pallas kernels, call(): pl.pallas_call(kernel, out_shape=out, scratch_shapes=scratch, name=name,...  70.4 us
    all_to_all x1, blocking collectives, shards(): mine = lax.all_to_all(copies, others, 0, 0, tiled=True)  23.5 us
    all_to_all x4, waiting for transfers between devices, exchange(): return lax.all_to_all(value, 'mesh', 0, 0, tiled=True)  20.7 us
    all_to_all x4, starting transfers between devices, exchange(): return lax.all_to_all(value, 'mesh', 0, 0, tiled=True)  20.6 us
    all_to_all x1, blocking collectives, shards(): lax.all_to_all(pair_sum(keep, give, 'add_pair'), others, 0, 0, tiled=True)  18.2 us
    all_to_all x1, waiting for transfers between devices, shards(): lax.all_to_all(pair_sum(keep, give, 'add_umesh'), others, 0, 0, tiled=True)  7.12 us
    all_to_all x1, starting transfers between devices, shards(): lax.all_to_all(pair_sum(keep, give, 'add_umesh'), others, 0, 0, tiled=True)  7.04 us
    unnamed x25, local copies, waits for them, and re-layouts  6.37 us
  transfers between devices with their start and end apart: 8, of which 4 were waited for; matrix products, arithmetic and copies ran while one was open for 1% of the time, Pallas kernels for 24%

profile of v2, /device:TPU:0, one launch (start us, length us, event | category | flops | bytes accessed | tf_op | source)
XLA Modules:
  0.0 180.1 jit_solution(1066119603468096827)
XLA Ops:
  2.0 2.5 %prep.1 = (s32[32,128]{1,0:T(8,128)}, s32[8,128]{1,0:T(8,128)}) custom-call(s32[32,128]{1,0:T(8,128)} %subtract_bitcast_fusion.1.em_ref), custom_call_target="tpu_custom_call" | custom-call | flops 1000000000 | bytes 36864 | tf_op jit(solution)/shard_map/prep/pallas_call | solution.py:59
  4.5 7.3 %all-to-all-start = ((s32[8,1,128]{2,1,0:T(1,128)}), s32[8,1,128]{2,1,0:T(1,128)S(1)}, u32[]{:S(2)}, u32[]{:S(2)}) async-start(s32[8,1,128]{2,1,0:T(1,128)} %bitcast.32), calls=%async_computation | async-start | bytes 8192 | tf_op jit(solution)/shard_map/all_to_all | solution.py:326
  11.8 3.1 %node_pre.1 = (bf16[320,512]{1,0:T(8,128)(2,1)}, f32[320,512]{1,0:T(8,128)}, f32[320,512]{1,0:T(8,128)}) custom-call(bf16[320,512]{1,0:T(8,128)(2,1)} %ml_ref.3, bf16[320,512]{1,0:T(8,128)(2,1)} %cot_ref.3, bf16[512,512]{1,0:T(8,128)(2,1)} %um_ref.3, bf16[512,512]{1,0:T(8,128)(2,1)} %ws_ref.3, f32[1,512]{1,0:T(1,128)} %bitcast.33, bf16[512,512]{1,0:T(8,128)(2,1)} %wno_ref.3), custom_call_target="tpu_custom_call" | custom-call | flops 503316480 | bytes 3868672 | tf_op jit(solution)/shard_map/node_pre/pallas_call | solution.py:59
  15.9 2.2 %all-to-all-done = s32[8,1,128]{2,1,0:T(1,128)S(1)} async-done(((s32[8,1,128]{2,1,0:T(1,128)}), s32[8,1,128]{2,1,0:T(1,128)S(1)}, u32[]{:S(2)}, u32[]{:S(2)}) %all-to-all-start) | async-done | bytes 4128 | tf_op jit(solution)/shard_map/all_to_all | solution.py:326
  18.8 2.2 %ask.1 = (bf16[384,512]{1,0:T(8,128)(2,1)}, bf16[384,320]{1,0:T(8,128)(2,1)}) custom-call(s32[8,128]{1,0:T(8,128)} %bitcast.30, bf16[320,512]{1,0:T(8,128)(2,1)} %get-tuple-element.33.pm_ref), custom_call_target="tpu_custom_call" | custom-call | flops 125829120 | bytes 970752 | tf_op jit(solution)/shard_map/ask/pallas_call | solution.py:59
  21.0 3.8 %all-to-all-start.1 = ((bf16[8,48,512]{2,1,0:T(8,128)(2,1)}), bf16[8,48,512]{2,1,0:T(8,128)(2,1)S(1)}, u32[]{:S(2)}, u32[]{:S(2)}) async-start(bf16[8,48,512]{2,1,0:T(8,128)(2,1)} %bitcast.28), calls=%async_computation.1 | async-start | bytes 786432 | tf_op jit(solution)/shard_map/all_to_all | solution.py:326
  24.7 5.8 %embed.1 = (bf16[512,1024]{1,0:T(8,128)(2,1)}, bf16[1024,512]{1,0:T(8,128)(2,1)}) custom-call(bf16[1024,227]{1,0:T(8,128)(2,1)} %copy.23.gv_ref, bf16[227,512]{1,0:T(8,128)(2,1)} %win_ref.1, f32[1,512]{1,0:T(1,128)} %bitcast.34, bf16[512,512]{1,0:T(8,128)(2,1)} %wout_ref.1, f32[1,512]{1,0:T(1,128)} %bitcast.35, bf16[512,512]{1,0:T(8,128)(2,1)} %ug_ref.1), custom_call_target="tpu_custom_call" | custom-call | flops 1311768576 | bytes 3847168 | tf_op jit(solution)/shard_map/embed/pallas_call | solution.py:59
  31.2 7.8 %take_grid.1.pg_ref = bf16[4096,512]{1,0:T(8,128)(2,1)} custom-call(s32[32,128]{1,0:T(8,128)} %subtract_bitcast_fusion.ids_ref, bf16[1024,512]{1,0:T(8,128)(2,1)} %get-tuple-element.31.pg_ref), custom_call_target="tpu_custom_call" | custom-call | flops 4294967296 | bytes 5259264 | tf_op jit(solution)/shard_map/take_grid/pallas_call | solution.py:59
  39.7 13.0 %edge.1 = (f32[4096,512]{1,0:T(8,128)}, bf16[384,1024]{1,0:T(8,128)(2,1)}, bf16[384,512]{1,0:T(8,128)(2,1)}) custom-call(s32[32,128]{1,0:T(8,128)} %get-tuple-element.30.slot_ref, bf16[4096,512]{1,0:T(8,128)(2,1)} %take_grid.1.pg_ref, bf16[384,512]{1,0:T(8,128)(2,1)} %bitcast.27, f32[1,512]{1,0:T(1,128)} %bitcast.36, bf16[512,512]{1,0:T(8,128)(2,1)} %we_ref.5), custom_call_target="tpu_custom_call" | custom-call | flops 4831838208 | bytes 14698496 | tf_op jit(solution)/shard_map/edge/pallas_call | solution.py:59
  52.7 6.0 %all-to-all-start.2 = ((bf16[8,48,1024]{2,1,0:T(8,128)(2,1)}), bf16[8,48,1024]{2,1,0:T(8,128)(2,1)S(1)}, u32[]{:S(2)}, u32[]{:S(2)}) async-start(bf16[8,48,1024]{2,1,0:T(8,128)(2,1)} %bitcast.26), calls=%async_computation.2 | async-start | bytes 1572864 | tf_op jit(solution)/shard_map/all_to_all | solution.py:326
  59.3 18.5 %all-to-all-done.2 = bf16[8,48,1024]{2,1,0:T(8,128)(2,1)S(1)} async-done(((bf16[8,48,1024]{2,1,0:T(8,128)(2,1)}), bf16[8,48,1024]{2,1,0:T(8,128)(2,1)S(1)}, u32[]{:S(2)}, u32[]{:S(2)}) %all-to-all-start.2) | async-done | bytes 786464 | tf_op jit(solution)/shard_map/all_to_all | solution.py:326
  78.7 3.8 %node.1 = (bf16[384,512]{1,0:T(8,128)(2,1)}, bf16[320,512]{1,0:T(8,128)(2,1)}, bf16[320,512]{1,0:T(8,128)(2,1)}, bf16[320,512]{1,0:T(8,128)(2,1)}) custom-call(bf16[384,1024]{1,0:T(8,128)(2,1)} %bitcast.21, s32[1,384]{1,0:T(1,128)} %reshape.53.row_ref, bf16[384,320]{1,0:T(8,128)(2,1)} %get-tuple-element.36.oh_ref, f32[320,512]{1,0:T(8,128)} %get-tuple-element.37.self_ref, ...), custom_call_target="tpu_custom_call" | custom-call | flops 587202560 | bytes 4244992 | tf_op jit(solution)/shard_map/node/pallas_call | solution.py:59
  82.5 3.5 %all-to-all-start.4 = ((bf16[8,48,512]{2,1,0:T(8,128)(2,1)}), bf16[8,48,512]{2,1,0:T(8,128)(2,1)S(1)}, u32[]{:S(2)}, u32[]{:S(2)}) async-start(bf16[8,48,512]{2,1,0:T(8,128)(2,1)} %bitcast.29), calls=%async_computation.4 | async-start | bytes 786432 | tf_op jit(solution)/shard_map/all_to_all | solution.py:326
  86.0 7.3 %take_latent.1.lat_t_ref = bf16[512,4096]{1,0:T(8,128)(2,1)} custom-call(s32[32,128]{1,0:T(8,128)} %subtract_bitcast_fusion.ids_ref, bf16[512,1024]{1,0:T(8,128)(2,1)} %get-tuple-element.47.lat_t_ref), custom_call_target="tpu_custom_call" | custom-call | flops 4294967296 | bytes 5259264 | tf_op jit(solution)/shard_map/take_latent/pallas_call | solution.py:59
  93.4 4.7 %node_post.1 = (bf16[320,512]{1,0:T(8,128)(2,1)}, bf16[320,512]{1,0:T(8,128)(2,1)}, bf16[256,512]{1,0:T(8,128)(2,1)}, bf16[256,512]{1,0:T(8,128)(2,1)}) custom-call(bf16[384,1024]{1,0:T(8,128)(2,1)} %bitcast.22, s32[1,384]{1,0:T(1,128)} %reshape.53.row_ref, bf16[320,512]{1,0:T(8,128)(2,1)} %get-tuple-element.39.gagg_ref, ...), custom_call_target="tpu_custom_call" | custom-call | flops 964689920 | bytes 5703168 | tf_op jit(solution)/shard_map/node_post/pallas_call | solution.py:59
  98.8 10.9 %edge_back.1 = (bf16[512,512]{1,0:T(8,128)(2,1)}, bf16[512,512]{1,0:T(8,128)(2,1)}) custom-call(s32[32,128]{1,0:T(8,128)} %get-tuple-element.30.slot_ref, f32[4096,512]{1,0:T(8,128)} %get-tuple-element.46.slope_ref, bf16[512,4096]{1,0:T(8,128)(2,1)} %take_latent.1.lat_t_ref, bf16[384,512]{1,0:T(8,128)(2,1)} %bitcast.24, ...), custom_call_target="tpu_custom_call" | custom-call | flops 3758096384 | bytes 14958592 | tf_op jit(solution)/shard_map/edge_back/pallas_call | solution.py:59
  112.7 7.0 %all-to-all-start.3 = ((bf16[16,16,512]{2,1,0:T(8,128)(2,1)}), bf16[16,16,512]{2,1,0:T(8,128)(2,1)S(1)}, u32[]{:S(2)}, u32[]{:S(2)}) async-start(bf16[16,16,512]{2,1,0:T(8,128)(2,1)} %bitcast.25), calls=%async_computation.3 | async-start | bytes 524288 | tf_op jit(solution)/shard_map/all_to_all | solution.py:441
  120.6 2.1 %add_pair.1 = bf16[512,512]{1,0:T(8,128)(2,1)} custom-call(bf16[512,512]{1,0:T(8,128)(2,1)} %get-tuple-element.50.keep_ref, bf16[512,512]{1,0:T(8,128)(2,1)} %copy-done.5), custom_call_target="tpu_custom_call" | custom-call | flops 262144 | bytes 1572864 | tf_op jit(solution)/shard_map/add_pair/pallas_call | solution.py:59
  122.7 7.1 %all-to-all-done.3.umesh_ref = bf16[16,16,512]{2,1,0:T(8,128)(2,1)S(1)} async-done(((bf16[16,16,512]{2,1,0:T(8,128)(2,1)}), bf16[16,16,512]{2,1,0:T(8,128)(2,1)S(1)}, u32[]{:S(2)}, u32[]{:S(2)}) %all-to-all-start.3) | async-done | bytes 262176 | tf_op jit(solution)/shard_map/all_to_all | solution.py:441
  129.8 18.2 %all_to_all.67.pair_ref = bf16[16,32,512]{2,1,0:T(8,128)(2,1)} all-to-all(bf16[16,32,512]{2,1,0:T(8,128)(2,1)} %bitcast.23), channel_id=1, replica_groups=mesh['x'=2,'core'=2,'mesh'=8] {'x','mesh'}, dimensions={0} | all-to-all | bytes 1048576 | tf_op jit(solution)/shard_map/all_to_all | solution.py:458
  148.0 2.1 %spread.1 = bf16[16,48,512]{2,1,0:T(8,128)(2,1)} custom-call(bf16[16,16,512]{2,1,0:T(8,128)(2,1)} %copy-done.3, bf16[16,32,512]{2,1,0:T(8,128)(2,1)} %all_to_all.67.pair_ref), custom_call_target="tpu_custom_call" | custom-call | flops 393216 | bytes 1572864 | tf_op jit(solution)/shard_map/spread/pallas_call | solution.py:59
  150.1 23.5 %all_to_all.68.mine_ref = bf16[16,48,512]{2,1,0:T(8,128)(2,1)S(1)} all-to-all(bf16[16,48,512]{2,1,0:T(8,128)(2,1)} %spread.1), channel_id=1, replica_groups=mesh['x'=2,'core'=2,'mesh'=8] {'x','mesh'}, dimensions={0} | all-to-all | bytes 1572864 | tf_op jit(solution)/shard_map/all_to_all | solution.py:468
  173.7 2.3 %collective-permute-done.2.other_ref = bf16[16,48,512]{2,1,0:T(8,128)(2,1)S(1)} collective-permute-done((bf16[16,48,512]{2,1,0:T(8,128)(2,1)S(1)}, bf16[16,48,512]{2,1,0:T(8,128)(2,1)S(1)}, u32[]{:S(2)}, u32[]{:S(2)}) %collective-permute-start.2) | collective-permute-done | bytes 786464 | tf_op jit(solution)/shard_map/ppermute | solution.py:469
  176.9 3.2 %finish.1 = (f32[512,512]{1,0:T(8,128)}, f32[512,512]{1,0:T(8,128)}, f32[512,512]{1,0:T(8,128)}) custom-call(bf16[16,48,512]{2,1,0:T(8,128)(2,1)} %copy-done.1, bf16[16,48,512]{2,1,0:T(8,128)(2,1)} %copy-done.4), custom_call_target="tpu_custom_call" | custom-call | flops 786432 | bytes 4718592 | tf_op jit(solution)/shard_map/finish/pallas_call | solution.py:59
  (36 shorter events, 11.3 us)
Async XLA Ops:
  0.6 14.3 %copy-start.6 = (bf16[1024,227]{0,1:T(8,128)(2,1)S(1)}, bf16[1024,227]{0,1:T(8,128)(2,1)}, u32[]{:S(2)}) copy-start(bf16[1024,227]{0,1:T(8,128)(2,1)} %param.17) | copy-start | bytes 1394692
  4.5 13.7 %all-to-all-start = ((s32[8,1,128]{2,1,0:T(1,128)}), s32[8,1,128]{2,1,0:T(1,128)S(1)}, u32[]{:S(2)}, u32[]{:S(2)}) async-start(s32[8,1,128]{2,1,0:T(1,128)} %bitcast.32), calls=%async_computation | async-start | bytes 8192 | tf_op jit(solution)/shard_map/all_to_all | solution.py:326
  11.8 18.8 %copy-start.9 = (s32[4096]{0:T(1024)S(1)}, s32[4096]{0:T(1024)}, u32[]{:S(2)}) copy-start(s32[4096]{0:T(1024)} %param.20) | copy-start | bytes 49156
  18.2 0.6 copy-start.10
  21.0 17.9 %all-to-all-start.1 = ((bf16[8,48,512]{2,1,0:T(8,128)(2,1)}), bf16[8,48,512]{2,1,0:T(8,128)(2,1)S(1)}, u32[]{:S(2)}, u32[]{:S(2)}) async-start(bf16[8,48,512]{2,1,0:T(8,128)(2,1)} %bitcast.28), calls=%async_computation.1 | async-start | bytes 786432 | tf_op jit(solution)/shard_map/all_to_all | solution.py:326
  38.9 0.7 copy-start.7
  39.7 19.0 %copy-start.11 = (s32[8,1,128]{2,1,0:T(1,128)S(1)}, s32[8,1,128]{2,1,0:T(1,128)}, u32[]{:S(2)}) copy-start(s32[8,1,128]{2,1,0:T(1,128)} %copy-done.10) | copy-start | bytes 12292
  52.7 25.1 %all-to-all-start.2 = ((bf16[8,48,1024]{2,1,0:T(8,128)(2,1)}), bf16[8,48,1024]{2,1,0:T(8,128)(2,1)S(1)}, u32[]{:S(2)}, u32[]{:S(2)}) async-start(bf16[8,48,1024]{2,1,0:T(8,128)(2,1)} %bitcast.26), calls=%async_computation.2 | async-start | bytes 1572864 | tf_op jit(solution)/shard_map/all_to_all | solution.py:326
  77.8 0.9 copy-start
  82.5 15.6 %all-to-all-start.4 = ((bf16[8,48,512]{2,1,0:T(8,128)(2,1)}), bf16[8,48,512]{2,1,0:T(8,128)(2,1)S(1)}, u32[]{:S(2)}, u32[]{:S(2)}) async-start(bf16[8,48,512]{2,1,0:T(8,128)(2,1)} %bitcast.29), calls=%async_computation.4 | async-start | bytes 786432 | tf_op jit(solution)/shard_map/all_to_all | solution.py:326
  98.0 12.2 %collective-permute-start = (bf16[256,512]{1,0:T(8,128)(2,1)}, bf16[256,512]{1,0:T(8,128)(2,1)S(1)}, u32[]{:S(2)}, u32[]{:S(2)}) collective-permute-start(bf16[256,512]{1,0:T(8,128)(2,1)} %get-tuple-element.45), channel_id=1, source_target_pairs={{0,8},{8,0},{1,9},{9,1},{2,10},{10,2},{3,11},{11,3},{4,12},{12,4},... | collective-permute-start | bytes 786440 | tf_op jit(solution)/shard_map/ppermute | solution.py:288
  98.1 0.7 copy-start.2
  109.7 10.0 %collective-permute-start.1 = (bf16[512,512]{1,0:T(8,128)(2,1)}, bf16[512,512]{1,0:T(8,128)(2,1)S(1)}, u32[]{:S(2)}, u32[]{:S(2)}) collective-permute-start(bf16[512,512]{1,0:T(8,128)(2,1)} %get-tuple-element.51), channel_id=1, source_target_pairs={{0,8},{8,0},{1,9},{9,1},{2,10},{10,2},{3,11},{11,3},{4,12},{12,4},... | collective-permute-start | bytes 1572872 | tf_op jit(solution)/shard_map/ppermute | solution.py:288
  110.2 0.7 copy-start.8
  112.7 17.1 %all-to-all-start.3 = ((bf16[16,16,512]{2,1,0:T(8,128)(2,1)}), bf16[16,16,512]{2,1,0:T(8,128)(2,1)S(1)}, u32[]{:S(2)}, u32[]{:S(2)}) async-start(bf16[16,16,512]{2,1,0:T(8,128)(2,1)} %bitcast.25), calls=%async_computation.3 | async-start | bytes 524288 | tf_op jit(solution)/shard_map/all_to_all | solution.py:441
  119.8 0.8 copy-start.5
  129.8 18.2 %copy-start.3 = (bf16[16,16,512]{2,1,0:T(8,128)(2,1)}, bf16[16,16,512]{2,1,0:T(8,128)(2,1)S(1)}, u32[]{:S(2)}) copy-start(bf16[16,16,512]{2,1,0:T(8,128)(2,1)S(1)} %all-to-all-done.3.umesh_ref) | copy-start | bytes 786436
  173.7 2.3 %copy-start.1 = (bf16[16,48,512]{2,1,0:T(8,128)(2,1)}, bf16[16,48,512]{2,1,0:T(8,128)(2,1)S(1)}, u32[]{:S(2)}) copy-start(bf16[16,48,512]{2,1,0:T(8,128)(2,1)S(1)} %all_to_all.68.mine_ref) | copy-start | bytes 2359300
  173.7 2.3 %collective-permute-start.2 = (bf16[16,48,512]{2,1,0:T(8,128)(2,1)S(1)}, bf16[16,48,512]{2,1,0:T(8,128)(2,1)S(1)}, u32[]{:S(2)}, u32[]{:S(2)}) collective-permute-start(bf16[16,48,512]{2,1,0:T(8,128)(2,1)S(1)} %all_to_all.68.mine_ref), channel_id=1, source_target_pairs={{0,8},{8,0},{1,9},{9,1},{2,10},{10,2},{3,11},{11,3},{4,12},{12,4},... | collective-permute-start | bytes 2359304 | tf_op jit(solution)/shard_map/ppermute | solution.py:469
  176.0 0.9 copy-start.4

commit v3 on v2

v3 whole, which is shorter than its diff:
```python
import functools

import jax
import jax.numpy as jnp
from jax import lax
from jax.experimental import pallas as pl
from jax.experimental.pallas import tpu as pltpu
from jax.sharding import Mesh
from jax.sharding import PartitionSpec as P

CAP = 48
LANES = 128
ROWS = 8
BF16 = jnp.bfloat16
F32 = jnp.float32


def dot(a, b):
    return jnp.dot(a, b, preferred_element_type=F32)


def dot_nt(a, b):
    return lax.dot_general(a, b, (((1,), (1,)), ((), ())), preferred_element_type=F32)


def dot_tn(a, b):
    return lax.dot_general(a, b, (((0,), (0,)), ((), ())), preferred_element_type=F32)


def sigmoid(v):
    return 0.5 + 0.5 * jnp.tanh(0.5 * v)


def as_bf16(mask):
    return jnp.where(mask, 1.0, 0.0).astype(BF16)


def edges_by_ids(ids, count):
    columns = jnp.transpose(ids)
    lanes = lax.broadcasted_iota(jnp.int32, (LANES, count), 1)
    return jnp.concatenate(
        [as_bf16(columns[:, j : j + 1] == lanes) for j in range(ids.shape[0])], axis=0
    )


def ids_by_edges(ids, count):
    places = lax.broadcasted_iota(jnp.int32, (count, LANES), 0)
    return jnp.concatenate(
        [as_bf16(ids[j : j + 1, :] == places) for j in range(ids.shape[0])], axis=1
    )


def call(kernel, name, out, args, flops, grid=None, in_specs=None, out_specs=None, scratch=(), vmem=16, after=()):
    moved = sum(a.size * a.dtype.itemsize for a in args)
    moved += sum(o.size * o.dtype.itemsize for o in out)
    count = len(args)

    def body(*refs):
        kernel(*refs[:count], *refs[count + len(after) :])

    if in_specs is None:
        in_specs = [pl.BlockSpec(memory_space=pltpu.VMEM)] * count
    extra = {} if grid is None else dict(grid=grid)
    if out_specs is not None:
        extra["out_specs"] = out_specs
    return pl.pallas_call(
        body,
        out_shape=out,
        in_specs=list(in_specs) + [pl.BlockSpec(memory_space=pl.ANY)] * len(after),
        scratch_shapes=scratch,
        name=name,
        cost_estimate=pl.CostEstimate(flops=int(flops), bytes_accessed=int(moved), transcendentals=0),
        compiler_params=pltpu.CompilerParams(vmem_limit_bytes=vmem << 20),
        **extra,
    )(*args, *after)


def whole(shape):
    return pl.BlockSpec(shape, lambda i: (0,) * len(shape))


def band_index():
    return lax.axis_index("x") * lax.axis_size("core") + lax.axis_index("core")


def grid_block(ids_ref, count):
    device = band_index() * lax.axis_size("mesh") + lax.axis_index("mesh")
    return ids_ref[...] - device * count


def prep_kernel(owners, mesh_dev, em_ref, slot_ref, ids_ref):
    m = em_ref[...] - band_index() * (owners * mesh_dev)
    rows = m.shape[0]
    lane = lax.broadcasted_iota(jnp.int32, m.shape, 1)
    row = lax.broadcasted_iota(jnp.int32, m.shape, 0)
    turned = pltpu.roll(m, 1, axis=1)
    before = jnp.where(lane == 0, pltpu.roll(turned, 1, axis=0), turned)
    fresh = (m != before) | ((lane == 0) & (row == 0))
    fresh_b = as_bf16(fresh)
    upto = lax.broadcasted_iota(jnp.int32, (LANES, LANES), 0) <= lax.broadcasted_iota(
        jnp.int32, (LANES, LANES), 1
    )
    inside = dot(fresh_b, as_bf16(upto))
    totals = jnp.broadcast_to(inside[:, LANES - 1 :], inside.shape).astype(BF16)
    above = lax.broadcasted_iota(jnp.int32, (rows, rows), 1) < lax.broadcasted_iota(
        jnp.int32, (rows, rows), 0
    )
    rank = (inside + dot(as_bf16(above), totals)).astype(jnp.int32) - 1
    slot = rank
    local = m
    fresh_i = fresh.astype(jnp.int32)
    for o in range(1, owners):
        past = m >= o * mesh_dev
        start = jnp.sum(
            jnp.sum(jnp.where(past, 0, fresh_i), axis=0, keepdims=True), axis=1, keepdims=True
        )
        slot = jnp.where(past, rank + (o * CAP - start), slot)
        local = jnp.where(past, m - o * mesh_dev, local)
    slot_ref[...] = slot
    value = jnp.where(fresh, local + 1, 0)
    found = []
    for o in range(owners):
        places = o * CAP + lax.broadcasted_iota(jnp.int32, (CAP, LANES), 0)
        total = jnp.zeros((CAP, LANES), jnp.int32)
        for r in range(rows):
            total = total + jnp.where(slot[r : r + 1, :] == places, value[r : r + 1, :], 0)
        found.append(total)
    pad = jnp.zeros((LANES - CAP, LANES), jnp.int32)
    for o in range(owners):
        square = jnp.transpose(jnp.concatenate([found[o], pad], axis=0))
        ids_ref[o : o + 1, :] = jnp.sum(square, axis=0, keepdims=True) - 1


def node_pre_kernel(ml_ref, cot_ref, ws_ref, bn_ref, wno_ref, self_ref, cw_ref):
    self_ref[...] = dot(ml_ref[...], ws_ref[...]) + bn_ref[...]
    cw_ref[...] = dot_nt(cot_ref[...], wno_ref[...])


def hidden_kernel(gv_ref, win_ref, bin_ref, out_ref):
    v = dot(gv_ref[...], win_ref[...]) + bin_ref[...]
    out_ref[...] = (v * sigmoid(v)).astype(BF16)


def grid_kernel(ids_ref, hid_ref, wout_ref, gain_ref, ug_ref, lat_t_ref, out_ref, pg):
    @pl.when(pl.program_id(0) == 0)
    def _():
        out = dot(hid_ref[...], wout_ref[...])
        mean = jnp.mean(out, axis=-1, keepdims=True)
        centred = out - mean
        var = jnp.mean(centred * centred, axis=-1, keepdims=True)
        latent = centred * lax.rsqrt(var + 1e-05) * gain_ref[...]
        pg[...] = dot(latent.astype(BF16), ug_ref[...]).astype(BF16)
        lat_t_ref[...] = jnp.transpose(latent).astype(BF16)

    onehot = edges_by_ids(grid_block(ids_ref, pg.shape[0]), pg.shape[0])
    out_ref[...] = dot(onehot, pg[...]).astype(BF16)


def take_latent_kernel(ids_ref, lat_t_ref, out_ref):
    onehot = ids_by_edges(grid_block(ids_ref, lat_t_ref.shape[1]), lat_t_ref.shape[1])
    out_ref[...] = dot(lat_t_ref[...], onehot).astype(BF16)


def ask_kernel(ids_ref, ml_ref, asked_ref, onehot_ref):
    owners = ids_ref.shape[0]
    nodes = ml_ref.shape[0]
    columns = jnp.transpose(ids_ref[...])
    lanes = lax.broadcasted_iota(jnp.int32, (CAP, nodes), 1)
    onehot = jnp.concatenate(
        [as_bf16(columns[:CAP, o : o + 1] == lanes) for o in range(owners)], axis=0
    )
    onehot_ref[...] = onehot
    asked_ref[...] = dot(onehot, ml_ref[...]).astype(BF16)


def pre_of(slot, pm, pg, bias):
    return dot(edges_by_ids(slot, pm.shape[0]), pm) + pg.astype(F32) + bias


def edge_kernel(steps, slot_ref, pg_ref, ml_ref, um_ref, be_ref, we_ref, sums_ref, act_ref, pm_ref, total):
    step = pl.program_id(0)

    @pl.when(step == 0)
    def _():
        total[...] = jnp.zeros_like(total)
        pm_ref[...] = dot(ml_ref[...], um_ref[...]).astype(BF16)

    slot = slot_ref[...]
    pre = pre_of(slot, pm_ref[...], pg_ref[...], be_ref[...])
    act = (pre * sigmoid(pre)).astype(BF16)
    total[...] += dot(ids_by_edges(slot, total.shape[0]), act)

    @pl.when(step == steps - 1)
    def _():
        sums = total[...]
        high = sums.astype(BF16)
        low = (sums - high.astype(F32)).astype(BF16)
        act_ref[...] = high
        sums_ref[...] = (dot(high, we_ref[...]) + dot(low, we_ref[...])).astype(BF16)


def slope_kernel(slot_ref, pg_ref, pm_ref, be_ref, slope_ref, total_ref):
    @pl.when(pl.program_id(0) == 0)
    def _():
        total_ref[...] = jnp.zeros_like(total_ref)

    slot = slot_ref[...]
    pre = pre_of(slot, pm_ref[...], pg_ref[...], be_ref[...])
    s = sigmoid(pre)
    slope = (s * (1.0 + pre * (1.0 - s))).astype(BF16)
    slope_ref[...] = slope
    total_ref[...] += dot(ids_by_edges(slot, total_ref.shape[0]), slope)


def owned(row_ref, rec_ref, nodes):
    places = lax.broadcasted_iota(jnp.int32, (nodes, row_ref.shape[1]), 0)
    return dot(as_bf16(places == row_ref[...]), rec_ref[...]).astype(BF16)


def node_kernel(rec_ref, row_ref, oh_ref, self_ref, cw_ref, wa_ref, gask_ref, gnode_ref, nact_ref):
    agg = owned(row_ref, rec_ref, self_ref.shape[0])
    pre = self_ref[...] + dot(agg, wa_ref[...])
    s = sigmoid(pre)
    g_node = (cw_ref[...] * (s * (1.0 + pre * (1.0 - s)))).astype(BF16)
    g_agg = dot_nt(g_node, wa_ref[...]).astype(BF16)
    gask_ref[...] = dot(oh_ref[...], g_agg).astype(BF16)
    gnode_ref[...] = g_node
    nact_ref[...] = (pre * s).astype(BF16)


def slot_grad_kernel(gc_ref, we_ref, slope_ref, gsum_ref, h_ref):
    h = dot_nt(gc_ref[...], we_ref[...])
    h_ref[...] = h.astype(BF16)
    gsum_ref[...] = (h * slope_ref[...]).astype(BF16)


def node_post_kernel(
    rec_ref, row_ref, gnode_ref, nact_ref, ml_ref, cot_ref, wno_ref, ws_ref, um_ref, mo_ref, gm_ref
):
    g_pmesh = owned(row_ref, rec_ref, ml_ref.shape[0])
    mo_ref[...] = (ml_ref[...].astype(F32) + dot(nact_ref[...], wno_ref[...])).astype(BF16)
    gm_ref[...] = (
        cot_ref[...].astype(F32) + dot_nt(gnode_ref[...], ws_ref[...]) + dot_nt(g_pmesh, um_ref[...])
    ).astype(BF16)


def put_halves(place, value, keep_ref, give_ref):
    core = lax.axis_index("core")
    half = value.shape[0] // 2

    @pl.when(core == 0)
    def _():
        keep_ref[place] = value[:half]
        give_ref[place] = value[half:]

    @pl.when(core != 0)
    def _():
        keep_ref[place] = value[half:]
        give_ref[place] = value[:half]


def edge_back_kernel(
    steps, slot_ref, slope_ref, lat_t_ref, h_ref, gsum_ref, ml_ref, gc_ref, act_ref, keep_ref, give_ref, total
):
    step = pl.program_id(0)

    @pl.when(step == 0)
    def _():
        total[...] = jnp.zeros_like(total)

    onehot = edges_by_ids(slot_ref[...], h_ref.shape[0])
    g_edge = (dot(onehot, h_ref[...]) * slope_ref[...].astype(F32)).astype(BF16)
    total[...] += dot(lat_t_ref[...], g_edge)

    @pl.when(step == steps - 1)
    def _():
        put_halves(0, total[...].astype(BF16), keep_ref, give_ref)
        put_halves(1, dot_tn(act_ref[...], gc_ref[...]).astype(BF16), keep_ref, give_ref)
        put_halves(2, dot_tn(ml_ref[...], gsum_ref[...]).astype(BF16), keep_ref, give_ref)


def parts_kernel(keep_ref, got_ref, out_ref):
    count, _, width = out_ref.shape
    low = keep_ref.shape[1] // count
    for i in range(keep_ref.shape[0]):
        both = (keep_ref[i].astype(F32) + got_ref[i].astype(F32)).astype(BF16)
        out_ref[:, i * low : (i + 1) * low] = both.reshape(count, low, width)


def spread_kernel(scale, parts_ref, out_ref):
    total = (jnp.sum(parts_ref[...].astype(F32), axis=0) * scale).astype(BF16)
    out_ref[...] = jnp.broadcast_to(total[None], out_ref.shape)


def finish_kernel(mine_ref, other_ref, *out_refs):
    count, rows, width = mine_ref.shape
    low = rows // len(out_refs)
    half = count * low
    core = lax.axis_index("core")

    def put(upper_ref, lower_ref):
        for i, out_ref in enumerate(out_refs):
            piece = slice(i * low, (i + 1) * low)
            out_ref[:half] = upper_ref[:, piece].astype(F32).reshape(half, width)
            out_ref[half:] = lower_ref[:, piece].astype(F32).reshape(half, width)

    @pl.when(core == 0)
    def _():
        put(mine_ref, other_ref)

    @pl.when(core != 0)
    def _():
        put(other_ref, mine_ref)


def other_core(value):
    return lax.ppermute(value, "core", [(0, 1), (1, 0)])


def held(value, after):
    def body(*refs):
        pass

    anywhere = pl.BlockSpec(memory_space=pl.ANY)
    return pl.pallas_call(
        body,
        out_shape=jax.ShapeDtypeStruct(value.shape, value.dtype),
        in_specs=[anywhere] * (1 + len(after)),
        out_specs=anywhere,
        input_output_aliases={0: 0},
        name="held",
    )(value, *after)


def shards(
    grid_vars,
    mesh_latent,
    cotangent,
    edge_grid,
    edge_mesh,
    w_in,
    b_in,
    w_out,
    norm_gain,
    u_grid,
    u_mesh,
    b_edge,
    w_edge,
    w_self,
    w_agg,
    b_node,
    w_node_out,
):
    grid_dev, variables = grid_vars.shape
    mesh_dev, width = mesh_latent.shape
    edge_dev = edge_grid.shape[0]
    owners = lax.axis_size("mesh")
    slots = owners * CAP
    rows = edge_dev // LANES
    block = ROWS * LANES
    steps = edge_dev // block
    scale = (edge_dev * lax.axis_size("x") * lax.axis_size("core") * owners) ** (-0.5)
    sds = jax.ShapeDtypeStruct

    def exchange(value):
        return lax.all_to_all(value, "mesh", 0, 0, tiled=True)

    grid_ids = edge_grid.reshape(rows, LANES)
    slot, ids = call(
        functools.partial(prep_kernel, owners, mesh_dev),
        "prep",
        [sds((rows, LANES), jnp.int32), sds((owners, LANES), jnp.int32)],
        [edge_mesh.reshape(rows, LANES)],
        1e9,
    )
    incoming = exchange(ids)

    tile = min(256, grid_dev)
    grid_spec = pl.BlockSpec((tile, width), lambda i: (i, 0))
    (hidden,) = call(
        hidden_kernel,
        "hidden",
        [sds((grid_dev, width), BF16)],
        [grid_vars, w_in, b_in.reshape(1, width)],
        2 * grid_dev * width * variables,
        grid=(grid_dev // tile,),
        in_specs=[
            pl.BlockSpec((tile, variables), lambda i: (i, 0)),
            whole((variables, width)),
            whole((1, width)),
        ],
        out_specs=[grid_spec],
        after=[ids],
    )

    node_f, node_b = sds((mesh_dev, width), F32), sds((mesh_dev, width), BF16)
    self_part, cot_part = call(
        node_pre_kernel,
        "node_pre",
        [node_f, node_f],
        [mesh_latent, cotangent, w_self, b_node.reshape(1, width), w_node_out],
        4 * mesh_dev * width * width,
        vmem=52,
        after=[hidden],
    )
    asked, onehot_in = call(
        ask_kernel,
        "ask",
        [sds((slots, width), BF16), sds((slots, mesh_dev), BF16)],
        [incoming, mesh_latent],
        2 * slots * mesh_dev * width,
        after=[self_part],
    )
    incoming_row = incoming[:, :CAP].reshape(1, slots)
    slot_latent = exchange(asked)

    id_spec = pl.BlockSpec((ROWS, LANES), lambda i: (i, 0))
    edge_spec = pl.BlockSpec((block, width), lambda i: (i, 0))
    edge_t_spec = pl.BlockSpec((width, block), lambda i: (0, i))
    latent_t, edge_pgrid = call(
        grid_kernel,
        "grid",
        [sds((width, grid_dev), BF16), sds((edge_dev, width), BF16)],
        [grid_ids, hidden, w_out, norm_gain.reshape(1, width), u_grid],
        4 * grid_dev * width * width + 2 * edge_dev * grid_dev * width,
        grid=(steps,),
        in_specs=[
            id_spec, whole((grid_dev, width)), whole((width, width)), whole((1, width)),
            whole((width, width)),
        ],
        out_specs=[whole((width, grid_dev)), edge_spec],
        scratch=[pltpu.VMEM((grid_dev, width), BF16)],
        vmem=52,
        after=[asked],
    )

    slots_b, slots_f = sds((slots, width), BF16), sds((slots, width), F32)
    slots_spec = whole((slots, width))
    mesh_spec = whole((mesh_dev, width))
    weight_spec = whole((width, width))
    row_spec = whole((1, slots))
    bias = b_edge.reshape(1, width)
    sums, act_sums, slot_pmesh = call(
        functools.partial(edge_kernel, steps),
        "edge",
        [slots_b, slots_b, slots_b],
        [slot, edge_pgrid, slot_latent, u_mesh, bias, w_edge],
        4 * edge_dev * slots * width + 6 * slots * width * width,
        grid=(steps,),
        in_specs=[id_spec, edge_spec, slots_spec, weight_spec, whole((1, width)), weight_spec],
        out_specs=[slots_spec, slots_spec, slots_spec],
        scratch=[pltpu.VMEM((slots, width), F32)],
        vmem=52,
    )
    received = exchange(sums)

    slope, slope_sums = call(
        slope_kernel,
        "slope",
        [sds((edge_dev, width), BF16), slots_f],
        [slot, edge_pgrid, slot_pmesh, bias],
        4 * edge_dev * slots * width,
        grid=(steps,),
        in_specs=[id_spec, edge_spec, slots_spec, whole((1, width))],
        out_specs=[edge_spec, slots_spec],
        vmem=52,
        after=[sums],
    )
    g_asked, g_node, node_act = call(
        node_kernel,
        "node",
        [slots_b, node_b, node_b],
        [received, incoming_row, onehot_in, self_part, cot_part, w_agg],
        4 * mesh_dev * width * width + 4 * mesh_dev * slots * width,
        vmem=52,
        after=[slope_sums],
    )
    slot_g = exchange(g_asked)

    (edge_latent_t,) = call(
        take_latent_kernel,
        "take_latent",
        [sds((width, edge_dev), BF16)],
        [grid_ids, latent_t],
        2 * edge_dev * grid_dev * width,
        grid=(steps,),
        in_specs=[id_spec, whole((width, grid_dev))],
        out_specs=[edge_t_spec],
        vmem=52,
        after=[g_asked],
    )
    half = width // 2
    gsum, h = call(
        slot_grad_kernel,
        "slot_grad",
        [slots_b, slots_b],
        [slot_g, w_edge, slope_sums],
        2 * slots * width * width,
        vmem=52,
        after=[edge_latent_t],
    )
    gsum_received = exchange(gsum)

    three = sds((3, half, width), BF16)
    keep, give = call(
        functools.partial(edge_back_kernel, steps),
        "edge_back",
        [three, three],
        [slot, slope, edge_latent_t, h, gsum, slot_latent, slot_g, act_sums],
        2 * edge_dev * (slots + width) * width + 4 * slots * width * width,
        grid=(steps,),
        in_specs=[id_spec, edge_spec, edge_t_spec] + [slots_spec] * 5,
        out_specs=[whole(three.shape), whole(three.shape)],
        scratch=[pltpu.VMEM((width, width), F32)],
        vmem=52,
    )
    others = ("x", "mesh")
    count = lax.axis_size("x") * owners
    pieces = sds((count, 3 * half // count, width), BF16)
    (parts,) = call(
        parts_kernel,
        "parts",
        [pieces],
        [keep, other_core(held(give, [gsum_received]))],
        3 * half * width,
    )
    summed = lax.all_to_all(parts, others, 0, 0, tiled=True)

    mesh_out, grad_mesh = call(
        node_post_kernel,
        "node_post",
        [node_b, node_b],
        [
            gsum_received, incoming_row, g_node, node_act, mesh_latent, cotangent,
            w_node_out, w_self, u_mesh,
        ],
        6 * mesh_dev * width * width + 2 * mesh_dev * slots * width,
        vmem=52,
        after=[parts],
    )
    (copies,) = call(
        functools.partial(spread_kernel, scale),
        "spread",
        [pieces],
        [summed],
        3 * half * width,
        after=[mesh_out],
    )
    mine = lax.all_to_all(copies, others, 0, 0, tiled=True)
    weight = sds((width, width), F32)
    grad_ugrid, grad_edge, grad_umesh = call(
        finish_kernel, "finish", [weight] * 3, [mine, other_core(mine)], 3 * width * width
    )
    return mesh_out, grad_mesh, grad_edge, grad_ugrid, grad_umesh


def solution(mesh):
    bands, owners = mesh.shape["band"], mesh.shape["mesh"]
    cores = 2
    fine = Mesh(mesh.devices.reshape(bands // cores, cores, owners), ("x", "core", "mesh"))
    split = ("x", "core", "mesh")
    return jax.shard_map(
        shards,
        mesh=fine,
        in_specs=(P(split, None),) * 3 + (P(split),) * 2 + (P(),) * 12,
        out_specs=(P(split, None), P(split, None), P(), P(), P()),
        check_vma=False,
    )
```

time: 181 us -> 163 us (0.901)
  blocking collectives: 41.7 us -> 24.6 us
  Pallas kernels: 70.4 us -> 61.2 us
  local copies, waits for them, and re-layouts: 6.99 us -> 13.7 us
  starting transfers between devices: 28.1 us -> 33.4 us
  waiting for transfers between devices: 30.1 us -> 27.8 us
  other arithmetic: 1.99 us -> 0 us
    all_to_all x1 -> x0, blocking collectives: 18.2 us -> none  [shards(): lax.all_to_all(pair_sum(keep, give, 'add_pair'), others, 0, 0, tiled=True)]
    all_to_all x4 -> x5, waiting for transfers between devices: 20.7 us -> 5.33 us  [exchange(): return lax.all_to_all(value, 'mesh', 0, 0, tiled=True)]
    all_to_all x1, waiting for transfers between devices: 7.12 us -> 17.7 us  [shards(): summed = lax.all_to_all(parts, others, 0, 0, tiled=True)]
    pallas_call x14 -> x16, Pallas kernels: 70.4 us -> 61.2 us  [the longest x15 61.2 us: call(): pl.pallas_call(body, out_shape=out, in_specs=list(in_specs) + [pl.BlockSp...]
    unnamed x25 -> x53, local copies, waits for them, and re-layouts: 6.37 us -> 13.7 us
    all_to_all x4 -> x5, starting transfers between devices: 20.6 us -> 26.4 us  [exchange(): return lax.all_to_all(value, 'mesh', 0, 0, tiled=True)]
    ppermute x3 -> x2, waiting for transfers between devices: 2.29 us -> 4.78 us  [other_core(): return lax.ppermute(value, 'core', [(0, 1), (1, 0)])]
    reshape x2 -> x0, other arithmetic: 1.99 us -> none  [the longest x1 1.38 us: shards(): mesh_local = (edge_mesh - band * (owners * mesh_dev)).reshape(rows, LANES)]
  transfers between devices with their start and end apart: 8 -> 8, of which waited for: 4 -> 7; matrix products, arithmetic and copies ran while one was open for 1% -> 1% of each run, Pallas kernels for 24% -> 25%
where the time goes in v3:
time: 163 us; the launch traced here: 162 us
  Pallas kernels  61.2 us (38%)
  starting transfers between devices  33.4 us (20%)
  waiting for transfers between devices  27.8 us (17%)
  blocking collectives  24.6 us (15%)
  local copies, waits for them, and re-layouts  13.7 us (8%)
    pallas_call x15, Pallas kernels, call(): pl.pallas_call(body, out_shape=out, in_specs=list(in_specs) + [pl.BlockSp...  61.2 us
    all_to_all x5, starting transfers between devices, exchange(): return lax.all_to_all(value, 'mesh', 0, 0, tiled=True)  26.4 us
    all_to_all x1, blocking collectives, shards(): mine = lax.all_to_all(copies, others, 0, 0, tiled=True)  24.6 us
    all_to_all x1, waiting for transfers between devices, shards(): summed = lax.all_to_all(parts, others, 0, 0, tiled=True)  17.7 us
    unnamed x53, local copies, waits for them, and re-layouts  13.7 us
    all_to_all x1, starting transfers between devices, shards(): summed = lax.all_to_all(parts, others, 0, 0, tiled=True)  6.99 us
    all_to_all x5, waiting for transfers between devices, exchange(): return lax.all_to_all(value, 'mesh', 0, 0, tiled=True)  5.33 us
    ppermute x2, waiting for transfers between devices, other_core(): return lax.ppermute(value, 'core', [(0, 1), (1, 0)])  4.78 us
  transfers between devices with their start and end apart: 8, of which 7 were waited for; matrix products, arithmetic and copies ran while one was open for 1% of the time, Pallas kernels for 25%

profile of v3, /device:TPU:0, one launch (start us, length us, event | category | flops | bytes accessed | tf_op | source)
XLA Modules:
  0.0 161.6 jit_solution(5712517682648829740)
XLA Ops:
  1.6 1.8 %prep.1 = (s32[32,128]{1,0:T(8,128)S(1)}, s32[8,128]{1,0:T(8,128)}) custom-call(s32[32,128]{1,0:T(8,128)S(1)} %bitcast.30), custom_call_target="tpu_custom_call" | custom-call | flops 1000000000 | bytes 36864 | tf_op jit(solution)/shard_map/prep/pallas_call | solution.py:66
  3.3 7.4 %all-to-all-start = ((s32[8,1,128]{2,1,0:T(1,128)}), s32[8,1,128]{2,1,0:T(1,128)S(1)}, u32[]{:S(2)}, u32[]{:S(2)}) async-start(s32[8,1,128]{2,1,0:T(1,128)} %bitcast.5), calls=%async_computation | async-start | bytes 8192 | tf_op jit(solution)/shard_map/all_to_all | solution.py:366
  10.8 1.2 copy.24.refs_0_
  14.2 1.4 node_pre.1
  15.6 1.6 all-to-all-done
  19.5 4.5 %all-to-all-start.1 = ((bf16[8,48,512]{2,1,0:T(8,128)(2,1)}), bf16[8,48,512]{2,1,0:T(8,128)(2,1)S(1)}, u32[]{:S(2)}, u32[]{:S(2)}) async-start(bf16[8,48,512]{2,1,0:T(8,128)(2,1)} %bitcast.8), calls=%async_computation.1 | async-start | bytes 786432 | tf_op jit(solution)/shard_map/all_to_all | solution.py:366
  25.0 9.3 %grid.1 = (bf16[512,1024]{1,0:T(8,128)(2,1)}, bf16[4096,512]{1,0:T(8,128)(2,1)}) custom-call(s32[32,128]{1,0:T(8,128)S(1)} %bitcast.31, bf16[1024,512]{1,0:T(8,128)(2,1)} %copy-done, bf16[512,512]{1,0:T(8,128)(2,1)S(1)} %copy-done.15, f32[1,512]{1,0:T(1,128)S(1)} %bitcast.33, bf16[512,512]{1,0:T(8,128)(2,1)S(1)} %copy-done.16, ...), custom_call_target="tpu_custom_call" | custom-call | flops 5368709120 | bytes 7358464 | tf_op jit(solution)/shard_map/grid/pallas_call | solution.py:66
  35.0 9.6 %edge.1 = (bf16[384,512]{1,0:T(8,128)(2,1)}, bf16[384,512]{1,0:T(8,128)(2,1)S(1)}, bf16[384,512]{1,0:T(8,128)(2,1)S(1)}) custom-call(s32[32,128]{1,0:T(8,128)S(1)} %get-tuple-element.30.refs_0_, bf16[4096,512]{1,0:T(8,128)(2,1)} %get-tuple-element.34.refs_1_, bf16[384,512]{1,0:T(8,128)(2,1)S(1)} %bitcast.24, bf16[512,512]{1,0:T(8,128)(2,1)} %refs_8_.1, ...), custom_call_target="tpu_custom_call" | custom-call | flops 3825205248 | bytes 6834176 | tf_op jit(solution)/shard_map/edge/pallas_call | solution.py:66
  45.4 5.3 %all-to-all-start.2 = ((bf16[8,48,512]{2,1,0:T(8,128)(2,1)}), bf16[8,48,512]{2,1,0:T(8,128)(2,1)S(1)}, u32[]{:S(2)}, u32[]{:S(2)}) async-start(bf16[8,48,512]{2,1,0:T(8,128)(2,1)} %bitcast.11), calls=%async_computation.2 | async-start | bytes 786432 | tf_op jit(solution)/shard_map/all_to_all | solution.py:366
  50.7 9.2 %slope.1 = (bf16[4096,512]{1,0:T(8,128)(2,1)}, f32[384,512]{1,0:T(8,128)S(1)}) custom-call(s32[32,128]{1,0:T(8,128)S(1)} %get-tuple-element.30.refs_0_, bf16[4096,512]{1,0:T(8,128)(2,1)} %get-tuple-element.34.refs_1_, bf16[384,512]{1,0:T(8,128)(2,1)S(1)} %get-tuple-element.38.refs_2_, f32[1,512]{1,0:T(1,128)S(1)} %bitcast.35, ...), custom_call_target="tpu_custom_call" | custom-call | flops 3221225472 | bytes 9586688 | tf_op jit(solution)/shard_map/slope/pallas_call | solution.py:66
  61.2 3.5 %node.1 = (bf16[384,512]{1,0:T(8,128)(2,1)}, bf16[320,512]{1,0:T(8,128)(2,1)S(1)}, bf16[320,512]{1,0:T(8,128)(2,1)S(1)}) custom-call(bf16[384,512]{1,0:T(8,128)(2,1)S(1)} %bitcast.23, s32[1,384]{1,0:T(1,128)S(1)} %reshape.47.refs_1_, bf16[384,320]{1,0:T(8,128)(2,1)S(1)} %get-tuple-element.36.refs_2_, f32[320,512]{1,0:T(8,128)} %get-tuple-element.32.refs_2_.refs_3_, ...), custom_call_target="tpu_custom_call" | custom-call | flops 587202560 | bytes 3524096 | tf_op jit(solution)/shard_map/node/pallas_call | solution.py:66
  64.7 5.5 %all-to-all-start.3 = ((bf16[8,48,512]{2,1,0:T(8,128)(2,1)}), bf16[8,48,512]{2,1,0:T(8,128)(2,1)S(1)}, u32[]{:S(2)}, u32[]{:S(2)}) async-start(bf16[8,48,512]{2,1,0:T(8,128)(2,1)} %bitcast.13), calls=%async_computation.3 | async-start | bytes 786432 | tf_op jit(solution)/shard_map/all_to_all | solution.py:366
  71.5 6.2 %take_latent.1.refs_3_.refs_2_ = bf16[512,4096]{1,0:T(8,128)(2,1)} custom-call(s32[32,128]{1,0:T(8,128)S(1)} %bitcast.32, bf16[512,1024]{1,0:T(8,128)(2,1)S(1)} %copy-done.25, bf16[384,512]{1,0:T(8,128)(2,1)} %get-tuple-element.40.refs_2_), custom_call_target="tpu_custom_call" | custom-call | flops 4294967296 | bytes 5259264 | tf_op jit(solution)/shard_map/take_latent/pallas_call | solution.py:66
  77.6 2.6 %all-to-all-done.3 = bf16[8,48,512]{2,1,0:T(8,128)(2,1)S(1)} async-done(((bf16[8,48,512]{2,1,0:T(8,128)(2,1)}), bf16[8,48,512]{2,1,0:T(8,128)(2,1)S(1)}, u32[]{:S(2)}, u32[]{:S(2)}) %all-to-all-start.3) | async-done | bytes 393248 | tf_op jit(solution)/shard_map/all_to_all | solution.py:366
  80.2 2.3 %slot_grad.1 = (bf16[384,512]{1,0:T(8,128)(2,1)}, bf16[384,512]{1,0:T(8,128)(2,1)S(1)}) custom-call(bf16[384,512]{1,0:T(8,128)(2,1)S(1)} %bitcast.21, bf16[512,512]{1,0:T(8,128)(2,1)S(1)} %copy-done.10, f32[384,512]{1,0:T(8,128)} %copy-done.3, bf16[512,4096]{1,0:T(8,128)(2,1)} %take_latent.1.refs_3_.refs_2_), custom_call_target="tpu_custom_call" | custom-call | flops 201326592 | bytes 2490368 | tf_op jit(solution)/shard_map/slot_grad/pallas_call | solution.py:66
  83.3 3.7 %all-to-all-start.4 = ((bf16[8,48,512]{2,1,0:T(8,128)(2,1)}), bf16[8,48,512]{2,1,0:T(8,128)(2,1)S(1)}, u32[]{:S(2)}, u32[]{:S(2)}) async-start(bf16[8,48,512]{2,1,0:T(8,128)(2,1)} %bitcast.15), calls=%async_computation.4 | async-start | bytes 786432 | tf_op jit(solution)/shard_map/all_to_all | solution.py:366
  88.9 9.7 %edge_back.1 = (bf16[3,256,512]{2,1,0:T(8,128)(2,1)}, bf16[3,256,512]{2,1,0:T(8,128)(2,1)}) custom-call(s32[32,128]{1,0:T(8,128)S(1)} %get-tuple-element.30.refs_0_, bf16[4096,512]{1,0:T(8,128)(2,1)} %get-tuple-element.45.refs_1_, bf16[512,4096]{1,0:T(8,128)(2,1)} %take_latent.1.refs_3_.refs_2_, bf16[384,512]{1,0:T(8,128)(2,1)S(1)} %copy-done.18, ...), custom_call_target="tpu_custom_call" | custom-call | flops 4160749568 | bytes 11943936 | tf_op jit(solution)/shard_map/edge_back/pallas_call | solution.py:66
  99.4 2.5 %collective-permute-done.refs_1_ = bf16[3,256,512]{2,1,0:T(8,128)(2,1)S(1)} collective-permute-done((bf16[3,256,512]{2,1,0:T(8,128)(2,1)}, bf16[3,256,512]{2,1,0:T(8,128)(2,1)S(1)}, u32[]{:S(2)}, u32[]{:S(2)}) %collective-permute-start) | collective-permute-done | bytes 786464 | tf_op jit(solution)/shard_map/ppermute | solution.py:317
  104.1 7.0 %all-to-all-start.5 = ((bf16[16,48,512]{2,1,0:T(8,128)(2,1)}), bf16[16,48,512]{2,1,0:T(8,128)(2,1)S(1)}, u32[]{:S(2)}, u32[]{:S(2)}) async-start(bf16[16,48,512]{2,1,0:T(8,128)(2,1)} %parts.1.refs_9_), calls=%async_computation.5 | async-start | bytes 1572864 | tf_op jit(solution)/shard_map/all_to_all | solution.py:527
  111.1 2.9 %node_post.1 = (bf16[320,512]{1,0:T(8,128)(2,1)}, bf16[320,512]{1,0:T(8,128)(2,1)}) custom-call(bf16[384,512]{1,0:T(8,128)(2,1)S(1)} %bitcast.20, s32[1,384]{1,0:T(1,128)S(1)} %reshape.47.refs_1_, bf16[320,512]{1,0:T(8,128)(2,1)S(1)} %get-tuple-element.43.refs_2_, bf16[320,512]{1,0:T(8,128)(2,1)S(1)} %get-tuple-element.44.refs_3_, ...), custom_call_target="tpu_custom_call" | custom-call | flops 629145600 | bytes 3933696 | tf_op jit(solution)/shard_map/node_post/pallas_call | solution.py:66
  114.0 17.7 %all-to-all-done.5.refs_0_ = bf16[16,48,512]{2,1,0:T(8,128)(2,1)S(1)} async-done(((bf16[16,48,512]{2,1,0:T(8,128)(2,1)}), bf16[16,48,512]{2,1,0:T(8,128)(2,1)S(1)}, u32[]{:S(2)}, u32[]{:S(2)}) %all-to-all-start.5) | async-done | bytes 786464 | tf_op jit(solution)/shard_map/all_to_all | solution.py:527
  132.8 24.6 %all_to_all.65.refs_0_ = bf16[16,48,512]{2,1,0:T(8,128)(2,1)S(1)} all-to-all(bf16[16,48,512]{2,1,0:T(8,128)(2,1)S(1)} %spread.1), channel_id=1, replica_groups=mesh['x'=2,'core'=2,'mesh'=8] {'x','mesh'}, dimensions={0} | all-to-all | bytes 1572864 | tf_op jit(solution)/shard_map/all_to_all | solution.py:549
  157.5 2.3 %collective-permute-done.1.refs_1_ = bf16[16,48,512]{2,1,0:T(8,128)(2,1)S(1)} collective-permute-done((bf16[16,48,512]{2,1,0:T(8,128)(2,1)S(1)}, bf16[16,48,512]{2,1,0:T(8,128)(2,1)S(1)}, u32[]{:S(2)}, u32[]{:S(2)}) %collective-permute-start.1) | collective-permute-done | bytes 786464 | tf_op jit(solution)/shard_map/ppermute | solution.py:317
  159.8 1.9 %finish.1 = (f32[512,512]{1,0:T(8,128)}, f32[512,512]{1,0:T(8,128)}, f32[512,512]{1,0:T(8,128)}) custom-call(bf16[16,48,512]{2,1,0:T(8,128)(2,1)S(1)} %all_to_all.65.refs_0_, bf16[16,48,512]{2,1,0:T(8,128)(2,1)S(1)} %collective-permute-done.1.refs_1_), custom_call_target="tpu_custom_call" | custom-call | flops 786432 | bytes 4718592 | tf_op jit(solution)/shard_map/finish/pallas_call | solution.py:66
  (63 shorter events, 17.3 us)
Async XLA Ops:
  0.6 11.4 %copy-start.14 = (f32[512]{0:T(512)S(1)}, f32[512]{0:T(512)}, u32[]{:S(2)}) copy-start(f32[512]{0:T(512)} %param.23) | copy-start | bytes 6148
  0.6 11.4 %copy-start.12 = (bf16[227,512]{1,0:T(8,128)(2,1)S(1)}, bf16[227,512]{1,0:T(8,128)(2,1)}, u32[]{:S(2)}) copy-start(bf16[227,512]{1,0:T(8,128)(2,1)} %refs_1_.4) | copy-start | bytes 697348
  0.7 13.5 %copy-start.13 = (f32[512]{0:T(512)S(1)}, f32[512]{0:T(512)}, u32[]{:S(2)}) copy-start(f32[512]{0:T(512)} %param.32) | copy-start | bytes 6148
  0.7 13.5 %copy-start.4 = (bf16[320,512]{1,0:T(8,128)(2,1)S(1)}, bf16[320,512]{1,0:T(8,128)(2,1)}, u32[]{:S(2)}) copy-start(bf16[320,512]{1,0:T(8,128)(2,1)} %refs_4_.5) | copy-start | bytes 983044
  0.7 13.5 %copy-start.8 = (bf16[320,512]{1,0:T(8,128)(2,1)S(1)}, bf16[320,512]{1,0:T(8,128)(2,1)}, u32[]{:S(2)}) copy-start(bf16[320,512]{1,0:T(8,128)(2,1)} %refs_5_.5) | copy-start | bytes 983044
  0.7 13.5 %copy-start.6 = (bf16[512,512]{1,0:T(8,128)(2,1)S(1)}, bf16[512,512]{1,0:T(8,128)(2,1)}, u32[]{:S(2)}) copy-start(bf16[512,512]{1,0:T(8,128)(2,1)} %refs_7_.1) | copy-start | bytes 1572868
  0.7 13.5 %copy-start.7 = (bf16[512,512]{1,0:T(8,128)(2,1)S(1)}, bf16[512,512]{1,0:T(8,128)(2,1)}, u32[]{:S(2)}) copy-start(bf16[512,512]{1,0:T(8,128)(2,1)} %refs_6_.1) | copy-start | bytes 1572868
  3.3 20.6 %copy-start.15 = (bf16[512,512]{1,0:T(8,128)(2,1)S(1)}, bf16[512,512]{1,0:T(8,128)(2,1)}, u32[]{:S(2)}) copy-start(bf16[512,512]{1,0:T(8,128)(2,1)} %refs_2_.3) | copy-start | bytes 1572868
  3.3 20.6 %copy-start.20 = (s32[4096]{0:T(1024)S(1)}, s32[4096]{0:T(1024)}, u32[]{:S(2)}) copy-start(s32[4096]{0:T(1024)} %param.20) | copy-start | bytes 49156
  3.3 20.6 %copy-start.21 = (f32[512]{0:T(512)S(1)}, f32[512]{0:T(512)}, u32[]{:S(2)}) copy-start(f32[512]{0:T(512)} %param.25) | copy-start | bytes 6148
  3.3 13.8 %all-to-all-start = ((s32[8,1,128]{2,1,0:T(1,128)}), s32[8,1,128]{2,1,0:T(1,128)S(1)}, u32[]{:S(2)}, u32[]{:S(2)}) async-start(s32[8,1,128]{2,1,0:T(1,128)} %bitcast.5), calls=%async_computation | async-start | bytes 8192 | tf_op jit(solution)/shard_map/all_to_all | solution.py:366
  17.1 1.1 copy-start.5
  19.5 15.6 %all-to-all-start.1 = ((bf16[8,48,512]{2,1,0:T(8,128)(2,1)}), bf16[8,48,512]{2,1,0:T(8,128)(2,1)S(1)}, u32[]{:S(2)}, u32[]{:S(2)}) async-start(bf16[8,48,512]{2,1,0:T(8,128)(2,1)} %bitcast.8), calls=%async_computation.1 | async-start | bytes 786432 | tf_op jit(solution)/shard_map/all_to_all | solution.py:366
  25.0 10.0 %copy-start.22 = (f32[512]{0:T(512)S(1)}, f32[512]{0:T(512)}, u32[]{:S(2)}) copy-start(f32[512]{0:T(512)} %param.28) | copy-start | bytes 6148
  45.4 15.8 %all-to-all-start.2 = ((bf16[8,48,512]{2,1,0:T(8,128)(2,1)}), bf16[8,48,512]{2,1,0:T(8,128)(2,1)S(1)}, u32[]{:S(2)}, u32[]{:S(2)}) async-start(bf16[8,48,512]{2,1,0:T(8,128)(2,1)} %bitcast.11), calls=%async_computation.2 | async-start | bytes 786432 | tf_op jit(solution)/shard_map/all_to_all | solution.py:366
  64.7 15.6 %all-to-all-start.3 = ((bf16[8,48,512]{2,1,0:T(8,128)(2,1)}), bf16[8,48,512]{2,1,0:T(8,128)(2,1)S(1)}, u32[]{:S(2)}, u32[]{:S(2)}) async-start(bf16[8,48,512]{2,1,0:T(8,128)(2,1)} %bitcast.13), calls=%async_computation.3 | async-start | bytes 786432 | tf_op jit(solution)/shard_map/all_to_all | solution.py:366
  70.2 1.2 copy-start.25
  71.5 8.8 %copy-start.10 = (bf16[512,512]{1,0:T(8,128)(2,1)S(1)}, bf16[512,512]{1,0:T(8,128)(2,1)}, u32[]{:S(2)}) copy-start(bf16[512,512]{1,0:T(8,128)(2,1)} %refs_1_.7) | copy-start | bytes 1572868
  83.3 15.3 %all-to-all-start.4 = ((bf16[8,48,512]{2,1,0:T(8,128)(2,1)}), bf16[8,48,512]{2,1,0:T(8,128)(2,1)S(1)}, u32[]{:S(2)}, u32[]{:S(2)}) async-start(bf16[8,48,512]{2,1,0:T(8,128)(2,1)} %bitcast.15), calls=%async_computation.4 | async-start | bytes 786432 | tf_op jit(solution)/shard_map/all_to_all | solution.py:366
  99.4 11.7 %copy-start.2 = (bf16[8,48,512]{2,1,0:T(8,128)(2,1)S(1)}, bf16[8,48,512]{2,1,0:T(8,128)(2,1)}, u32[]{:S(2)}) copy-start(bf16[8,48,512]{2,1,0:T(8,128)(2,1)} %copy-done.1) | copy-start | bytes 1179652
  99.4 2.5 %collective-permute-start = (bf16[3,256,512]{2,1,0:T(8,128)(2,1)}, bf16[3,256,512]{2,1,0:T(8,128)(2,1)S(1)}, u32[]{:S(2)}, u32[]{:S(2)}) collective-permute-start(bf16[3,256,512]{2,1,0:T(8,128)(2,1)} %held.1), channel_id=1, source_target_pairs={{0,8},{8,0},{1,9},{9,1},{2,10},{10,2},{3,11},{11,3},{4,12},{12,4},... | collective-permute-start | bytes 2359304 | tf_op jit(solution)/shard_map/ppermute | solution.py:317
  101.9 1.1 copy-start.9
  104.1 27.7 %all-to-all-start.5 = ((bf16[16,48,512]{2,1,0:T(8,128)(2,1)}), bf16[16,48,512]{2,1,0:T(8,128)(2,1)S(1)}, u32[]{:S(2)}, u32[]{:S(2)}) async-start(bf16[16,48,512]{2,1,0:T(8,128)(2,1)} %parts.1.refs_9_), calls=%async_computation.5 | async-start | bytes 1572864 | tf_op jit(solution)/shard_map/all_to_all | solution.py:527
  157.5 2.3 %collective-permute-start.1 = (bf16[16,48,512]{2,1,0:T(8,128)(2,1)S(1)}, bf16[16,48,512]{2,1,0:T(8,128)(2,1)S(1)}, u32[]{:S(2)}, u32[]{:S(2)}) collective-permute-start(bf16[16,48,512]{2,1,0:T(8,128)(2,1)S(1)} %all_to_all.65.refs_0_), channel_id=1, source_target_pairs={{0,8},{8,0},{1,9},{9,1},{2,10},{10,2},{3,11},{11,3},{4,12},{12,4},... | collective-permute-start | bytes 2359304 | tf_op jit(solution)/shard_map/ppermute | solution.py:317
  (10 other events, 9.0 us)

commit v4 on v3

--- a/solution.py
+++ b/solution.py
@@ -1,4 +1,5 @@
 import functools
+import math
 
 import jax
 import jax.numpy as jnp
@@ -23,23 +24,19 @@
     return lax.dot_general(a, b, (((1,), (1,)), ((), ())), preferred_element_type=F32)
 
 
-def dot_tn(a, b):
-    return lax.dot_general(a, b, (((0,), (0,)), ((), ())), preferred_element_type=F32)
-
-
 def sigmoid(v):
     return 0.5 + 0.5 * jnp.tanh(0.5 * v)
 
 
-def as_bf16(mask):
-    return jnp.where(mask, 1.0, 0.0).astype(BF16)
-
-
-def edges_by_ids(ids, count):
+def as_bf16(mask, one=1.0):
+    return jnp.where(mask, one, 0.0).astype(BF16)
+
+
+def edges_by_ids(ids, count, one=1.0):
     columns = jnp.transpose(ids)
     lanes = lax.broadcasted_iota(jnp.int32, (LANES, count), 1)
     return jnp.concatenate(
-        [as_bf16(columns[:, j : j + 1] == lanes) for j in range(ids.shape[0])], axis=0
+        [as_bf16(columns[:, j : j + 1] == lanes, one) for j in range(ids.shape[0])], axis=0
     )
 
 
@@ -50,23 +47,28 @@
     )
 
 
-def call(kernel, name, out, args, flops, grid=None, in_specs=None, out_specs=None, scratch=(), vmem=16, after=()):
-    moved = sum(a.size * a.dtype.itemsize for a in args)
-    moved += sum(o.size * o.dtype.itemsize for o in out)
-    count = len(args)
+def call(kernel, name, out, args, flops, grid=None, in_specs=None, out_specs=None, scratch=(), vmem=16, after=(), token=False):
+    moved = sum(math.prod(a.shape) * a.dtype.itemsize for a in [*args, *out])
+    count, last = len(args), len(args) + len(after) + len(out)
 
     def body(*refs):
-        kernel(*refs[:count], *refs[count + len(after) :])
-
+        kernel(*refs[:count], *refs[count + len(after) : last], *refs[last + token :])
+        if token:
+            refs[last][...] = jnp.zeros_like(refs[last])
+
+    if out_specs is None:
+        out_specs = [pl.BlockSpec(memory_space=pltpu.VMEM)] * len(out)
+    if token:
+        out = [*out, jax.ShapeDtypeStruct((8, LANES), jnp.int32)]
+        out_specs = [*out_specs, pl.BlockSpec((8, LANES), lambda *_: (0, 0))]
     if in_specs is None:
         in_specs = [pl.BlockSpec(memory_space=pltpu.VMEM)] * count
     extra = {} if grid is None else dict(grid=grid)
-    if out_specs is not None:
-        extra["out_specs"] = out_specs
     return pl.pallas_call(
         body,
         out_shape=out,
         in_specs=list(in_specs) + [pl.BlockSpec(memory_space=pl.ANY)] * len(after),
+        out_specs=out_specs,
         scratch_shapes=scratch,
         name=name,
         cost_estimate=pl.CostEstimate(flops=int(flops), bytes_accessed=int(moved), transcendentals=0),
@@ -152,11 +154,16 @@
         pg[...] = dot(latent.astype(BF16), ug_ref[...]).astype(BF16)
         lat_t_ref[...] = jnp.transpose(latent).astype(BF16)
 
-    onehot = edges_by_ids(grid_block(ids_ref, pg.shape[0]), pg.shape[0])
+    onehot = edges_by_ids(grid_block(ids_ref, pg.shape[0]), pg.shape[0], 0.5)
     out_ref[...] = dot(onehot, pg[...]).astype(BF16)
 
 
-def take_latent_kernel(ids_ref, lat_t_ref, out_ref):
+def take_latent_kernel(ids_ref, lat_t_ref, act_ref, ml_ref, out_ref, act_t_ref, ml_t_ref):
+    @pl.when(pl.program_id(0) == 0)
+    def _():
+        act_t_ref[...] = jnp.transpose(act_ref[...])
+        ml_t_ref[...] = jnp.transpose(ml_ref[...])
+
     onehot = ids_by_edges(grid_block(ids_ref, lat_t_ref.shape[1]), lat_t_ref.shape[1])
     out_ref[...] = dot(lat_t_ref[...], onehot).astype(BF16)
 
@@ -173,8 +180,8 @@
     asked_ref[...] = dot(onehot, ml_ref[...]).astype(BF16)
 
 
-def pre_of(slot, pm, pg, bias):
-    return dot(edges_by_ids(slot, pm.shape[0]), pm) + pg.astype(F32) + bias
+def half_pre(slot, pm, half_pg, bias):
+    return dot(edges_by_ids(slot, pm.shape[0], 0.5), pm) + half_pg.astype(F32) + 0.5 * bias
 
 
 def edge_kernel(steps, slot_ref, pg_ref, ml_ref, um_ref, be_ref, we_ref, sums_ref, act_ref, pm_ref, total):
@@ -186,8 +193,8 @@
         pm_ref[...] = dot(ml_ref[...], um_ref[...]).astype(BF16)
 
     slot = slot_ref[...]
-    pre = pre_of(slot, pm_ref[...], pg_ref[...], be_ref[...])
-    act = (pre * sigmoid(pre)).astype(BF16)
+    v = half_pre(slot, pm_ref[...], pg_ref[...], be_ref[...])
+    act = (v + v * jnp.tanh(v)).astype(BF16)
     total[...] += dot(ids_by_edges(slot, total.shape[0]), act)
 
     @pl.when(step == steps - 1)
@@ -205,9 +212,9 @@
         total_ref[...] = jnp.zeros_like(total_ref)
 
     slot = slot_ref[...]
-    pre = pre_of(slot, pm_ref[...], pg_ref[...], be_ref[...])
-    s = sigmoid(pre)
-    slope = (s * (1.0 + pre * (1.0 - s))).astype(BF16)
+    v = half_pre(slot, pm_ref[...], pg_ref[...], be_ref[...])
+    t = jnp.tanh(v)
+    slope = ((1.0 + t) * (1.0 + v * (1.0 - t))).astype(BF16)
     slope_ref[...] = slope
     total_ref[...] += dot(ids_by_edges(slot, total_ref.shape[0]), slope)
 
@@ -217,19 +224,36 @@
     return dot(as_bf16(places == row_ref[...]), rec_ref[...]).astype(BF16)
 
 
-def node_kernel(rec_ref, row_ref, oh_ref, self_ref, cw_ref, wa_ref, gask_ref, gnode_ref, nact_ref):
+def load(pairs, sems):
+    copies = [pltpu.make_async_copy(a, b, sems.at[i]) for i, (a, b) in enumerate(pairs)]
+    for copy in copies:
+        copy.start()
+    return copies
+
+
+def node_kernel(
+    rec_ref, row_ref, oh_hbm, self_hbm, cw_hbm, wa_hbm, gask_ref, gnode_ref, nact_ref,
+    oh_ref, self_ref, cw_ref, wa_ref, sems,
+):
+    pairs = [(wa_hbm, wa_ref), (self_hbm, self_ref), (cw_hbm, cw_ref), (oh_hbm, oh_ref)]
+    wa, own, cw, oh = load(pairs, sems)
     agg = owned(row_ref, rec_ref, self_ref.shape[0])
-    pre = self_ref[...] + dot(agg, wa_ref[...])
+    wa.wait()
+    pre = dot(agg, wa_ref[...])
+    own.wait()
+    pre = self_ref[...] + pre
     s = sigmoid(pre)
+    cw.wait()
     g_node = (cw_ref[...] * (s * (1.0 + pre * (1.0 - s)))).astype(BF16)
     g_agg = dot_nt(g_node, wa_ref[...]).astype(BF16)
+    oh.wait()
     gask_ref[...] = dot(oh_ref[...], g_agg).astype(BF16)
     gnode_ref[...] = g_node
     nact_ref[...] = (pre * s).astype(BF16)
 
 
 def slot_grad_kernel(gc_ref, we_ref, slope_ref, gsum_ref, h_ref):
-    h = dot_nt(gc_ref[...], we_ref[...])
+    h = 0.5 * dot_nt(gc_ref[...], we_ref[...])
     h_ref[...] = h.astype(BF16)
     gsum_ref[...] = (h * slope_ref[...]).astype(BF16)
 
@@ -260,13 +284,16 @@
 
 
 def edge_back_kernel(
-    steps, slot_ref, slope_ref, lat_t_ref, h_ref, gsum_ref, ml_ref, gc_ref, act_ref, keep_ref, give_ref, total
+    steps, slot_ref, slope_ref, lat_t_ref, h_ref, gsum_hbm, ml_hbm, gc_hbm, act_hbm, keep_ref, give_ref,
+    total, gsum_ref, ml_ref, gc_ref, act_ref, sems,
 ):
     step = pl.program_id(0)
+    late = [(act_hbm, act_ref), (gc_hbm, gc_ref), (ml_hbm, ml_ref), (gsum_hbm, gsum_ref)]
 
     @pl.when(step == 0)
     def _():
         total[...] = jnp.zeros_like(total)
+        load(late, sems)
 
     onehot = edges_by_ids(slot_ref[...], h_ref.shape[0])
     g_edge = (dot(onehot, h_ref[...]) * slope_ref[...].astype(F32)).astype(BF16)
@@ -274,9 +301,11 @@
 
     @pl.when(step == steps - 1)
     def _():
+        for i, (a, b) in enumerate(late):
+            pltpu.make_async_copy(a, b, sems.at[i]).wait()
         put_halves(0, total[...].astype(BF16), keep_ref, give_ref)
-        put_halves(1, dot_tn(act_ref[...], gc_ref[...]).astype(BF16), keep_ref, give_ref)
-        put_halves(2, dot_tn(ml_ref[...], gsum_ref[...]).astype(BF16), keep_ref, give_ref)
+        put_halves(1, dot(act_ref[...], gc_ref[...]).astype(BF16), keep_ref, give_ref)
+        put_halves(2, dot(ml_ref[...], gsum_ref[...]).astype(BF16), keep_ref, give_ref)
 
 
 def parts_kernel(keep_ref, got_ref, out_ref):
@@ -329,6 +358,7 @@
         out_specs=anywhere,
         input_output_aliases={0: 0},
         name="held",
+        compiler_params=pltpu.CompilerParams(vmem_limit_bytes=60 << 20),
     )(value, *after)
 
 
@@ -360,7 +390,7 @@
     block = ROWS * LANES
     steps = edge_dev // block
     scale = (edge_dev * lax.axis_size("x") * lax.axis_size("core") * owners) ** (-0.5)
-    sds = jax.ShapeDtypeStruct
+    sds, hbm = jax.ShapeDtypeStruct, pltpu.HBM
 
     def exchange(value):
         return lax.all_to_all(value, "mesh", 0, 0, tiled=True)
@@ -377,10 +407,10 @@
 
     tile = min(256, grid_dev)
     grid_spec = pl.BlockSpec((tile, width), lambda i: (i, 0))
-    (hidden,) = call(
+    hidden, hidden_done = call(
         hidden_kernel,
         "hidden",
-        [sds((grid_dev, width), BF16)],
+        [hbm((grid_dev, width), BF16)],
         [grid_vars, w_in, b_in.reshape(1, width)],
         2 * grid_dev * width * variables,
         grid=(grid_dev // tile,),
@@ -391,17 +421,19 @@
         ],
         out_specs=[grid_spec],
         after=[ids],
-    )
-
-    node_f, node_b = sds((mesh_dev, width), F32), sds((mesh_dev, width), BF16)
-    self_part, cot_part = call(
+        token=True,
+    )
+
+    node_f, node_b = hbm((mesh_dev, width), F32), hbm((mesh_dev, width), BF16)
+    self_part, cot_part, node_pre_done = call(
         node_pre_kernel,
         "node_pre",
         [node_f, node_f],
         [mesh_latent, cotangent, w_self, b_node.reshape(1, width), w_node_out],
         4 * mesh_dev * width * width,
         vmem=52,
-        after=[hidden],
+        after=[hidden_done],
+        token=True,
     )
     asked, onehot_in = call(
         ask_kernel,
@@ -409,7 +441,7 @@
         [sds((slots, width), BF16), sds((slots, mesh_dev), BF16)],
         [incoming, mesh_latent],
         2 * slots * mesh_dev * width,
-        after=[self_part],
+        after=[node_pre_done],
     )
     incoming_row = incoming[:, :CAP].reshape(1, slots)
     slot_latent = exchange(asked)
@@ -430,11 +462,11 @@
         ],
         out_specs=[whole((width, grid_dev)), edge_spec],
         scratch=[pltpu.VMEM((grid_dev, width), BF16)],
-        vmem=52,
+        vmem=60,
         after=[asked],
     )
 
-    slots_b, slots_f = sds((slots, width), BF16), sds((slots, width), F32)
+    slots_b, slots_h = sds((slots, width), BF16), hbm((slots, width), BF16)
     slots_spec = whole((slots, width))
     mesh_spec = whole((mesh_dev, width))
     weight_spec = whole((width, width))
@@ -443,7 +475,7 @@
     sums, act_sums, slot_pmesh = call(
         functools.partial(edge_kernel, steps),
         "edge",
-        [slots_b, slots_b, slots_b],
+        [slots_b, slots_h, slots_h],
         [slot, edge_pgrid, slot_latent, u_mesh, bias, w_edge],
         4 * edge_dev * slots * width + 6 * slots * width * width,
         grid=(steps,),
@@ -454,17 +486,18 @@
     )
     received = exchange(sums)
 
-    slope, slope_sums = call(
+    slope, slope_sums, slope_done = call(
         slope_kernel,
         "slope",
-        [sds((edge_dev, width), BF16), slots_f],
+        [hbm((edge_dev, width), BF16), hbm((slots, width), F32)],
         [slot, edge_pgrid, slot_pmesh, bias],
         4 * edge_dev * slots * width,
         grid=(steps,),
         in_specs=[id_spec, edge_spec, slots_spec, whole((1, width))],
         out_specs=[edge_spec, slots_spec],
-        vmem=52,
+        vmem=60,
         after=[sums],
+        token=True,
     )
     g_asked, g_node, node_act = call(
         node_kernel,
@@ -472,47 +505,59 @@
         [slots_b, node_b, node_b],
         [received, incoming_row, onehot_in, self_part, cot_part, w_agg],
         4 * mesh_dev * width * width + 4 * mesh_dev * slots * width,
-        vmem=52,
-        after=[slope_sums],
+        in_specs=[pl.BlockSpec(memory_space=pltpu.VMEM)] * 2 + [pl.BlockSpec(memory_space=pl.ANY)] * 4,
+        scratch=[
+            pltpu.VMEM((slots, mesh_dev), BF16),
+            pltpu.VMEM((mesh_dev, width), F32),
+            pltpu.VMEM((mesh_dev, width), F32),
+            pltpu.VMEM((width, width), BF16),
+            pltpu.SemaphoreType.DMA((4,)),
+        ],
+        vmem=60,
+        after=[slope_done],
     )
     slot_g = exchange(g_asked)
 
-    (edge_latent_t,) = call(
+    slots_t_spec = whole((width, slots))
+    edge_latent_t, act_sums_t, slot_latent_t, take_done = call(
         take_latent_kernel,
         "take_latent",
-        [sds((width, edge_dev), BF16)],
-        [grid_ids, latent_t],
+        [hbm((width, edge_dev), BF16), hbm((width, slots), BF16), hbm((width, slots), BF16)],
+        [grid_ids, latent_t, act_sums, slot_latent],
         2 * edge_dev * grid_dev * width,
         grid=(steps,),
-        in_specs=[id_spec, whole((width, grid_dev))],
-        out_specs=[edge_t_spec],
+        in_specs=[id_spec, whole((width, grid_dev)), slots_spec, slots_spec],
+        out_specs=[edge_t_spec, slots_t_spec, slots_t_spec],
         vmem=52,
         after=[g_asked],
+        token=True,
     )
     half = width // 2
     gsum, h = call(
         slot_grad_kernel,
         "slot_grad",
-        [slots_b, slots_b],
+        [slots_h, slots_h],
         [slot_g, w_edge, slope_sums],
         2 * slots * width * width,
         vmem=52,
-        after=[edge_latent_t],
+        after=[take_done],
     )
     gsum_received = exchange(gsum)
 
-    three = sds((3, half, width), BF16)
+    three = hbm((3, half, width), BF16)
     keep, give = call(
         functools.partial(edge_back_kernel, steps),
         "edge_back",
         [three, three],
-        [slot, slope, edge_latent_t, h, gsum, slot_latent, slot_g, act_sums],
+        [slot, slope, edge_latent_t, h, gsum, slot_latent_t, slot_g, act_sums_t],
         2 * edge_dev * (slots + width) * width + 4 * slots * width * width,
         grid=(steps,),
-        in_specs=[id_spec, edge_spec, edge_t_spec] + [slots_spec] * 5,
+        in_specs=[id_spec, edge_spec, edge_t_spec, slots_spec] + [pl.BlockSpec(memory_space=pl.ANY)] * 4,
         out_specs=[whole(three.shape), whole(three.shape)],
-        scratch=[pltpu.VMEM((width, width), F32)],
-        vmem=52,
+        scratch=[pltpu.VMEM((width, width), F32)]
+        + [pltpu.VMEM(a, BF16) for a in ((slots, width), (width, slots)) * 2]
+        + [pltpu.SemaphoreType.DMA((4,))],
+        vmem=60,
     )
     others = ("x", "mesh")
     count = lax.axis_size("x") * owners
@@ -526,7 +571,7 @@
     )
     summed = lax.all_to_all(parts, others, 0, 0, tiled=True)
 
-    mesh_out, grad_mesh = call(
+    mesh_out, grad_mesh, node_post_done = call(
         node_post_kernel,
         "node_post",
         [node_b, node_b],
@@ -537,6 +582,7 @@
         6 * mesh_dev * width * width + 2 * mesh_dev * slots * width,
         vmem=52,
         after=[parts],
+        token=True,
     )
     (copies,) = call(
         functools.partial(spread_kernel, scale),
@@ -544,7 +590,7 @@
         [pieces],
         [summed],
         3 * half * width,
-        after=[mesh_out],
+        after=[node_post_done],
     )
     mine = lax.all_to_all(copies, others, 0, 0, tiled=True)
     weight = sds((width, width), F32)

time: 163 us -> 158 us (0.969)
  local copies, waits for them, and re-layouts: 13.7 us -> 7.17 us
  Pallas kernels: 61.2 us -> 63.9 us
    unnamed x53 -> x51, local copies, waits for them, and re-layouts: 13.7 us -> 6.5 us
    pallas_call x15, Pallas kernels: 61.2 us -> 63.9 us  [call(): pl.pallas_call(body, out_shape=out, in_specs=list(in_specs) + [pl.BlockSp...]
  transfers between devices with their start and end apart: 8 -> 8, of which waited for: 7 -> 7; matrix products, arithmetic and copies ran while one was open for 1% -> 1% of each run, Pallas kernels for 25% -> 27%
where the time goes in v4:
time: 158 us; the launch traced here: 157 us
  Pallas kernels  63.9 us (40%)
  starting transfers between devices  33.6 us (21%)
  waiting for transfers between devices  27.2 us (17%)
  blocking collectives  24.6 us (16%)
  local copies, waits for them, and re-layouts  7.17 us (5%)
    pallas_call x15, Pallas kernels, call(): pl.pallas_call(body, out_shape=out, in_specs=list(in_specs) + [pl.BlockSp...  63.9 us
    all_to_all x5, starting transfers between devices, exchange(): return lax.all_to_all(value, 'mesh', 0, 0, tiled=True)  26.6 us
    all_to_all x1, blocking collectives, shards(): mine = lax.all_to_all(copies, others, 0, 0, tiled=True)  24.6 us
    all_to_all x1, waiting for transfers between devices, shards(): summed = lax.all_to_all(parts, others, 0, 0, tiled=True)  17.7 us
    all_to_all x1, starting transfers between devices, shards(): summed = lax.all_to_all(parts, others, 0, 0, tiled=True)  7.02 us
    unnamed x51, local copies, waits for them, and re-layouts  6.5 us
    ppermute x2, waiting for transfers between devices, other_core(): return lax.ppermute(value, 'core', [(0, 1), (1, 0)])  4.78 us
    all_to_all x5, waiting for transfers between devices, exchange(): return lax.all_to_all(value, 'mesh', 0, 0, tiled=True)  4.74 us
  transfers between devices with their start and end apart: 8, of which 7 were waited for; matrix products, arithmetic and copies ran while one was open for 1% of the time, Pallas kernels for 27%

profile of v4, /device:TPU:0, one launch (start us, length us, event | category | flops | bytes accessed | tf_op | source)
XLA Modules:
  0.0 157.4 jit_solution(14964020146313288499)
XLA Ops:
  1.6 1.8 %prep.1 = (s32[32,128]{1,0:T(8,128)S(1)}, s32[8,128]{1,0:T(8,128)}) custom-call(s32[32,128]{1,0:T(8,128)S(1)} %bitcast.29), custom_call_target="tpu_custom_call" | custom-call | flops 1000000000 | bytes 36864 | tf_op jit(solution)/shard_map/prep/pallas_call | solution.py:67
  3.3 7.3 %all-to-all-start = ((s32[8,1,128]{2,1,0:T(1,128)}), s32[8,1,128]{2,1,0:T(1,128)S(1)}, u32[]{:S(2)}, u32[]{:S(2)}) async-start(s32[8,1,128]{2,1,0:T(1,128)} %bitcast.5), calls=%async_computation | async-start | bytes 8192 | tf_op jit(solution)/shard_map/all_to_all | solution.py:396
  11.9 2.3 %hidden.1 = (bf16[1024,512]{1,0:T(8,128)(2,1)}, s32[8,128]{1,0:T(8,128)S(1)}) custom-call(bf16[1024,227]{1,0:T(8,128)(2,1)S(1)} %copy.24.refs_0_, bf16[227,512]{1,0:T(8,128)(2,1)S(1)} %copy-done.17, f32[1,512]{1,0:T(1,128)S(1)} %bitcast.32, s32[8,128]{1,0:T(8,128)} %get-tuple-element.40.refs_3_), custom_call_target="tpu_custom_call" | custom-call | flops 238026752 | bytes 1747968 | tf_op jit(solution)/shard_map/hidden/pallas_call | solution.py:67
  14.2 1.4 node_pre.1
  15.6 1.4 all-to-all-done
  19.0 4.6 %all-to-all-start.1 = ((bf16[8,48,512]{2,1,0:T(8,128)(2,1)}), bf16[8,48,512]{2,1,0:T(8,128)(2,1)S(1)}, u32[]{:S(2)}, u32[]{:S(2)}) async-start(bf16[8,48,512]{2,1,0:T(8,128)(2,1)} %bitcast.8), calls=%async_computation.1 | async-start | bytes 786432 | tf_op jit(solution)/shard_map/all_to_all | solution.py:396
  23.6 9.7 %grid.1 = (bf16[512,1024]{1,0:T(8,128)(2,1)}, bf16[4096,512]{1,0:T(8,128)(2,1)}) custom-call(s32[32,128]{1,0:T(8,128)} %bitcast.30, bf16[1024,512]{1,0:T(8,128)(2,1)} %get-tuple-element.41.refs_1_, bf16[512,512]{1,0:T(8,128)(2,1)} %refs_2_.3, f32[1,512]{1,0:T(1,128)} %bitcast.37, bf16[512,512]{1,0:T(8,128)(2,1)} %refs_4_.4, ...), custom_call_target="tpu_custom_call" | custom-call | flops 5368709120 | bytes 7358464 | tf_op jit(solution)/shard_map/grid/pallas_call | solution.py:67
  33.3 1.4 all-to-all-done.1
  34.7 9.1 %edge.1 = (bf16[384,512]{1,0:T(8,128)(2,1)}, bf16[384,512]{1,0:T(8,128)(2,1)}, bf16[384,512]{1,0:T(8,128)(2,1)}) custom-call(s32[32,128]{1,0:T(8,128)S(1)} %get-tuple-element.39.refs_0_, bf16[4096,512]{1,0:T(8,128)(2,1)} %get-tuple-element.45.refs_1_, bf16[384,512]{1,0:T(8,128)(2,1)S(1)} %bitcast.23, bf16[512,512]{1,0:T(8,128)(2,1)S(1)} %copy-done.9, ...), custom_call_target="tpu_custom_call" | custom-call | flops 3825205248 | bytes 6834176 | tf_op jit(solution)/shard_map/edge/pallas_call | solution.py:67
  43.8 4.6 %all-to-all-start.2 = ((bf16[8,48,512]{2,1,0:T(8,128)(2,1)}), bf16[8,48,512]{2,1,0:T(8,128)(2,1)S(1)}, u32[]{:S(2)}, u32[]{:S(2)}) async-start(bf16[8,48,512]{2,1,0:T(8,128)(2,1)} %bitcast.11), calls=%async_computation.2 | async-start | bytes 786432 | tf_op jit(solution)/shard_map/all_to_all | solution.py:396
  49.1 9.0 %slope.1 = (bf16[4096,512]{1,0:T(8,128)(2,1)}, f32[384,512]{1,0:T(8,128)}, s32[8,128]{1,0:T(8,128)}) custom-call(s32[32,128]{1,0:T(8,128)} %copy-done.23, bf16[4096,512]{1,0:T(8,128)(2,1)} %get-tuple-element.45.refs_1_, bf16[384,512]{1,0:T(8,128)(2,1)} %get-tuple-element.50.refs_2_, f32[1,512]{1,0:T(1,128)} %bitcast.33, ...), custom_call_target="tpu_custom_call" | custom-call | flops 3221225472 | bytes 9586688 | tf_op jit(solution)/shard_map/slope/pallas_call | solution.py:67
  59.7 4.2 %node.1 = (bf16[384,512]{1,0:T(8,128)(2,1)}, bf16[320,512]{1,0:T(8,128)(2,1)}, bf16[320,512]{1,0:T(8,128)(2,1)}) custom-call(bf16[384,512]{1,0:T(8,128)(2,1)} %bitcast.35, s32[1,384]{1,0:T(1,128)} %reshape.47.refs_1_, bf16[384,320]{1,0:T(8,128)(2,1)} %copy-done.14, f32[320,512]{1,0:T(8,128)} %get-tuple-element.48.refs_3_, ...), custom_call_target="tpu_custom_call" | custom-call | flops 587202560 | bytes 3524096 | tf_op jit(solution)/shard_map/node/pallas_call | solution.py:67
  64.0 5.2 %all-to-all-start.3 = ((bf16[8,48,512]{2,1,0:T(8,128)(2,1)}), bf16[8,48,512]{2,1,0:T(8,128)(2,1)S(1)}, u32[]{:S(2)}, u32[]{:S(2)}) async-start(bf16[8,48,512]{2,1,0:T(8,128)(2,1)} %bitcast.25), calls=%async_computation.3 | async-start | bytes 786432 | tf_op jit(solution)/shard_map/all_to_all | solution.py:396
  70.2 7.8 %take_latent.1 = (bf16[512,4096]{1,0:T(8,128)(2,1)}, bf16[512,384]{1,0:T(8,128)(2,1)}, bf16[512,384]{1,0:T(8,128)(2,1)}, s32[8,128]{1,0:T(8,128)S(1)}) custom-call(s32[32,128]{1,0:T(8,128)S(1)} %bitcast.31, bf16[512,1024]{1,0:T(8,128)(2,1)} %get-tuple-element.54.refs_1_, bf16[384,512]{1,0:T(8,128)(2,1)S(1)} %copy-done.22, bf16[384,512]{1,0:T(8,128)(2,1)S(1)} %bitcast.24, ...), custom_call_target="tpu_custom_call" | custom-call | flops 4294967296 | bytes 6832128 | tf_op jit(solution)/shard_map/take_latent/pallas_call | solution.py:67
  79.1 1.3 slot_grad.1
  80.4 4.9 %all-to-all-start.4 = ((bf16[8,48,512]{2,1,0:T(8,128)(2,1)}), bf16[8,48,512]{2,1,0:T(8,128)(2,1)S(1)}, u32[]{:S(2)}, u32[]{:S(2)}) async-start(bf16[8,48,512]{2,1,0:T(8,128)(2,1)} %bitcast.36), calls=%async_computation.4 | async-start | bytes 786432 | tf_op jit(solution)/shard_map/all_to_all | solution.py:396
  85.3 10.0 %edge_back.1 = (bf16[3,256,512]{2,1,0:T(8,128)(2,1)}, bf16[3,256,512]{2,1,0:T(8,128)(2,1)}) custom-call(s32[32,128]{1,0:T(8,128)} %copy-done.23, bf16[4096,512]{1,0:T(8,128)(2,1)} %get-tuple-element.60.refs_1_, bf16[512,4096]{1,0:T(8,128)(2,1)} %get-tuple-element.61.refs_2_, bf16[384,512]{1,0:T(8,128)(2,1)} %get-tuple-element.62.refs_3_, ...), custom_call_target="tpu_custom_call" | custom-call | flops 4160749568 | bytes 11943936 | tf_op jit(solution)/shard_map/edge_back/pallas_call | solution.py:67
  96.1 2.5 %collective-permute-done.refs_1_ = bf16[3,256,512]{2,1,0:T(8,128)(2,1)S(1)} collective-permute-done((bf16[3,256,512]{2,1,0:T(8,128)(2,1)}, bf16[3,256,512]{2,1,0:T(8,128)(2,1)S(1)}, u32[]{:S(2)}, u32[]{:S(2)}) %collective-permute-start) | collective-permute-done | bytes 786464 | tf_op jit(solution)/shard_map/ppermute | solution.py:346
  100.8 7.0 %all-to-all-start.5 = ((bf16[16,48,512]{2,1,0:T(8,128)(2,1)}), bf16[16,48,512]{2,1,0:T(8,128)(2,1)S(1)}, u32[]{:S(2)}, u32[]{:S(2)}) async-start(bf16[16,48,512]{2,1,0:T(8,128)(2,1)} %parts.1.refs_9_), calls=%async_computation.5 | async-start | bytes 1572864 | tf_op jit(solution)/shard_map/all_to_all | solution.py:572
  107.8 2.9 %node_post.1 = (bf16[320,512]{1,0:T(8,128)(2,1)}, bf16[320,512]{1,0:T(8,128)(2,1)}, s32[8,128]{1,0:T(8,128)S(1)}) custom-call(bf16[384,512]{1,0:T(8,128)(2,1)S(1)} %bitcast.20, s32[1,384]{1,0:T(1,128)S(1)} %copy-done.15, bf16[320,512]{1,0:T(8,128)(2,1)S(1)} %copy-done.12, bf16[320,512]{1,0:T(8,128)(2,1)S(1)} %copy-done.13, bf16[320,512]{1,0:T(8,128)(2,1)S(1)} %copy-done.5, ...), custom_call_target="tpu_custom_call" | custom-call | flops 629145600 | bytes 3933696 | tf_op jit(solution)/shard_map/node_post/pallas_call | solution.py:67
  110.8 17.7 %all-to-all-done.5.refs_0_ = bf16[16,48,512]{2,1,0:T(8,128)(2,1)S(1)} async-done(((bf16[16,48,512]{2,1,0:T(8,128)(2,1)}), bf16[16,48,512]{2,1,0:T(8,128)(2,1)S(1)}, u32[]{:S(2)}, u32[]{:S(2)}) %all-to-all-start.5) | async-done | bytes 786464 | tf_op jit(solution)/shard_map/all_to_all | solution.py:572
  128.6 24.6 %all_to_all.65.refs_0_ = bf16[16,48,512]{2,1,0:T(8,128)(2,1)S(1)} all-to-all(bf16[16,48,512]{2,1,0:T(8,128)(2,1)S(1)} %spread.1), channel_id=1, replica_groups=mesh['x'=2,'core'=2,'mesh'=8] {'x','mesh'}, dimensions={0} | all-to-all | bytes 1572864 | tf_op jit(solution)/shard_map/all_to_all | solution.py:595
  153.3 2.3 %collective-permute-done.1.refs_1_ = bf16[16,48,512]{2,1,0:T(8,128)(2,1)S(1)} collective-permute-done((bf16[16,48,512]{2,1,0:T(8,128)(2,1)S(1)}, bf16[16,48,512]{2,1,0:T(8,128)(2,1)S(1)}, u32[]{:S(2)}, u32[]{:S(2)}) %collective-permute-start.1) | collective-permute-done | bytes 786464 | tf_op jit(solution)/shard_map/ppermute | solution.py:346
  155.5 1.9 %finish.1 = (f32[512,512]{1,0:T(8,128)}, f32[512,512]{1,0:T(8,128)}, f32[512,512]{1,0:T(8,128)}) custom-call(bf16[16,48,512]{2,1,0:T(8,128)(2,1)S(1)} %all_to_all.65.refs_0_, bf16[16,48,512]{2,1,0:T(8,128)(2,1)S(1)} %collective-permute-done.1.refs_1_), custom_call_target="tpu_custom_call" | custom-call | flops 786432 | bytes 4718592 | tf_op jit(solution)/shard_map/finish/pallas_call | solution.py:67
  (61 shorter events, 11.6 us)
Async XLA Ops:
  0.6 11.2 %copy-start.17 = (bf16[227,512]{1,0:T(8,128)(2,1)S(1)}, bf16[227,512]{1,0:T(8,128)(2,1)}, u32[]{:S(2)}) copy-start(bf16[227,512]{1,0:T(8,128)(2,1)} %refs_1_.4) | copy-start | bytes 697348
  0.6 13.5 %copy-start.16 = (f32[512]{0:T(512)S(1)}, f32[512]{0:T(512)}, u32[]{:S(2)}) copy-start(f32[512]{0:T(512)} %param.32) | copy-start | bytes 6148
  0.7 13.5 %copy-start.5 = (bf16[320,512]{1,0:T(8,128)(2,1)S(1)}, bf16[320,512]{1,0:T(8,128)(2,1)}, u32[]{:S(2)}) copy-start(bf16[320,512]{1,0:T(8,128)(2,1)} %refs_4_.5) | copy-start | bytes 983044
  0.7 13.5 %copy-start.6 = (bf16[320,512]{1,0:T(8,128)(2,1)S(1)}, bf16[320,512]{1,0:T(8,128)(2,1)}, u32[]{:S(2)}) copy-start(bf16[320,512]{1,0:T(8,128)(2,1)} %refs_5_.5) | copy-start | bytes 983044
  0.7 13.5 %copy-start.2 = (bf16[512,512]{1,0:T(8,128)(2,1)S(1)}, bf16[512,512]{1,0:T(8,128)(2,1)}, u32[]{:S(2)}) copy-start(bf16[512,512]{1,0:T(8,128)(2,1)} %refs_7_.1) | copy-start | bytes 1572868
  0.7 13.5 %copy-start.3 = (bf16[512,512]{1,0:T(8,128)(2,1)S(1)}, bf16[512,512]{1,0:T(8,128)(2,1)}, u32[]{:S(2)}) copy-start(bf16[512,512]{1,0:T(8,128)(2,1)} %refs_6_.1) | copy-start | bytes 1572868
  3.3 31.4 %copy-start.23 = (s32[32,128]{1,0:T(8,128)}, s32[32,128]{1,0:T(8,128)S(1)}, u32[]{:S(2)}) copy-start(s32[32,128]{1,0:T(8,128)S(1)} %get-tuple-element.39.refs_0_) | copy-start | bytes 49156
  3.3 13.7 %all-to-all-start = ((s32[8,1,128]{2,1,0:T(1,128)}), s32[8,1,128]{2,1,0:T(1,128)S(1)}, u32[]{:S(2)}, u32[]{:S(2)}) async-start(s32[8,1,128]{2,1,0:T(1,128)} %bitcast.5), calls=%async_computation | async-start | bytes 8192 | tf_op jit(solution)/shard_map/all_to_all | solution.py:396
  19.0 15.7 %all-to-all-start.1 = ((bf16[8,48,512]{2,1,0:T(8,128)(2,1)}), bf16[8,48,512]{2,1,0:T(8,128)(2,1)S(1)}, u32[]{:S(2)}, u32[]{:S(2)}) async-start(bf16[8,48,512]{2,1,0:T(8,128)(2,1)} %bitcast.8), calls=%async_computation.1 | async-start | bytes 786432 | tf_op jit(solution)/shard_map/all_to_all | solution.py:396
  23.6 11.1 %copy-start.9 = (bf16[512,512]{1,0:T(8,128)(2,1)S(1)}, bf16[512,512]{1,0:T(8,128)(2,1)}, u32[]{:S(2)}) copy-start(bf16[512,512]{1,0:T(8,128)(2,1)} %refs_8_.1) | copy-start | bytes 1572868
  23.6 11.1 %copy-start.10 = (bf16[512,512]{1,0:T(8,128)(2,1)S(1)}, bf16[512,512]{1,0:T(8,128)(2,1)}, u32[]{:S(2)}) copy-start(bf16[512,512]{1,0:T(8,128)(2,1)} %refs_1_.7) | copy-start | bytes 1572868
  23.6 11.1 %copy-start.21 = (f32[512]{0:T(512)S(1)}, f32[512]{0:T(512)}, u32[]{:S(2)}) copy-start(f32[512]{0:T(512)} %param.28) | copy-start | bytes 6148
  43.8 15.2 %all-to-all-start.2 = ((bf16[8,48,512]{2,1,0:T(8,128)(2,1)}), bf16[8,48,512]{2,1,0:T(8,128)(2,1)S(1)}, u32[]{:S(2)}, u32[]{:S(2)}) async-start(bf16[8,48,512]{2,1,0:T(8,128)(2,1)} %bitcast.11), calls=%async_computation.2 | async-start | bytes 786432 | tf_op jit(solution)/shard_map/all_to_all | solution.py:396
  49.1 20.1 %copy-start.19 = (s32[4096]{0:T(1024)S(1)}, s32[4096]{0:T(1024)}, u32[]{:S(2)}) copy-start(s32[4096]{0:T(1024)} %param.20) | copy-start | bytes 49156
  49.1 20.1 %copy-start.22 = (bf16[384,512]{1,0:T(8,128)(2,1)S(1)}, bf16[384,512]{1,0:T(8,128)(2,1)}, u32[]{:S(2)}) copy-start(bf16[384,512]{1,0:T(8,128)(2,1)} %get-tuple-element.55.refs_2_) | copy-start | bytes 1179652
  64.0 15.2 %all-to-all-start.3 = ((bf16[8,48,512]{2,1,0:T(8,128)(2,1)}), bf16[8,48,512]{2,1,0:T(8,128)(2,1)S(1)}, u32[]{:S(2)}, u32[]{:S(2)}) async-start(bf16[8,48,512]{2,1,0:T(8,128)(2,1)} %bitcast.25), calls=%async_computation.3 | async-start | bytes 786432 | tf_op jit(solution)/shard_map/all_to_all | solution.py:396
  80.4 14.9 %all-to-all-start.4 = ((bf16[8,48,512]{2,1,0:T(8,128)(2,1)}), bf16[8,48,512]{2,1,0:T(8,128)(2,1)S(1)}, u32[]{:S(2)}, u32[]{:S(2)}) async-start(bf16[8,48,512]{2,1,0:T(8,128)(2,1)} %bitcast.36), calls=%async_computation.4 | async-start | bytes 786432 | tf_op jit(solution)/shard_map/all_to_all | solution.py:396
  95.3 12.5 %copy-start.12 = (bf16[320,512]{1,0:T(8,128)(2,1)S(1)}, bf16[320,512]{1,0:T(8,128)(2,1)}, u32[]{:S(2)}) copy-start(bf16[320,512]{1,0:T(8,128)(2,1)} %get-tuple-element.58.refs_2_) | copy-start | bytes 983044
  95.3 12.5 %copy-start.13 = (bf16[320,512]{1,0:T(8,128)(2,1)S(1)}, bf16[320,512]{1,0:T(8,128)(2,1)}, u32[]{:S(2)}) copy-start(bf16[320,512]{1,0:T(8,128)(2,1)} %get-tuple-element.59.refs_3_) | copy-start | bytes 983044
  95.3 12.5 %copy-start.15 = (s32[1,384]{1,0:T(1,128)S(1)}, s32[1,384]{1,0:T(1,128)}, u32[]{:S(2)}) copy-start(s32[1,384]{1,0:T(1,128)} %reshape.47.refs_1_) | copy-start | bytes 4612
  96.1 11.7 %copy-start.1 = (bf16[8,48,512]{2,1,0:T(8,128)(2,1)S(1)}, bf16[8,48,512]{2,1,0:T(8,128)(2,1)}, u32[]{:S(2)}) copy-start(bf16[8,48,512]{2,1,0:T(8,128)(2,1)} %copy-done) | copy-start | bytes 1179652
  96.1 2.5 %collective-permute-start = (bf16[3,256,512]{2,1,0:T(8,128)(2,1)}, bf16[3,256,512]{2,1,0:T(8,128)(2,1)S(1)}, u32[]{:S(2)}, u32[]{:S(2)}) collective-permute-start(bf16[3,256,512]{2,1,0:T(8,128)(2,1)} %held.1), channel_id=1, source_target_pairs={{0,8},{8,0},{1,9},{9,1},{2,10},{10,2},{3,11},{11,3},{4,12},{12,4},... | collective-permute-start | bytes 2359304 | tf_op jit(solution)/shard_map/ppermute | solution.py:346
  100.8 27.7 %all-to-all-start.5 = ((bf16[16,48,512]{2,1,0:T(8,128)(2,1)}), bf16[16,48,512]{2,1,0:T(8,128)(2,1)S(1)}, u32[]{:S(2)}, u32[]{:S(2)}) async-start(bf16[16,48,512]{2,1,0:T(8,128)(2,1)} %parts.1.refs_9_), calls=%async_computation.5 | async-start | bytes 1572864 | tf_op jit(solution)/shard_map/all_to_all | solution.py:572
  153.3 2.3 %collective-permute-start.1 = (bf16[16,48,512]{2,1,0:T(8,128)(2,1)S(1)}, bf16[16,48,512]{2,1,0:T(8,128)(2,1)S(1)}, u32[]{:S(2)}, u32[]{:S(2)}) collective-permute-start(bf16[16,48,512]{2,1,0:T(8,128)(2,1)S(1)} %all_to_all.65.refs_0_), channel_id=1, source_target_pairs={{0,8},{8,0},{1,9},{9,1},{2,10},{10,2},{3,11},{11,3},{4,12},{12,4},... | collective-permute-start | bytes 2359304 | tf_op jit(solution)/shard_map/ppermute | solution.py:346
  (9 other events, 30.7 us)

commit v5 on v4

--- a/solution.py
+++ b/solution.py
@@ -321,25 +321,37 @@
     out_ref[...] = jnp.broadcast_to(total[None], out_ref.shape)
 
 
-def finish_kernel(mine_ref, other_ref, *out_refs):
-    count, rows, width = mine_ref.shape
+def finish_kernel(ours, part_ref, *refs):
+    *out_refs, rows_ref, sems = refs[-5:]
+    count, rows, width = part_ref.shape
     low = rows // len(out_refs)
     half = count * low
     core = lax.axis_index("core")
-
-    def put(upper_ref, lower_ref):
-        for i, out_ref in enumerate(out_refs):
-            piece = slice(i * low, (i + 1) * low)
-            out_ref[:half] = upper_ref[:, piece].astype(F32).reshape(half, width)
-            out_ref[half:] = lower_ref[:, piece].astype(F32).reshape(half, width)
-
-    @pl.when(core == 0)
-    def _():
-        put(mine_ref, other_ref)
-
-    @pl.when(core != 0)
-    def _():
-        put(other_ref, mine_ref)
+    start = pl.multiple_of((core if ours else 1 - core) * half, half)
+    copies = []
+    for i, out_ref in enumerate(out_refs):
+        piece = part_ref[:, i * low : (i + 1) * low]
+        rows_ref[i] = piece.astype(F32).reshape(half, width)
+        copies.append(pltpu.make_async_copy(rows_ref.at[i], out_ref.at[pl.ds(start, half)], sems.at[i]))
+        copies[i].start()
+    for copy in copies:
+        copy.wait()
+
+
+def finish(ours, part, width, before=()):
+    anywhere = pl.BlockSpec(memory_space=pl.ANY)
+    half = width // 2
+    return pl.pallas_call(
+        functools.partial(finish_kernel, ours),
+        out_shape=[jax.ShapeDtypeStruct((width, width), F32)] * 3,
+        in_specs=[pl.BlockSpec(memory_space=pltpu.VMEM)] + [anywhere] * len(before),
+        out_specs=[anywhere] * 3,
+        scratch_shapes=[pltpu.VMEM((3, half, width), F32), pltpu.SemaphoreType.DMA((3,))],
+        input_output_aliases={i + 1: i for i in range(len(before))},
+        name="finish_ours" if ours else "finish_other",
+        cost_estimate=pl.CostEstimate(flops=3 * half * width, bytes_accessed=18 * half * width, transcendentals=0),
+        compiler_params=pltpu.CompilerParams(vmem_limit_bytes=16 << 20),
+    )(part, *before)
 
 
 def other_core(value):
@@ -402,6 +414,7 @@
         [sds((rows, LANES), jnp.int32), sds((owners, LANES), jnp.int32)],
         [edge_mesh.reshape(rows, LANES)],
         1e9,
+        vmem=60,
     )
     incoming = exchange(ids)
 
@@ -513,7 +526,7 @@
             pltpu.VMEM((width, width), BF16),
             pltpu.SemaphoreType.DMA((4,)),
         ],
-        vmem=60,
+        vmem=52,
         after=[slope_done],
     )
     slot_g = exchange(g_asked)
@@ -593,10 +606,8 @@
         after=[node_post_done],
     )
     mine = lax.all_to_all(copies, others, 0, 0, tiled=True)
-    weight = sds((width, width), F32)
-    grad_ugrid, grad_edge, grad_umesh = call(
-        finish_kernel, "finish", [weight] * 3, [mine, other_core(mine)], 3 * width * width
-    )
+    other = other_core(mine)
+    grad_ugrid, grad_edge, grad_umesh = finish(False, other, width, finish(True, mine, width))
     return mesh_out, grad_mesh, grad_edge, grad_ugrid, grad_umesh
 
 

time: 158 us -> 155 us (0.981)
  local copies, waits for them, and re-layouts: 7.17 us -> 4.65 us
    pallas_call x0 -> x2, Pallas kernels: none -> 2.4 us  [finish(): pl.pallas_call(functools.partial(finish_kernel, ours), out_shape=[jax.Sha...]
    pallas_call x15 -> x14, Pallas kernels: 63.9 us -> 61.8 us  [call(): pl.pallas_call(body, out_shape=out, in_specs=list(in_specs) + [pl.BlockSp...]
    unnamed x51, local copies, waits for them, and re-layouts: 6.5 us -> 4.58 us
  transfers between devices with their start and end apart: 8 -> 8, of which waited for: 7 -> 8; matrix products, arithmetic and copies ran while one was open for 1% -> 1% of each run, Pallas kernels for 27% -> 29%
where the time goes in v5:
time: 155 us; the launch traced here: 154 us
  Pallas kernels  64.2 us (41%)
  starting transfers between devices  32.1 us (21%)
  waiting for transfers between devices  27.5 us (18%)
  blocking collectives  24.6 us (16%)
  local copies, waits for them, and re-layouts  4.65 us (3%)
    pallas_call x14, Pallas kernels, call(): pl.pallas_call(body, out_shape=out, in_specs=list(in_specs) + [pl.BlockSp...  61.8 us
    all_to_all x5, starting transfers between devices, exchange(): return lax.all_to_all(value, 'mesh', 0, 0, tiled=True)  25.7 us
    all_to_all x1, blocking collectives, shards(): mine = lax.all_to_all(copies, others, 0, 0, tiled=True)  24.6 us
    all_to_all x1, waiting for transfers between devices, shards(): summed = lax.all_to_all(parts, others, 0, 0, tiled=True)  17.7 us
    all_to_all x1, starting transfers between devices, shards(): summed = lax.all_to_all(parts, others, 0, 0, tiled=True)  6.44 us
    all_to_all x5, waiting for transfers between devices, exchange(): return lax.all_to_all(value, 'mesh', 0, 0, tiled=True)  6.2 us
    unnamed x51, local copies, waits for them, and re-layouts  4.58 us
    ppermute x2, waiting for transfers between devices, other_core(): return lax.ppermute(value, 'core', [(0, 1), (1, 0)])  3.57 us
  transfers between devices with their start and end apart: 8, of which 8 were waited for; matrix products, arithmetic and copies ran while one was open for 1% of the time, Pallas kernels for 29%

profile of v5, /device:TPU:0, one launch (start us, length us, event | category | flops | bytes accessed | tf_op | source)
XLA Modules:
  0.0 154.2 jit_solution(10514421393548151586)
XLA Ops:
  0.7 2.6 %prep.1 = (s32[32,128]{1,0:T(8,128)}, s32[8,128]{1,0:T(8,128)}) custom-call(s32[32,128]{1,0:T(8,128)} %bitcast.36), custom_call_target="tpu_custom_call" | custom-call | flops 1000000000 | bytes 36864 | tf_op jit(solution)/shard_map/prep/pallas_call | solution.py:67
  3.3 7.3 %all-to-all-start = ((s32[8,1,128]{2,1,0:T(1,128)}), s32[8,1,128]{2,1,0:T(1,128)S(1)}, u32[]{:S(2)}, u32[]{:S(2)}) async-start(s32[8,1,128]{2,1,0:T(1,128)} %bitcast.28), calls=%async_computation | async-start | bytes 8192 | tf_op jit(solution)/shard_map/all_to_all | solution.py:408
  12.6 2.2 %hidden.1 = (bf16[1024,512]{1,0:T(8,128)(2,1)}, s32[8,128]{1,0:T(8,128)S(1)}) custom-call(bf16[1024,227]{1,0:T(8,128)(2,1)S(1)} %copy.27.refs_0_, bf16[227,512]{1,0:T(8,128)(2,1)S(1)} %copy-done.19, f32[1,512]{1,0:T(1,128)S(1)} %bitcast.32, s32[8,128]{1,0:T(8,128)S(1)} %copy-done.17), custom_call_target="tpu_custom_call" | custom-call | flops 238026752 | bytes 1747968 | tf_op jit(solution)/shard_map/hidden/pallas_call | solution.py:67
  14.8 1.4 node_pre.1
  17.0 1.2 ask.1
  18.3 5.3 %all-to-all-start.1 = ((bf16[8,48,512]{2,1,0:T(8,128)(2,1)}), bf16[8,48,512]{2,1,0:T(8,128)(2,1)S(1)}, u32[]{:S(2)}, u32[]{:S(2)}) async-start(bf16[8,48,512]{2,1,0:T(8,128)(2,1)} %bitcast.8), calls=%async_computation.1 | async-start | bytes 786432 | tf_op jit(solution)/shard_map/all_to_all | solution.py:408
  23.6 9.8 %grid.1 = (bf16[512,1024]{1,0:T(8,128)(2,1)}, bf16[4096,512]{1,0:T(8,128)(2,1)}) custom-call(s32[32,128]{1,0:T(8,128)} %bitcast.30, bf16[1024,512]{1,0:T(8,128)(2,1)} %get-tuple-element.44.refs_1_, bf16[512,512]{1,0:T(8,128)(2,1)} %refs_2_.3, f32[1,512]{1,0:T(1,128)} %bitcast.37, bf16[512,512]{1,0:T(8,128)(2,1)} %refs_4_.4, ...), custom_call_target="tpu_custom_call" | custom-call | flops 5368709120 | bytes 7358464 | tf_op jit(solution)/shard_map/grid/pallas_call | solution.py:67
  33.3 1.3 all-to-all-done.1
  34.7 9.2 %edge.1 = (bf16[384,512]{1,0:T(8,128)(2,1)}, bf16[384,512]{1,0:T(8,128)(2,1)}, bf16[384,512]{1,0:T(8,128)(2,1)}) custom-call(s32[32,128]{1,0:T(8,128)S(1)} %copy-done.24, bf16[4096,512]{1,0:T(8,128)(2,1)} %get-tuple-element.48.refs_1_, bf16[384,512]{1,0:T(8,128)(2,1)S(1)} %bitcast.24, bf16[512,512]{1,0:T(8,128)(2,1)S(1)} %copy-done.10, ...), custom_call_target="tpu_custom_call" | custom-call | flops 3825205248 | bytes 6834176 | tf_op jit(solution)/shard_map/edge/pallas_call | solution.py:67
  43.8 4.6 %all-to-all-start.2 = ((bf16[8,48,512]{2,1,0:T(8,128)(2,1)}), bf16[8,48,512]{2,1,0:T(8,128)(2,1)S(1)}, u32[]{:S(2)}, u32[]{:S(2)}) async-start(bf16[8,48,512]{2,1,0:T(8,128)(2,1)} %bitcast.11), calls=%async_computation.2 | async-start | bytes 786432 | tf_op jit(solution)/shard_map/all_to_all | solution.py:408
  48.6 9.1 %slope.1 = (bf16[4096,512]{1,0:T(8,128)(2,1)}, f32[384,512]{1,0:T(8,128)}, s32[8,128]{1,0:T(8,128)}) custom-call(s32[32,128]{1,0:T(8,128)} %get-tuple-element.42.refs_0_, bf16[4096,512]{1,0:T(8,128)(2,1)} %get-tuple-element.48.refs_1_, bf16[384,512]{1,0:T(8,128)(2,1)} %get-tuple-element.53.refs_2_, f32[1,512]{1,0:T(1,128)} %bitcast.33, ...), custom_call_target="tpu_custom_call" | custom-call | flops 3221225472 | bytes 9586688 | tf_op jit(solution)/shard_map/slope/pallas_call | solution.py:67
  57.7 1.4 all-to-all-done.2
  59.8 3.0 %node.1 = (bf16[384,512]{1,0:T(8,128)(2,1)}, bf16[320,512]{1,0:T(8,128)(2,1)}, bf16[320,512]{1,0:T(8,128)(2,1)}) custom-call(bf16[384,512]{1,0:T(8,128)(2,1)S(1)} %bitcast.21, s32[1,384]{1,0:T(1,128)S(1)} %reshape.47.refs_1_, bf16[384,320]{1,0:T(8,128)(2,1)S(1)} %get-tuple-element.50.refs_2_, f32[320,512]{1,0:T(8,128)} %get-tuple-element.51.refs_3_, ...), custom_call_target="tpu_custom_call" | custom-call | flops 587202560 | bytes 3524096 | tf_op jit(solution)/shard_map/node/pallas_call | solution.py:67
  62.8 4.7 %all-to-all-start.3 = ((bf16[8,48,512]{2,1,0:T(8,128)(2,1)}), bf16[8,48,512]{2,1,0:T(8,128)(2,1)S(1)}, u32[]{:S(2)}, u32[]{:S(2)}) async-start(bf16[8,48,512]{2,1,0:T(8,128)(2,1)} %bitcast.13), calls=%async_computation.3 | async-start | bytes 786432 | tf_op jit(solution)/shard_map/all_to_all | solution.py:408
  67.5 7.8 %take_latent.1 = (bf16[512,4096]{1,0:T(8,128)(2,1)}, bf16[512,384]{1,0:T(8,128)(2,1)}, bf16[512,384]{1,0:T(8,128)(2,1)}, s32[8,128]{1,0:T(8,128)S(1)}) custom-call(s32[32,128]{1,0:T(8,128)S(1)} %bitcast.31, bf16[512,1024]{1,0:T(8,128)(2,1)} %get-tuple-element.57.refs_1_, bf16[384,512]{1,0:T(8,128)(2,1)S(1)} %copy-done.23, bf16[384,512]{1,0:T(8,128)(2,1)S(1)} %bitcast.25, ...), custom_call_target="tpu_custom_call" | custom-call | flops 4294967296 | bytes 6832128 | tf_op jit(solution)/shard_map/take_latent/pallas_call | solution.py:67
  75.3 2.1 %all-to-all-done.3 = bf16[8,48,512]{2,1,0:T(8,128)(2,1)S(1)} async-done(((bf16[8,48,512]{2,1,0:T(8,128)(2,1)}), bf16[8,48,512]{2,1,0:T(8,128)(2,1)S(1)}, u32[]{:S(2)}, u32[]{:S(2)}) %all-to-all-start.3) | async-done | bytes 393248 | tf_op jit(solution)/shard_map/all_to_all | solution.py:408
  77.5 1.3 slot_grad.1
  78.8 3.9 %all-to-all-start.4 = ((bf16[8,48,512]{2,1,0:T(8,128)(2,1)}), bf16[8,48,512]{2,1,0:T(8,128)(2,1)S(1)}, u32[]{:S(2)}, u32[]{:S(2)}) async-start(bf16[8,48,512]{2,1,0:T(8,128)(2,1)} %bitcast.35), calls=%async_computation.4 | async-start | bytes 786432 | tf_op jit(solution)/shard_map/all_to_all | solution.py:408
  82.6 10.0 %edge_back.1 = (bf16[3,256,512]{2,1,0:T(8,128)(2,1)}, bf16[3,256,512]{2,1,0:T(8,128)(2,1)}) custom-call(s32[32,128]{1,0:T(8,128)} %get-tuple-element.42.refs_0_, bf16[4096,512]{1,0:T(8,128)(2,1)} %get-tuple-element.63.refs_1_, bf16[512,4096]{1,0:T(8,128)(2,1)} %get-tuple-element.64.refs_2_, bf16[384,512]{1,0:T(8,128)(2,1)} %get-tuple-element.65.refs_3_, ...), custom_call_target="tpu_custom_call" | custom-call | flops 4160749568 | bytes 11943936 | tf_op jit(solution)/shard_map/edge_back/pallas_call | solution.py:67
  94.0 2.5 %collective-permute-done.refs_1_ = bf16[3,256,512]{2,1,0:T(8,128)(2,1)S(1)} collective-permute-done((bf16[3,256,512]{2,1,0:T(8,128)(2,1)}, bf16[3,256,512]{2,1,0:T(8,128)(2,1)S(1)}, u32[]{:S(2)}, u32[]{:S(2)}) %collective-permute-start) | collective-permute-done | bytes 786464 | tf_op jit(solution)/shard_map/ppermute | solution.py:358
  98.7 6.4 %all-to-all-start.5 = ((bf16[16,48,512]{2,1,0:T(8,128)(2,1)}), bf16[16,48,512]{2,1,0:T(8,128)(2,1)S(1)}, u32[]{:S(2)}, u32[]{:S(2)}) async-start(bf16[16,48,512]{2,1,0:T(8,128)(2,1)} %parts.1.refs_9_), calls=%async_computation.5 | async-start | bytes 1572864 | tf_op jit(solution)/shard_map/all_to_all | solution.py:585
  105.1 2.9 %node_post.1 = (bf16[320,512]{1,0:T(8,128)(2,1)}, bf16[320,512]{1,0:T(8,128)(2,1)}, s32[8,128]{1,0:T(8,128)S(1)}) custom-call(bf16[384,512]{1,0:T(8,128)(2,1)S(1)} %bitcast.20, s32[1,384]{1,0:T(1,128)S(1)} %reshape.47.refs_1_, bf16[320,512]{1,0:T(8,128)(2,1)S(1)} %copy-done.14, bf16[320,512]{1,0:T(8,128)(2,1)S(1)} %copy-done.15, ...), custom_call_target="tpu_custom_call" | custom-call | flops 629145600 | bytes 3933696 | tf_op jit(solution)/shard_map/node_post/pallas_call | solution.py:67
  108.1 17.7 %all-to-all-done.5.refs_0_ = bf16[16,48,512]{2,1,0:T(8,128)(2,1)S(1)} async-done(((bf16[16,48,512]{2,1,0:T(8,128)(2,1)}), bf16[16,48,512]{2,1,0:T(8,128)(2,1)S(1)}, u32[]{:S(2)}, u32[]{:S(2)}) %all-to-all-start.5) | async-done | bytes 786464 | tf_op jit(solution)/shard_map/all_to_all | solution.py:585
  125.9 24.6 %all_to_all.65.part_ref = bf16[16,48,512]{2,1,0:T(8,128)(2,1)S(1)} all-to-all(bf16[16,48,512]{2,1,0:T(8,128)(2,1)S(1)} %spread.1), channel_id=1, replica_groups=mesh['x'=2,'core'=2,'mesh'=8] {'x','mesh'}, dimensions={0} | all-to-all | bytes 1572864 | tf_op jit(solution)/shard_map/all_to_all | solution.py:608
  (62 shorter events, 10.7 us)
Async XLA Ops:
  0.6 11.2 %copy-start.21 = (f32[512]{0:T(512)S(1)}, f32[512]{0:T(512)}, u32[]{:S(2)}) copy-start(f32[512]{0:T(512)} %param.23) | copy-start | bytes 6148
  0.6 11.2 %copy-start.19 = (bf16[227,512]{1,0:T(8,128)(2,1)S(1)}, bf16[227,512]{1,0:T(8,128)(2,1)}, u32[]{:S(2)}) copy-start(bf16[227,512]{1,0:T(8,128)(2,1)} %refs_1_.4) | copy-start | bytes 697348
  0.7 14.2 %copy-start.18 = (f32[512]{0:T(512)S(1)}, f32[512]{0:T(512)}, u32[]{:S(2)}) copy-start(f32[512]{0:T(512)} %param.32) | copy-start | bytes 6148
  0.7 14.1 %copy-start.5 = (bf16[320,512]{1,0:T(8,128)(2,1)S(1)}, bf16[320,512]{1,0:T(8,128)(2,1)}, u32[]{:S(2)}) copy-start(bf16[320,512]{1,0:T(8,128)(2,1)} %refs_4_.5) | copy-start | bytes 983044
  0.7 14.1 %copy-start.6 = (bf16[320,512]{1,0:T(8,128)(2,1)S(1)}, bf16[320,512]{1,0:T(8,128)(2,1)}, u32[]{:S(2)}) copy-start(bf16[320,512]{1,0:T(8,128)(2,1)} %refs_5_.5) | copy-start | bytes 983044
  0.7 14.1 %copy-start.2 = (bf16[512,512]{1,0:T(8,128)(2,1)S(1)}, bf16[512,512]{1,0:T(8,128)(2,1)}, u32[]{:S(2)}) copy-start(bf16[512,512]{1,0:T(8,128)(2,1)} %refs_7_.1) | copy-start | bytes 1572868
  0.7 14.1 %copy-start.3 = (bf16[512,512]{1,0:T(8,128)(2,1)S(1)}, bf16[512,512]{1,0:T(8,128)(2,1)}, u32[]{:S(2)}) copy-start(bf16[512,512]{1,0:T(8,128)(2,1)} %refs_6_.1) | copy-start | bytes 1572868
  3.3 13.7 %all-to-all-start = ((s32[8,1,128]{2,1,0:T(1,128)}), s32[8,1,128]{2,1,0:T(1,128)S(1)}, u32[]{:S(2)}, u32[]{:S(2)}) async-start(s32[8,1,128]{2,1,0:T(1,128)} %bitcast.28), calls=%async_computation | async-start | bytes 8192 | tf_op jit(solution)/shard_map/all_to_all | solution.py:408
  18.3 16.4 %all-to-all-start.1 = ((bf16[8,48,512]{2,1,0:T(8,128)(2,1)}), bf16[8,48,512]{2,1,0:T(8,128)(2,1)S(1)}, u32[]{:S(2)}, u32[]{:S(2)}) async-start(bf16[8,48,512]{2,1,0:T(8,128)(2,1)} %bitcast.8), calls=%async_computation.1 | async-start | bytes 786432 | tf_op jit(solution)/shard_map/all_to_all | solution.py:408
  23.5 11.1 %copy-start.10 = (bf16[512,512]{1,0:T(8,128)(2,1)S(1)}, bf16[512,512]{1,0:T(8,128)(2,1)}, u32[]{:S(2)}) copy-start(bf16[512,512]{1,0:T(8,128)(2,1)} %refs_8_.1) | copy-start | bytes 1572868
  23.5 11.1 %copy-start.11 = (bf16[512,512]{1,0:T(8,128)(2,1)S(1)}, bf16[512,512]{1,0:T(8,128)(2,1)}, u32[]{:S(2)}) copy-start(bf16[512,512]{1,0:T(8,128)(2,1)} %refs_1_.7) | copy-start | bytes 1572868
  23.5 11.1 %copy-start.22 = (f32[512]{0:T(512)S(1)}, f32[512]{0:T(512)}, u32[]{:S(2)}) copy-start(f32[512]{0:T(512)} %param.28) | copy-start | bytes 6148
  43.8 15.2 %all-to-all-start.2 = ((bf16[8,48,512]{2,1,0:T(8,128)(2,1)}), bf16[8,48,512]{2,1,0:T(8,128)(2,1)S(1)}, u32[]{:S(2)}, u32[]{:S(2)}) async-start(bf16[8,48,512]{2,1,0:T(8,128)(2,1)} %bitcast.11), calls=%async_computation.2 | async-start | bytes 786432 | tf_op jit(solution)/shard_map/all_to_all | solution.py:408
  48.6 18.9 %copy-start.13 = (bf16[8,48,512]{2,1,0:T(8,128)(2,1)S(1)}, bf16[8,48,512]{2,1,0:T(8,128)(2,1)}, u32[]{:S(2)}) copy-start(bf16[8,48,512]{2,1,0:T(8,128)(2,1)} %copy-done.12) | copy-start | bytes 1179652
  48.6 18.9 %copy-start.20 = (s32[4096]{0:T(1024)S(1)}, s32[4096]{0:T(1024)}, u32[]{:S(2)}) copy-start(s32[4096]{0:T(1024)} %param.20) | copy-start | bytes 49156
  48.6 18.9 %copy-start.23 = (bf16[384,512]{1,0:T(8,128)(2,1)S(1)}, bf16[384,512]{1,0:T(8,128)(2,1)}, u32[]{:S(2)}) copy-start(bf16[384,512]{1,0:T(8,128)(2,1)} %get-tuple-element.58.refs_2_) | copy-start | bytes 1179652
  62.8 14.7 %all-to-all-start.3 = ((bf16[8,48,512]{2,1,0:T(8,128)(2,1)}), bf16[8,48,512]{2,1,0:T(8,128)(2,1)S(1)}, u32[]{:S(2)}, u32[]{:S(2)}) async-start(bf16[8,48,512]{2,1,0:T(8,128)(2,1)} %bitcast.13), calls=%async_computation.3 | async-start | bytes 786432 | tf_op jit(solution)/shard_map/all_to_all | solution.py:408
  78.8 14.5 %all-to-all-start.4 = ((bf16[8,48,512]{2,1,0:T(8,128)(2,1)}), bf16[8,48,512]{2,1,0:T(8,128)(2,1)S(1)}, u32[]{:S(2)}, u32[]{:S(2)}) async-start(bf16[8,48,512]{2,1,0:T(8,128)(2,1)} %bitcast.35), calls=%async_computation.4 | async-start | bytes 786432 | tf_op jit(solution)/shard_map/all_to_all | solution.py:408
  92.6 12.5 %copy-start.14 = (bf16[320,512]{1,0:T(8,128)(2,1)S(1)}, bf16[320,512]{1,0:T(8,128)(2,1)}, u32[]{:S(2)}) copy-start(bf16[320,512]{1,0:T(8,128)(2,1)} %get-tuple-element.61.refs_2_) | copy-start | bytes 983044
  92.6 12.5 %copy-start.15 = (bf16[320,512]{1,0:T(8,128)(2,1)S(1)}, bf16[320,512]{1,0:T(8,128)(2,1)}, u32[]{:S(2)}) copy-start(bf16[320,512]{1,0:T(8,128)(2,1)} %get-tuple-element.62.refs_3_) | copy-start | bytes 983044
  94.0 11.2 %copy-start.1 = (bf16[8,48,512]{2,1,0:T(8,128)(2,1)S(1)}, bf16[8,48,512]{2,1,0:T(8,128)(2,1)}, u32[]{:S(2)}) copy-start(bf16[8,48,512]{2,1,0:T(8,128)(2,1)} %copy-done) | copy-start | bytes 1179652
  94.0 2.5 %collective-permute-start = (bf16[3,256,512]{2,1,0:T(8,128)(2,1)}, bf16[3,256,512]{2,1,0:T(8,128)(2,1)S(1)}, u32[]{:S(2)}, u32[]{:S(2)}) collective-permute-start(bf16[3,256,512]{2,1,0:T(8,128)(2,1)} %held.1), channel_id=1, source_target_pairs={{0,8},{8,0},{1,9},{9,1},{2,10},{10,2},{3,11},{11,3},{4,12},{12,4},... | collective-permute-start | bytes 2359304 | tf_op jit(solution)/shard_map/ppermute | solution.py:358
  98.7 27.1 %all-to-all-start.5 = ((bf16[16,48,512]{2,1,0:T(8,128)(2,1)}), bf16[16,48,512]{2,1,0:T(8,128)(2,1)S(1)}, u32[]{:S(2)}, u32[]{:S(2)}) async-start(bf16[16,48,512]{2,1,0:T(8,128)(2,1)} %parts.1.refs_9_), calls=%async_computation.5 | async-start | bytes 1572864 | tf_op jit(solution)/shard_map/all_to_all | solution.py:585
  150.6 2.3 %collective-permute-start.1 = (bf16[16,48,512]{2,1,0:T(8,128)(2,1)S(1)}, bf16[16,48,512]{2,1,0:T(8,128)(2,1)S(1)}, u32[]{:S(2)}, u32[]{:S(2)}) collective-permute-start(bf16[16,48,512]{2,1,0:T(8,128)(2,1)S(1)} %all_to_all.65.part_ref), channel_id=1, source_target_pairs={{0,8},{8,0},{1,9},{9,1},{2,10},{10,2},{3,11},{11,3},{4,12},{12,4},... | collective-permute-start | bytes 2359304 | tf_op jit(solution)/shard_map/ppermute | solution.py:358
  (9 other events, 49.2 us)

commit v6 on v5

--- a/solution.py
+++ b/solution.py
@@ -306,6 +306,10 @@
         put_halves(0, total[...].astype(BF16), keep_ref, give_ref)
         put_halves(1, dot(act_ref[...], gc_ref[...]).astype(BF16), keep_ref, give_ref)
         put_halves(2, dot(ml_ref[...], gsum_ref[...]).astype(BF16), keep_ref, give_ref)
+
+
+def stage_kernel(keep_ref, out_ref):
+    out_ref[...] = keep_ref[...]
 
 
 def parts_kernel(keep_ref, got_ref, out_ref):
@@ -433,7 +437,7 @@
             whole((1, width)),
         ],
         out_specs=[grid_spec],
-        after=[ids],
+        after=[slot],
         token=True,
     )
 
@@ -499,7 +503,7 @@
     )
     received = exchange(sums)
 
-    slope, slope_sums, slope_done = call(
+    slope, slope_sums = call(
         slope_kernel,
         "slope",
         [hbm((edge_dev, width), BF16), hbm((slots, width), F32)],
@@ -510,7 +514,6 @@
         out_specs=[edge_spec, slots_spec],
         vmem=60,
         after=[sums],
-        token=True,
     )
     g_asked, g_node, node_act = call(
         node_kernel,
@@ -527,7 +530,7 @@
             pltpu.SemaphoreType.DMA((4,)),
         ],
         vmem=52,
-        after=[slope_done],
+        after=[slope],
     )
     slot_g = exchange(g_asked)
 
@@ -575,11 +578,12 @@
     others = ("x", "mesh")
     count = lax.axis_size("x") * owners
     pieces = sds((count, 3 * half // count, width), BF16)
+    (staged,) = call(stage_kernel, "stage", [sds((3, half, width), BF16)], [keep], half * width)
     (parts,) = call(
         parts_kernel,
         "parts",
         [pieces],
-        [keep, other_core(held(give, [gsum_received]))],
+        [staged, other_core(held(give, [gsum_received]))],
         3 * half * width,
     )
     summed = lax.all_to_all(parts, others, 0, 0, tiled=True)

time: 155 us -> 154 us (level)
  waiting for transfers between devices: 27.5 us -> 24.7 us
  starting transfers between devices: 32.1 us -> 33.7 us
    unnamed x51 -> x47, local copies, waits for them, and re-layouts: 4.58 us -> 4.94 us
    pallas_call x14 -> x15, Pallas kernels: 61.8 us -> 61.8 us  [call(): pl.pallas_call(body, out_shape=out, in_specs=list(in_specs) + [pl.BlockSp...]
  transfers between devices with their start and end apart: 8 -> 8, of which waited for: 8 -> 7; matrix products, arithmetic and copies ran while one was open for 1% -> 1% of each run, Pallas kernels for 29% -> 29%
where the time goes in v6:
time: 154 us; the launch traced here: 153 us
  Pallas kernels  64.2 us (42%)
  starting transfers between devices  33.7 us (22%)
  waiting for transfers between devices  24.7 us (16%)
  blocking collectives  24.6 us (16%)
  local copies, waits for them, and re-layouts  5.02 us (3%)
    pallas_call x15, Pallas kernels, call(): pl.pallas_call(body, out_shape=out, in_specs=list(in_specs) + [pl.BlockSp...  61.8 us
    all_to_all x5, starting transfers between devices, exchange(): return lax.all_to_all(value, 'mesh', 0, 0, tiled=True)  26.7 us
    all_to_all x1, blocking collectives, shards(): mine = lax.all_to_all(copies, others, 0, 0, tiled=True)  24.6 us
    all_to_all x1, waiting for transfers between devices, shards(): summed = lax.all_to_all(parts, others, 0, 0, tiled=True)  17.7 us
    all_to_all x1, starting transfers between devices, shards(): summed = lax.all_to_all(parts, others, 0, 0, tiled=True)  7.01 us
    unnamed x47, local copies, waits for them, and re-layouts  4.94 us
    all_to_all x5, waiting for transfers between devices, exchange(): return lax.all_to_all(value, 'mesh', 0, 0, tiled=True)  4.67 us
  transfers between devices with their start and end apart: 8, of which 7 were waited for; matrix products, arithmetic and copies ran while one was open for 1% of the time, Pallas kernels for 29%

profile of v6, /device:TPU:0, one launch (start us, length us, event | category | flops | bytes accessed | tf_op | source)
XLA Modules:
  0.0 153.3 jit_solution(7505948103463714288)
XLA Ops:
  0.7 2.6 %prep.1 = (s32[32,128]{1,0:T(8,128)}, s32[8,128]{1,0:T(8,128)}) custom-call(s32[32,128]{1,0:T(8,128)} %bitcast.36), custom_call_target="tpu_custom_call" | custom-call | flops 1000000000 | bytes 36864 | tf_op jit(solution)/shard_map/prep/pallas_call | solution.py:67
  3.3 7.3 %all-to-all-start = ((s32[8,1,128]{2,1,0:T(1,128)}), s32[8,1,128]{2,1,0:T(1,128)S(1)}, u32[]{:S(2)}, u32[]{:S(2)}) async-start(s32[8,1,128]{2,1,0:T(1,128)} %bitcast.35), calls=%async_computation | async-start | bytes 8192 | tf_op jit(solution)/shard_map/all_to_all | solution.py:412
  10.6 1.2 copy.27.refs_0_
  12.6 2.2 %hidden.1 = (bf16[1024,512]{1,0:T(8,128)(2,1)}, s32[8,128]{1,0:T(8,128)S(1)}) custom-call(bf16[1024,227]{1,0:T(8,128)(2,1)S(1)} %copy.27.refs_0_, bf16[227,512]{1,0:T(8,128)(2,1)S(1)} %copy-done.17, f32[1,512]{1,0:T(1,128)S(1)} %bitcast.31, s32[32,128]{1,0:T(8,128)S(1)} %copy-done.21), custom_call_target="tpu_custom_call" | custom-call | flops 238026752 | bytes 1747968 | tf_op jit(solution)/shard_map/hidden/pallas_call | solution.py:67
  14.9 1.4 node_pre.1
  17.0 1.2 ask.1
  18.2 5.3 %all-to-all-start.1 = ((bf16[8,48,512]{2,1,0:T(8,128)(2,1)}), bf16[8,48,512]{2,1,0:T(8,128)(2,1)S(1)}, u32[]{:S(2)}, u32[]{:S(2)}) async-start(bf16[8,48,512]{2,1,0:T(8,128)(2,1)} %bitcast.8), calls=%async_computation.1 | async-start | bytes 786432 | tf_op jit(solution)/shard_map/all_to_all | solution.py:412
  23.6 9.7 %grid.1 = (bf16[512,1024]{1,0:T(8,128)(2,1)}, bf16[4096,512]{1,0:T(8,128)(2,1)}) custom-call(s32[32,128]{1,0:T(8,128)} %bitcast.29, bf16[1024,512]{1,0:T(8,128)(2,1)} %get-tuple-element.42.refs_1_, bf16[512,512]{1,0:T(8,128)(2,1)} %refs_2_.3, f32[1,512]{1,0:T(1,128)} %bitcast.37, bf16[512,512]{1,0:T(8,128)(2,1)} %refs_4_.4, ...), custom_call_target="tpu_custom_call" | custom-call | flops 5368709120 | bytes 7358464 | tf_op jit(solution)/shard_map/grid/pallas_call | solution.py:67
  33.3 1.3 all-to-all-done.1
  34.7 9.2 %edge.1 = (bf16[384,512]{1,0:T(8,128)(2,1)}, bf16[384,512]{1,0:T(8,128)(2,1)}, bf16[384,512]{1,0:T(8,128)(2,1)}) custom-call(s32[32,128]{1,0:T(8,128)S(1)} %copy-done.21, bf16[4096,512]{1,0:T(8,128)(2,1)} %get-tuple-element.47.refs_1_, bf16[384,512]{1,0:T(8,128)(2,1)S(1)} %bitcast.24, bf16[512,512]{1,0:T(8,128)(2,1)S(1)} %copy-done.10, ...), custom_call_target="tpu_custom_call" | custom-call | flops 3825205248 | bytes 6834176 | tf_op jit(solution)/shard_map/edge/pallas_call | solution.py:67
  43.9 4.6 %all-to-all-start.2 = ((bf16[8,48,512]{2,1,0:T(8,128)(2,1)}), bf16[8,48,512]{2,1,0:T(8,128)(2,1)S(1)}, u32[]{:S(2)}, u32[]{:S(2)}) async-start(bf16[8,48,512]{2,1,0:T(8,128)(2,1)} %bitcast.11), calls=%async_computation.2 | async-start | bytes 786432 | tf_op jit(solution)/shard_map/all_to_all | solution.py:412
  48.6 9.0 %slope.1 = (bf16[4096,512]{1,0:T(8,128)(2,1)}, f32[384,512]{1,0:T(8,128)}) custom-call(s32[32,128]{1,0:T(8,128)} %get-tuple-element.41.refs_3_.refs_0_, bf16[4096,512]{1,0:T(8,128)(2,1)} %get-tuple-element.47.refs_1_, bf16[384,512]{1,0:T(8,128)(2,1)} %get-tuple-element.52.refs_2_, f32[1,512]{1,0:T(1,128)} %bitcast.32, bf16[384,512]{1,0:T(8,128)(2,1)} %get-tuple-element.48.refs_4_), custom_call_target="tpu_custom_call" | custom-call | flops 3221225472 | bytes 9586688 | tf_op jit(solution)/shard_map/slope/pallas_call | solution.py:67
  57.7 1.4 all-to-all-done.2
  59.1 3.0 %node.1 = (bf16[384,512]{1,0:T(8,128)(2,1)}, bf16[320,512]{1,0:T(8,128)(2,1)}, bf16[320,512]{1,0:T(8,128)(2,1)}) custom-call(bf16[384,512]{1,0:T(8,128)(2,1)S(1)} %bitcast.21, s32[1,384]{1,0:T(1,128)S(1)} %reshape.47.refs_1_, bf16[384,320]{1,0:T(8,128)(2,1)S(1)} %get-tuple-element.49.refs_2_, f32[320,512]{1,0:T(8,128)} %get-tuple-element.50.refs_3_, ...), custom_call_target="tpu_custom_call" | custom-call | flops 587202560 | bytes 3524096 | tf_op jit(solution)/shard_map/node/pallas_call | solution.py:67
  62.1 4.7 %all-to-all-start.3 = ((bf16[8,48,512]{2,1,0:T(8,128)(2,1)}), bf16[8,48,512]{2,1,0:T(8,128)(2,1)S(1)}, u32[]{:S(2)}, u32[]{:S(2)}) async-start(bf16[8,48,512]{2,1,0:T(8,128)(2,1)} %bitcast.13), calls=%async_computation.3 | async-start | bytes 786432 | tf_op jit(solution)/shard_map/all_to_all | solution.py:412
  67.8 7.8 %take_latent.1 = (bf16[512,4096]{1,0:T(8,128)(2,1)}, bf16[512,384]{1,0:T(8,128)(2,1)}, bf16[512,384]{1,0:T(8,128)(2,1)}, s32[8,128]{1,0:T(8,128)S(1)}) custom-call(s32[32,128]{1,0:T(8,128)S(1)} %bitcast.30, bf16[512,1024]{1,0:T(8,128)(2,1)} %get-tuple-element.56.refs_1_, bf16[384,512]{1,0:T(8,128)(2,1)S(1)} %copy-done.22, bf16[384,512]{1,0:T(8,128)(2,1)S(1)} %bitcast.25, ...), custom_call_target="tpu_custom_call" | custom-call | flops 4294967296 | bytes 6832128 | tf_op jit(solution)/shard_map/take_latent/pallas_call | solution.py:67
  76.8 1.3 slot_grad.1
  78.1 4.8 %all-to-all-start.4 = ((bf16[8,48,512]{2,1,0:T(8,128)(2,1)}), bf16[8,48,512]{2,1,0:T(8,128)(2,1)S(1)}, u32[]{:S(2)}, u32[]{:S(2)}) async-start(bf16[8,48,512]{2,1,0:T(8,128)(2,1)} %bitcast.34), calls=%async_computation.4 | async-start | bytes 786432 | tf_op jit(solution)/shard_map/all_to_all | solution.py:412
  82.9 10.0 %edge_back.1 = (bf16[3,256,512]{2,1,0:T(8,128)(2,1)}, bf16[3,256,512]{2,1,0:T(8,128)(2,1)}) custom-call(s32[32,128]{1,0:T(8,128)} %get-tuple-element.41.refs_3_.refs_0_, bf16[4096,512]{1,0:T(8,128)(2,1)} %get-tuple-element.53.refs_6_.refs_1_, bf16[512,4096]{1,0:T(8,128)(2,1)} %get-tuple-element.62.refs_2_, bf16[384,512]{1,0:T(8,128)(2,1)} %get-tuple-element.63.refs_3_, ...), custom_call_target="tpu_custom_call" | custom-call | flops 4160749568 | bytes 11943936 | tf_op jit(solution)/shard_map/edge_back/pallas_call | solution.py:67
  94.9 1.3 collective-permute-done.refs_1_
  97.2 7.0 %all-to-all-start.5 = ((bf16[16,48,512]{2,1,0:T(8,128)(2,1)}), bf16[16,48,512]{2,1,0:T(8,128)(2,1)S(1)}, u32[]{:S(2)}, u32[]{:S(2)}) async-start(bf16[16,48,512]{2,1,0:T(8,128)(2,1)} %parts.1.refs_9_), calls=%async_computation.5 | async-start | bytes 1572864 | tf_op jit(solution)/shard_map/all_to_all | solution.py:589
  104.2 2.9 %node_post.1 = (bf16[320,512]{1,0:T(8,128)(2,1)}, bf16[320,512]{1,0:T(8,128)(2,1)}, s32[8,128]{1,0:T(8,128)S(1)}) custom-call(bf16[384,512]{1,0:T(8,128)(2,1)S(1)} %bitcast.20, s32[1,384]{1,0:T(1,128)S(1)} %reshape.47.refs_1_, bf16[320,512]{1,0:T(8,128)(2,1)S(1)} %copy-done.14, bf16[320,512]{1,0:T(8,128)(2,1)S(1)} %copy-done.15, ...), custom_call_target="tpu_custom_call" | custom-call | flops 629145600 | bytes 3933696 | tf_op jit(solution)/shard_map/node_post/pallas_call | solution.py:67
  107.2 17.7 %all-to-all-done.5.refs_0_ = bf16[16,48,512]{2,1,0:T(8,128)(2,1)S(1)} async-done(((bf16[16,48,512]{2,1,0:T(8,128)(2,1)}), bf16[16,48,512]{2,1,0:T(8,128)(2,1)S(1)}, u32[]{:S(2)}, u32[]{:S(2)}) %all-to-all-start.5) | async-done | bytes 786464 | tf_op jit(solution)/shard_map/all_to_all | solution.py:589
  125.0 24.6 %all_to_all.65.part_ref = bf16[16,48,512]{2,1,0:T(8,128)(2,1)S(1)} all-to-all(bf16[16,48,512]{2,1,0:T(8,128)(2,1)S(1)} %spread.1), channel_id=1, replica_groups=mesh['x'=2,'core'=2,'mesh'=8] {'x','mesh'}, dimensions={0} | all-to-all | bytes 1572864 | tf_op jit(solution)/shard_map/all_to_all | solution.py:612
  (59 shorter events, 10.4 us)
Async XLA Ops:
  0.6 11.2 %copy-start.19 = (f32[512]{0:T(512)S(1)}, f32[512]{0:T(512)}, u32[]{:S(2)}) copy-start(f32[512]{0:T(512)} %param.23) | copy-start | bytes 6148
  0.6 11.2 %copy-start.17 = (bf16[227,512]{1,0:T(8,128)(2,1)S(1)}, bf16[227,512]{1,0:T(8,128)(2,1)}, u32[]{:S(2)}) copy-start(bf16[227,512]{1,0:T(8,128)(2,1)} %refs_1_.4) | copy-start | bytes 697348
  0.7 14.2 %copy-start.16 = (f32[512]{0:T(512)S(1)}, f32[512]{0:T(512)}, u32[]{:S(2)}) copy-start(f32[512]{0:T(512)} %param.32) | copy-start | bytes 6148
  0.7 14.2 %copy-start.5 = (bf16[320,512]{1,0:T(8,128)(2,1)S(1)}, bf16[320,512]{1,0:T(8,128)(2,1)}, u32[]{:S(2)}) copy-start(bf16[320,512]{1,0:T(8,128)(2,1)} %refs_4_.5) | copy-start | bytes 983044
  0.7 14.2 %copy-start.6 = (bf16[320,512]{1,0:T(8,128)(2,1)S(1)}, bf16[320,512]{1,0:T(8,128)(2,1)}, u32[]{:S(2)}) copy-start(bf16[320,512]{1,0:T(8,128)(2,1)} %refs_5_.5) | copy-start | bytes 983044
  0.7 14.2 %copy-start.2 = (bf16[512,512]{1,0:T(8,128)(2,1)S(1)}, bf16[512,512]{1,0:T(8,128)(2,1)}, u32[]{:S(2)}) copy-start(bf16[512,512]{1,0:T(8,128)(2,1)} %refs_7_.1) | copy-start | bytes 1572868
  0.7 14.2 %copy-start.3 = (bf16[512,512]{1,0:T(8,128)(2,1)S(1)}, bf16[512,512]{1,0:T(8,128)(2,1)}, u32[]{:S(2)}) copy-start(bf16[512,512]{1,0:T(8,128)(2,1)} %refs_6_.1) | copy-start | bytes 1572868
  3.3 13.7 %all-to-all-start = ((s32[8,1,128]{2,1,0:T(1,128)}), s32[8,1,128]{2,1,0:T(1,128)S(1)}, u32[]{:S(2)}, u32[]{:S(2)}) async-start(s32[8,1,128]{2,1,0:T(1,128)} %bitcast.35), calls=%async_computation | async-start | bytes 8192 | tf_op jit(solution)/shard_map/all_to_all | solution.py:412
  18.2 16.4 %all-to-all-start.1 = ((bf16[8,48,512]{2,1,0:T(8,128)(2,1)}), bf16[8,48,512]{2,1,0:T(8,128)(2,1)S(1)}, u32[]{:S(2)}, u32[]{:S(2)}) async-start(bf16[8,48,512]{2,1,0:T(8,128)(2,1)} %bitcast.8), calls=%async_computation.1 | async-start | bytes 786432 | tf_op jit(solution)/shard_map/all_to_all | solution.py:412
  23.5 11.1 %copy-start.10 = (bf16[512,512]{1,0:T(8,128)(2,1)S(1)}, bf16[512,512]{1,0:T(8,128)(2,1)}, u32[]{:S(2)}) copy-start(bf16[512,512]{1,0:T(8,128)(2,1)} %refs_8_.1) | copy-start | bytes 1572868
  23.5 11.1 %copy-start.11 = (bf16[512,512]{1,0:T(8,128)(2,1)S(1)}, bf16[512,512]{1,0:T(8,128)(2,1)}, u32[]{:S(2)}) copy-start(bf16[512,512]{1,0:T(8,128)(2,1)} %refs_1_.7) | copy-start | bytes 1572868
  23.6 11.1 %copy-start.20 = (f32[512]{0:T(512)S(1)}, f32[512]{0:T(512)}, u32[]{:S(2)}) copy-start(f32[512]{0:T(512)} %param.28) | copy-start | bytes 6148
  34.6 9.2 %copy-start.12 = (bf16[8,48,512]{2,1,0:T(8,128)(2,1)}, bf16[8,48,512]{2,1,0:T(8,128)(2,1)S(1)}, u32[]{:S(2)}) copy-start(bf16[8,48,512]{2,1,0:T(8,128)(2,1)S(1)} %all-to-all-done.1) | copy-start | bytes 1179652
  43.9 15.2 %all-to-all-start.2 = ((bf16[8,48,512]{2,1,0:T(8,128)(2,1)}), bf16[8,48,512]{2,1,0:T(8,128)(2,1)S(1)}, u32[]{:S(2)}, u32[]{:S(2)}) async-start(bf16[8,48,512]{2,1,0:T(8,128)(2,1)} %bitcast.11), calls=%async_computation.2 | async-start | bytes 786432 | tf_op jit(solution)/shard_map/all_to_all | solution.py:412
  48.6 10.5 %copy-start.9 = (bf16[512,512]{1,0:T(8,128)(2,1)S(1)}, bf16[512,512]{1,0:T(8,128)(2,1)}, u32[]{:S(2)}) copy-start(bf16[512,512]{1,0:T(8,128)(2,1)} %refs_5_.4) | copy-start | bytes 1572868
  57.7 9.1 %copy-start.18 = (s32[4096]{0:T(1024)S(1)}, s32[4096]{0:T(1024)}, u32[]{:S(2)}) copy-start(s32[4096]{0:T(1024)} %param.20) | copy-start | bytes 49156
  62.1 14.7 %all-to-all-start.3 = ((bf16[8,48,512]{2,1,0:T(8,128)(2,1)}), bf16[8,48,512]{2,1,0:T(8,128)(2,1)S(1)}, u32[]{:S(2)}, u32[]{:S(2)}) async-start(bf16[8,48,512]{2,1,0:T(8,128)(2,1)} %bitcast.13), calls=%async_computation.3 | async-start | bytes 786432 | tf_op jit(solution)/shard_map/all_to_all | solution.py:412
  78.1 14.8 %all-to-all-start.4 = ((bf16[8,48,512]{2,1,0:T(8,128)(2,1)}), bf16[8,48,512]{2,1,0:T(8,128)(2,1)S(1)}, u32[]{:S(2)}, u32[]{:S(2)}) async-start(bf16[8,48,512]{2,1,0:T(8,128)(2,1)} %bitcast.34), calls=%async_computation.4 | async-start | bytes 786432 | tf_op jit(solution)/shard_map/all_to_all | solution.py:412
  92.9 11.4 %copy-start.14 = (bf16[320,512]{1,0:T(8,128)(2,1)S(1)}, bf16[320,512]{1,0:T(8,128)(2,1)}, u32[]{:S(2)}) copy-start(bf16[320,512]{1,0:T(8,128)(2,1)} %get-tuple-element.60.refs_2_) | copy-start | bytes 983044
  92.9 11.4 %copy-start.15 = (bf16[320,512]{1,0:T(8,128)(2,1)S(1)}, bf16[320,512]{1,0:T(8,128)(2,1)}, u32[]{:S(2)}) copy-start(bf16[320,512]{1,0:T(8,128)(2,1)} %get-tuple-element.61.refs_3_) | copy-start | bytes 983044
  93.6 10.6 %copy-start.1 = (bf16[8,48,512]{2,1,0:T(8,128)(2,1)S(1)}, bf16[8,48,512]{2,1,0:T(8,128)(2,1)}, u32[]{:S(2)}) copy-start(bf16[8,48,512]{2,1,0:T(8,128)(2,1)} %copy-done) | copy-start | bytes 1179652
  93.6 2.5 %collective-permute-start = (bf16[3,256,512]{2,1,0:T(8,128)(2,1)}, bf16[3,256,512]{2,1,0:T(8,128)(2,1)S(1)}, u32[]{:S(2)}, u32[]{:S(2)}) collective-permute-start(bf16[3,256,512]{2,1,0:T(8,128)(2,1)} %held.1), channel_id=1, source_target_pairs={{0,8},{8,0},{1,9},{9,1},{2,10},{10,2},{3,11},{11,3},{4,12},{12,4},... | collective-permute-start | bytes 2359304 | tf_op jit(solution)/shard_map/ppermute | solution.py:362
  97.2 27.7 %all-to-all-start.5 = ((bf16[16,48,512]{2,1,0:T(8,128)(2,1)}), bf16[16,48,512]{2,1,0:T(8,128)(2,1)S(1)}, u32[]{:S(2)}, u32[]{:S(2)}) async-start(bf16[16,48,512]{2,1,0:T(8,128)(2,1)} %parts.1.refs_9_), calls=%async_computation.5 | async-start | bytes 1572864 | tf_op jit(solution)/shard_map/all_to_all | solution.py:589
  149.7 2.3 %collective-permute-start.1 = (bf16[16,48,512]{2,1,0:T(8,128)(2,1)S(1)}, bf16[16,48,512]{2,1,0:T(8,128)(2,1)S(1)}, u32[]{:S(2)}, u32[]{:S(2)}) collective-permute-start(bf16[16,48,512]{2,1,0:T(8,128)(2,1)S(1)} %all_to_all.65.part_ref), channel_id=1, source_target_pairs={{0,8},{8,0},{1,9},{9,1},{2,10},{10,2},{3,11},{11,3},{4,12},{12,4},... | collective-permute-start | bytes 2359304 | tf_op jit(solution)/shard_map/ppermute | solution.py:362
  (7 other events, 27.9 us)

commit v7 on v6

--- a/solution.py
+++ b/solution.py
@@ -284,12 +284,19 @@
 
 
 def edge_back_kernel(
-    steps, slot_ref, slope_ref, lat_t_ref, h_ref, gsum_hbm, ml_hbm, gc_hbm, act_hbm, keep_ref, give_ref,
-    total, gsum_ref, ml_ref, gc_ref, act_ref, sems,
+    steps, slot_ref, slope_ref, lat_t_ref, h_ref, gsum_hbm, ml_hbm, gc_hbm, act_hbm, keep_hbm, give_hbm,
+    total, gsum_ref, ml_ref, gc_ref, act_ref, keep_ref, give_ref, sems, out_sems,
 ):
     step = pl.program_id(0)
     late = [(act_hbm, act_ref), (gc_hbm, gc_ref), (ml_hbm, ml_ref), (gsum_hbm, gsum_ref)]
 
+    def leaving(which):
+        rows = pl.ds(1, 2) if which else pl.ds(0, 1)
+        return [
+            pltpu.make_async_copy(keep_ref.at[rows], keep_hbm.at[rows], out_sems.at[2 * which]),
+            pltpu.make_async_copy(give_ref.at[rows], give_hbm.at[rows], out_sems.at[2 * which + 1]),
+        ]
+
     @pl.when(step == 0)
     def _():
         total[...] = jnp.zeros_like(total)
@@ -299,13 +306,22 @@
     g_edge = (dot(onehot, h_ref[...]) * slope_ref[...].astype(F32)).astype(BF16)
     total[...] += dot(lat_t_ref[...], g_edge)
 
-    @pl.when(step == steps - 1)
+    @pl.when(step == max(steps - 2, 0))
     def _():
         for i, (a, b) in enumerate(late):
             pltpu.make_async_copy(a, b, sems.at[i]).wait()
-        put_halves(0, total[...].astype(BF16), keep_ref, give_ref)
         put_halves(1, dot(act_ref[...], gc_ref[...]).astype(BF16), keep_ref, give_ref)
         put_halves(2, dot(ml_ref[...], gsum_ref[...]).astype(BF16), keep_ref, give_ref)
+        for copy in leaving(1):
+            copy.start()
+
+    @pl.when(step == steps - 1)
+    def _():
+        put_halves(0, total[...].astype(BF16), keep_ref, give_ref)
+        for copy in leaving(0):
+            copy.start()
+        for copy in leaving(1) + leaving(0):
+            copy.wait()
 
 
 def stage_kernel(keep_ref, out_ref):
@@ -569,10 +585,11 @@
         2 * edge_dev * (slots + width) * width + 4 * slots * width * width,
         grid=(steps,),
         in_specs=[id_spec, edge_spec, edge_t_spec, slots_spec] + [pl.BlockSpec(memory_space=pl.ANY)] * 4,
-        out_specs=[whole(three.shape), whole(three.shape)],
+        out_specs=[pl.BlockSpec(memory_space=pl.ANY)] * 2,
         scratch=[pltpu.VMEM((width, width), F32)]
         + [pltpu.VMEM(a, BF16) for a in ((slots, width), (width, slots)) * 2]
-        + [pltpu.SemaphoreType.DMA((4,))],
+        + [pltpu.VMEM((3, half, width), BF16)] * 2
+        + [pltpu.SemaphoreType.DMA((4,))] * 2,
         vmem=60,
     )
     others = ("x", "mesh")

time: 154 us -> 154 us (level)
  no operation moved by 1% of the time
where the time goes in v7:
time: 154 us; the launch traced here: 153 us
  Pallas kernels  63.8 us (41%)
  starting transfers between devices  33.7 us (22%)
  waiting for transfers between devices  24.7 us (16%)
  blocking collectives  24.6 us (16%)
  local copies, waits for them, and re-layouts  5.02 us (3%)
    pallas_call x15, Pallas kernels, call(): pl.pallas_call(body, out_shape=out, in_specs=list(in_specs) + [pl.BlockSp...  61.5 us
    all_to_all x5, starting transfers between devices, exchange(): return lax.all_to_all(value, 'mesh', 0, 0, tiled=True)  26.7 us
    all_to_all x1, blocking collectives, shards(): mine = lax.all_to_all(copies, others, 0, 0, tiled=True)  24.6 us
    all_to_all x1, waiting for transfers between devices, shards(): summed = lax.all_to_all(parts, others, 0, 0, tiled=True)  17.7 us
    all_to_all x1, starting transfers between devices, shards(): summed = lax.all_to_all(parts, others, 0, 0, tiled=True)  7.02 us
    unnamed x47, local copies, waits for them, and re-layouts  4.94 us
    all_to_all x5, waiting for transfers between devices, exchange(): return lax.all_to_all(value, 'mesh', 0, 0, tiled=True)  4.68 us
  transfers between devices with their start and end apart: 8, of which 7 were waited for; matrix products, arithmetic and copies ran while one was open for 1% of the time, Pallas kernels for 29%

profile of v7, /device:TPU:0, one launch (start us, length us, event | category | flops | bytes accessed | tf_op | source)
XLA Modules:
  0.0 153.0 jit_solution(10685684558015758878)
XLA Ops:
  0.7 2.6 %prep.1 = (s32[32,128]{1,0:T(8,128)}, s32[8,128]{1,0:T(8,128)}) custom-call(s32[32,128]{1,0:T(8,128)} %bitcast.36), custom_call_target="tpu_custom_call" | custom-call | flops 1000000000 | bytes 36864 | tf_op jit(solution)/shard_map/prep/pallas_call | solution.py:67
  3.3 7.3 %all-to-all-start = ((s32[8,1,128]{2,1,0:T(1,128)}), s32[8,1,128]{2,1,0:T(1,128)S(1)}, u32[]{:S(2)}, u32[]{:S(2)}) async-start(s32[8,1,128]{2,1,0:T(1,128)} %bitcast.35), calls=%async_computation | async-start | bytes 8192 | tf_op jit(solution)/shard_map/all_to_all | solution.py:428
  10.6 1.2 copy.27.refs_0_
  12.6 2.2 %hidden.1 = (bf16[1024,512]{1,0:T(8,128)(2,1)}, s32[8,128]{1,0:T(8,128)S(1)}) custom-call(bf16[1024,227]{1,0:T(8,128)(2,1)S(1)} %copy.27.refs_0_, bf16[227,512]{1,0:T(8,128)(2,1)S(1)} %copy-done.17, f32[1,512]{1,0:T(1,128)S(1)} %bitcast.31, s32[32,128]{1,0:T(8,128)S(1)} %copy-done.21), custom_call_target="tpu_custom_call" | custom-call | flops 238026752 | bytes 1747968 | tf_op jit(solution)/shard_map/hidden/pallas_call | solution.py:67
  14.9 1.4 node_pre.1
  17.0 1.2 ask.1
  18.2 5.3 %all-to-all-start.1 = ((bf16[8,48,512]{2,1,0:T(8,128)(2,1)}), bf16[8,48,512]{2,1,0:T(8,128)(2,1)S(1)}, u32[]{:S(2)}, u32[]{:S(2)}) async-start(bf16[8,48,512]{2,1,0:T(8,128)(2,1)} %bitcast.8), calls=%async_computation.1 | async-start | bytes 786432 | tf_op jit(solution)/shard_map/all_to_all | solution.py:428
  23.6 9.7 %grid.1 = (bf16[512,1024]{1,0:T(8,128)(2,1)}, bf16[4096,512]{1,0:T(8,128)(2,1)}) custom-call(s32[32,128]{1,0:T(8,128)} %bitcast.29, bf16[1024,512]{1,0:T(8,128)(2,1)} %get-tuple-element.42.refs_1_, bf16[512,512]{1,0:T(8,128)(2,1)} %refs_2_.3, f32[1,512]{1,0:T(1,128)} %bitcast.37, bf16[512,512]{1,0:T(8,128)(2,1)} %refs_4_.4, ...), custom_call_target="tpu_custom_call" | custom-call | flops 5368709120 | bytes 7358464 | tf_op jit(solution)/shard_map/grid/pallas_call | solution.py:67
  33.3 1.3 all-to-all-done.1
  34.7 9.2 %edge.1 = (bf16[384,512]{1,0:T(8,128)(2,1)}, bf16[384,512]{1,0:T(8,128)(2,1)}, bf16[384,512]{1,0:T(8,128)(2,1)}) custom-call(s32[32,128]{1,0:T(8,128)S(1)} %copy-done.21, bf16[4096,512]{1,0:T(8,128)(2,1)} %get-tuple-element.47.refs_1_, bf16[384,512]{1,0:T(8,128)(2,1)S(1)} %bitcast.24, bf16[512,512]{1,0:T(8,128)(2,1)S(1)} %copy-done.10, ...), custom_call_target="tpu_custom_call" | custom-call | flops 3825205248 | bytes 6834176 | tf_op jit(solution)/shard_map/edge/pallas_call | solution.py:67
  43.9 4.6 %all-to-all-start.2 = ((bf16[8,48,512]{2,1,0:T(8,128)(2,1)}), bf16[8,48,512]{2,1,0:T(8,128)(2,1)S(1)}, u32[]{:S(2)}, u32[]{:S(2)}) async-start(bf16[8,48,512]{2,1,0:T(8,128)(2,1)} %bitcast.11), calls=%async_computation.2 | async-start | bytes 786432 | tf_op jit(solution)/shard_map/all_to_all | solution.py:428
  48.6 9.0 %slope.1 = (bf16[4096,512]{1,0:T(8,128)(2,1)}, f32[384,512]{1,0:T(8,128)}) custom-call(s32[32,128]{1,0:T(8,128)} %get-tuple-element.41.refs_3_.refs_0_, bf16[4096,512]{1,0:T(8,128)(2,1)} %get-tuple-element.47.refs_1_, bf16[384,512]{1,0:T(8,128)(2,1)} %get-tuple-element.52.refs_2_, f32[1,512]{1,0:T(1,128)} %bitcast.32, bf16[384,512]{1,0:T(8,128)(2,1)} %get-tuple-element.48.refs_4_), custom_call_target="tpu_custom_call" | custom-call | flops 3221225472 | bytes 9586688 | tf_op jit(solution)/shard_map/slope/pallas_call | solution.py:67
  57.7 1.4 all-to-all-done.2
  59.1 3.0 %node.1 = (bf16[384,512]{1,0:T(8,128)(2,1)}, bf16[320,512]{1,0:T(8,128)(2,1)}, bf16[320,512]{1,0:T(8,128)(2,1)}) custom-call(bf16[384,512]{1,0:T(8,128)(2,1)S(1)} %bitcast.21, s32[1,384]{1,0:T(1,128)S(1)} %reshape.47.refs_1_, bf16[384,320]{1,0:T(8,128)(2,1)S(1)} %get-tuple-element.49.refs_2_, f32[320,512]{1,0:T(8,128)} %get-tuple-element.50.refs_3_, ...), custom_call_target="tpu_custom_call" | custom-call | flops 587202560 | bytes 3524096 | tf_op jit(solution)/shard_map/node/pallas_call | solution.py:67
  62.1 4.7 %all-to-all-start.3 = ((bf16[8,48,512]{2,1,0:T(8,128)(2,1)}), bf16[8,48,512]{2,1,0:T(8,128)(2,1)S(1)}, u32[]{:S(2)}, u32[]{:S(2)}) async-start(bf16[8,48,512]{2,1,0:T(8,128)(2,1)} %bitcast.13), calls=%async_computation.3 | async-start | bytes 786432 | tf_op jit(solution)/shard_map/all_to_all | solution.py:428
  67.8 7.8 %take_latent.1 = (bf16[512,4096]{1,0:T(8,128)(2,1)}, bf16[512,384]{1,0:T(8,128)(2,1)}, bf16[512,384]{1,0:T(8,128)(2,1)}, s32[8,128]{1,0:T(8,128)S(1)}) custom-call(s32[32,128]{1,0:T(8,128)S(1)} %bitcast.30, bf16[512,1024]{1,0:T(8,128)(2,1)} %get-tuple-element.56.refs_1_, bf16[384,512]{1,0:T(8,128)(2,1)S(1)} %copy-done.22, bf16[384,512]{1,0:T(8,128)(2,1)S(1)} %bitcast.25, ...), custom_call_target="tpu_custom_call" | custom-call | flops 4294967296 | bytes 6832128 | tf_op jit(solution)/shard_map/take_latent/pallas_call | solution.py:67
  76.8 1.3 slot_grad.1
  78.1 4.8 %all-to-all-start.4 = ((bf16[8,48,512]{2,1,0:T(8,128)(2,1)}), bf16[8,48,512]{2,1,0:T(8,128)(2,1)S(1)}, u32[]{:S(2)}, u32[]{:S(2)}) async-start(bf16[8,48,512]{2,1,0:T(8,128)(2,1)} %bitcast.34), calls=%async_computation.4 | async-start | bytes 786432 | tf_op jit(solution)/shard_map/all_to_all | solution.py:428
  82.9 9.6 %edge_back.1 = (bf16[3,256,512]{2,1,0:T(8,128)(2,1)}, bf16[3,256,512]{2,1,0:T(8,128)(2,1)}) custom-call(s32[32,128]{1,0:T(8,128)} %get-tuple-element.41.refs_3_.refs_0_, bf16[4096,512]{1,0:T(8,128)(2,1)} %get-tuple-element.53.refs_6_.refs_1_, bf16[512,4096]{1,0:T(8,128)(2,1)} %get-tuple-element.62.refs_2_, bf16[384,512]{1,0:T(8,128)(2,1)} %get-tuple-element.63.refs_3_, ...), custom_call_target="tpu_custom_call" | custom-call | flops 4160749568 | bytes 11943936 | tf_op jit(solution)/shard_map/edge_back/pallas_call | solution.py:67
  94.6 1.3 collective-permute-done.refs_1_
  96.9 7.0 %all-to-all-start.5 = ((bf16[16,48,512]{2,1,0:T(8,128)(2,1)}), bf16[16,48,512]{2,1,0:T(8,128)(2,1)S(1)}, u32[]{:S(2)}, u32[]{:S(2)}) async-start(bf16[16,48,512]{2,1,0:T(8,128)(2,1)} %parts.1.refs_9_), calls=%async_computation.5 | async-start | bytes 1572864 | tf_op jit(solution)/shard_map/all_to_all | solution.py:606
  103.9 2.9 %node_post.1 = (bf16[320,512]{1,0:T(8,128)(2,1)}, bf16[320,512]{1,0:T(8,128)(2,1)}, s32[8,128]{1,0:T(8,128)S(1)}) custom-call(bf16[384,512]{1,0:T(8,128)(2,1)S(1)} %bitcast.20, s32[1,384]{1,0:T(1,128)S(1)} %reshape.47.refs_1_, bf16[320,512]{1,0:T(8,128)(2,1)S(1)} %copy-done.14, bf16[320,512]{1,0:T(8,128)(2,1)S(1)} %copy-done.15, ...), custom_call_target="tpu_custom_call" | custom-call | flops 629145600 | bytes 3933696 | tf_op jit(solution)/shard_map/node_post/pallas_call | solution.py:67
  106.9 17.7 %all-to-all-done.5.refs_0_ = bf16[16,48,512]{2,1,0:T(8,128)(2,1)S(1)} async-done(((bf16[16,48,512]{2,1,0:T(8,128)(2,1)}), bf16[16,48,512]{2,1,0:T(8,128)(2,1)S(1)}, u32[]{:S(2)}, u32[]{:S(2)}) %all-to-all-start.5) | async-done | bytes 786464 | tf_op jit(solution)/shard_map/all_to_all | solution.py:606
  124.7 24.6 %all_to_all.65.part_ref = bf16[16,48,512]{2,1,0:T(8,128)(2,1)S(1)} all-to-all(bf16[16,48,512]{2,1,0:T(8,128)(2,1)S(1)} %spread.1), channel_id=1, replica_groups=mesh['x'=2,'core'=2,'mesh'=8] {'x','mesh'}, dimensions={0} | all-to-all | bytes 1572864 | tf_op jit(solution)/shard_map/all_to_all | solution.py:629
  (59 shorter events, 10.4 us)
Async XLA Ops:
  0.6 11.2 %copy-start.19 = (f32[512]{0:T(512)S(1)}, f32[512]{0:T(512)}, u32[]{:S(2)}) copy-start(f32[512]{0:T(512)} %param.23) | copy-start | bytes 6148
  0.6 11.2 %copy-start.17 = (bf16[227,512]{1,0:T(8,128)(2,1)S(1)}, bf16[227,512]{1,0:T(8,128)(2,1)}, u32[]{:S(2)}) copy-start(bf16[227,512]{1,0:T(8,128)(2,1)} %refs_1_.4) | copy-start | bytes 697348
  0.7 14.2 %copy-start.16 = (f32[512]{0:T(512)S(1)}, f32[512]{0:T(512)}, u32[]{:S(2)}) copy-start(f32[512]{0:T(512)} %param.32) | copy-start | bytes 6148
  0.7 14.2 %copy-start.5 = (bf16[320,512]{1,0:T(8,128)(2,1)S(1)}, bf16[320,512]{1,0:T(8,128)(2,1)}, u32[]{:S(2)}) copy-start(bf16[320,512]{1,0:T(8,128)(2,1)} %refs_4_.5) | copy-start | bytes 983044
  0.7 14.2 %copy-start.6 = (bf16[320,512]{1,0:T(8,128)(2,1)S(1)}, bf16[320,512]{1,0:T(8,128)(2,1)}, u32[]{:S(2)}) copy-start(bf16[320,512]{1,0:T(8,128)(2,1)} %refs_5_.5) | copy-start | bytes 983044
  0.7 14.2 %copy-start.2 = (bf16[512,512]{1,0:T(8,128)(2,1)S(1)}, bf16[512,512]{1,0:T(8,128)(2,1)}, u32[]{:S(2)}) copy-start(bf16[512,512]{1,0:T(8,128)(2,1)} %refs_7_.1) | copy-start | bytes 1572868
  0.7 14.2 %copy-start.3 = (bf16[512,512]{1,0:T(8,128)(2,1)S(1)}, bf16[512,512]{1,0:T(8,128)(2,1)}, u32[]{:S(2)}) copy-start(bf16[512,512]{1,0:T(8,128)(2,1)} %refs_6_.1) | copy-start | bytes 1572868
  3.3 13.7 %all-to-all-start = ((s32[8,1,128]{2,1,0:T(1,128)}), s32[8,1,128]{2,1,0:T(1,128)S(1)}, u32[]{:S(2)}, u32[]{:S(2)}) async-start(s32[8,1,128]{2,1,0:T(1,128)} %bitcast.35), calls=%async_computation | async-start | bytes 8192 | tf_op jit(solution)/shard_map/all_to_all | solution.py:428
  18.2 16.4 %all-to-all-start.1 = ((bf16[8,48,512]{2,1,0:T(8,128)(2,1)}), bf16[8,48,512]{2,1,0:T(8,128)(2,1)S(1)}, u32[]{:S(2)}, u32[]{:S(2)}) async-start(bf16[8,48,512]{2,1,0:T(8,128)(2,1)} %bitcast.8), calls=%async_computation.1 | async-start | bytes 786432 | tf_op jit(solution)/shard_map/all_to_all | solution.py:428
  23.5 11.1 %copy-start.10 = (bf16[512,512]{1,0:T(8,128)(2,1)S(1)}, bf16[512,512]{1,0:T(8,128)(2,1)}, u32[]{:S(2)}) copy-start(bf16[512,512]{1,0:T(8,128)(2,1)} %refs_8_.1) | copy-start | bytes 1572868
  23.5 11.1 %copy-start.11 = (bf16[512,512]{1,0:T(8,128)(2,1)S(1)}, bf16[512,512]{1,0:T(8,128)(2,1)}, u32[]{:S(2)}) copy-start(bf16[512,512]{1,0:T(8,128)(2,1)} %refs_1_.7) | copy-start | bytes 1572868
  23.6 11.1 %copy-start.20 = (f32[512]{0:T(512)S(1)}, f32[512]{0:T(512)}, u32[]{:S(2)}) copy-start(f32[512]{0:T(512)} %param.28) | copy-start | bytes 6148
  34.6 9.2 %copy-start.12 = (bf16[8,48,512]{2,1,0:T(8,128)(2,1)}, bf16[8,48,512]{2,1,0:T(8,128)(2,1)S(1)}, u32[]{:S(2)}) copy-start(bf16[8,48,512]{2,1,0:T(8,128)(2,1)S(1)} %all-to-all-done.1) | copy-start | bytes 1179652
  43.9 15.2 %all-to-all-start.2 = ((bf16[8,48,512]{2,1,0:T(8,128)(2,1)}), bf16[8,48,512]{2,1,0:T(8,128)(2,1)S(1)}, u32[]{:S(2)}, u32[]{:S(2)}) async-start(bf16[8,48,512]{2,1,0:T(8,128)(2,1)} %bitcast.11), calls=%async_computation.2 | async-start | bytes 786432 | tf_op jit(solution)/shard_map/all_to_all | solution.py:428
  48.6 10.5 %copy-start.9 = (bf16[512,512]{1,0:T(8,128)(2,1)S(1)}, bf16[512,512]{1,0:T(8,128)(2,1)}, u32[]{:S(2)}) copy-start(bf16[512,512]{1,0:T(8,128)(2,1)} %refs_5_.4) | copy-start | bytes 1572868
  57.7 9.1 %copy-start.18 = (s32[4096]{0:T(1024)S(1)}, s32[4096]{0:T(1024)}, u32[]{:S(2)}) copy-start(s32[4096]{0:T(1024)} %param.20) | copy-start | bytes 49156
  62.1 14.7 %all-to-all-start.3 = ((bf16[8,48,512]{2,1,0:T(8,128)(2,1)}), bf16[8,48,512]{2,1,0:T(8,128)(2,1)S(1)}, u32[]{:S(2)}, u32[]{:S(2)}) async-start(bf16[8,48,512]{2,1,0:T(8,128)(2,1)} %bitcast.13), calls=%async_computation.3 | async-start | bytes 786432 | tf_op jit(solution)/shard_map/all_to_all | solution.py:428
  78.1 14.5 %all-to-all-start.4 = ((bf16[8,48,512]{2,1,0:T(8,128)(2,1)}), bf16[8,48,512]{2,1,0:T(8,128)(2,1)S(1)}, u32[]{:S(2)}, u32[]{:S(2)}) async-start(bf16[8,48,512]{2,1,0:T(8,128)(2,1)} %bitcast.34), calls=%async_computation.4 | async-start | bytes 786432 | tf_op jit(solution)/shard_map/all_to_all | solution.py:428
  92.5 11.4 %copy-start.14 = (bf16[320,512]{1,0:T(8,128)(2,1)S(1)}, bf16[320,512]{1,0:T(8,128)(2,1)}, u32[]{:S(2)}) copy-start(bf16[320,512]{1,0:T(8,128)(2,1)} %get-tuple-element.60.refs_2_) | copy-start | bytes 983044
  92.5 11.4 %copy-start.15 = (bf16[320,512]{1,0:T(8,128)(2,1)S(1)}, bf16[320,512]{1,0:T(8,128)(2,1)}, u32[]{:S(2)}) copy-start(bf16[320,512]{1,0:T(8,128)(2,1)} %get-tuple-element.61.refs_3_) | copy-start | bytes 983044
  93.3 10.6 %copy-start.1 = (bf16[8,48,512]{2,1,0:T(8,128)(2,1)S(1)}, bf16[8,48,512]{2,1,0:T(8,128)(2,1)}, u32[]{:S(2)}) copy-start(bf16[8,48,512]{2,1,0:T(8,128)(2,1)} %copy-done) | copy-start | bytes 1179652
  93.3 2.5 %collective-permute-start = (bf16[3,256,512]{2,1,0:T(8,128)(2,1)}, bf16[3,256,512]{2,1,0:T(8,128)(2,1)S(1)}, u32[]{:S(2)}, u32[]{:S(2)}) collective-permute-start(bf16[3,256,512]{2,1,0:T(8,128)(2,1)} %held.1), channel_id=1, source_target_pairs={{0,8},{8,0},{1,9},{9,1},{2,10},{10,2},{3,11},{11,3},{4,12},{12,4},... | collective-permute-start | bytes 2359304 | tf_op jit(solution)/shard_map/ppermute | solution.py:378
  96.9 27.7 %all-to-all-start.5 = ((bf16[16,48,512]{2,1,0:T(8,128)(2,1)}), bf16[16,48,512]{2,1,0:T(8,128)(2,1)S(1)}, u32[]{:S(2)}, u32[]{:S(2)}) async-start(bf16[16,48,512]{2,1,0:T(8,128)(2,1)} %parts.1.refs_9_), calls=%async_computation.5 | async-start | bytes 1572864 | tf_op jit(solution)/shard_map/all_to_all | solution.py:606
  149.3 2.3 %collective-permute-start.1 = (bf16[16,48,512]{2,1,0:T(8,128)(2,1)S(1)}, bf16[16,48,512]{2,1,0:T(8,128)(2,1)S(1)}, u32[]{:S(2)}, u32[]{:S(2)}) collective-permute-start(bf16[16,48,512]{2,1,0:T(8,128)(2,1)S(1)} %all_to_all.65.part_ref), channel_id=1, source_target_pairs={{0,8},{8,0},{1,9},{9,1},{2,10},{10,2},{3,11},{11,3},{4,12},{12,4},... | collective-permute-start | bytes 2359304 | tf_op jit(solution)/shard_map/ppermute | solution.py:378
  (7 other events, 27.9 us)

commit v8 on v7

--- a/solution.py
+++ b/solution.py
@@ -592,7 +592,7 @@
         + [pltpu.SemaphoreType.DMA((4,))] * 2,
         vmem=60,
     )
-    others = ("x", "mesh")
+    others = ("mesh", "x")
     count = lax.axis_size("x") * owners
     pieces = sds((count, 3 * half // count, width), BF16)
     (staged,) = call(stage_kernel, "stage", [sds((3, half, width), BF16)], [keep], half * width)

time: 154 us -> 154 us (level)
  no operation moved by 1% of the time
where the time goes in v8:
time: 154 us; the launch traced here: 153 us
  Pallas kernels  63.8 us (41%)
  starting transfers between devices  33.7 us (22%)
  blocking collectives  25 us (16%)
  waiting for transfers between devices  24 us (16%)
  local copies, waits for them, and re-layouts  5.02 us (3%)
    pallas_call x15, Pallas kernels, call(): pl.pallas_call(body, out_shape=out, in_specs=list(in_specs) + [pl.BlockSp...  61.5 us
    all_to_all x5, starting transfers between devices, exchange(): return lax.all_to_all(value, 'mesh', 0, 0, tiled=True)  26.7 us
    all_to_all x1, blocking collectives, shards(): mine = lax.all_to_all(copies, others, 0, 0, tiled=True)  25 us
    all_to_all x1, waiting for transfers between devices, shards(): summed = lax.all_to_all(parts, others, 0, 0, tiled=True)  17 us
    all_to_all x1, starting transfers between devices, shards(): summed = lax.all_to_all(parts, others, 0, 0, tiled=True)  7.02 us
    unnamed x47, local copies, waits for them, and re-layouts  4.94 us
    all_to_all x5, waiting for transfers between devices, exchange(): return lax.all_to_all(value, 'mesh', 0, 0, tiled=True)  4.68 us
  transfers between devices with their start and end apart: 8, of which 7 were waited for; matrix products, arithmetic and copies ran while one was open for 1% of the time, Pallas kernels for 29%

profile of v8, /device:TPU:0, one launch (start us, length us, event | category | flops | bytes accessed | tf_op | source)
XLA Modules:
  0.0 152.7 jit_solution(14589067459658507976)
XLA Ops:
  0.7 2.6 %prep.1 = (s32[32,128]{1,0:T(8,128)}, s32[8,128]{1,0:T(8,128)}) custom-call(s32[32,128]{1,0:T(8,128)} %bitcast.36), custom_call_target="tpu_custom_call" | custom-call | flops 1000000000 | bytes 36864 | tf_op jit(solution)/shard_map/prep/pallas_call | solution.py:67
  3.3 7.3 %all-to-all-start = ((s32[8,1,128]{2,1,0:T(1,128)}), s32[8,1,128]{2,1,0:T(1,128)S(1)}, u32[]{:S(2)}, u32[]{:S(2)}) async-start(s32[8,1,128]{2,1,0:T(1,128)} %bitcast.35), calls=%async_computation | async-start | bytes 8192 | tf_op jit(solution)/shard_map/all_to_all | solution.py:428
  10.6 1.2 copy.27.refs_0_
  12.6 2.2 %hidden.1 = (bf16[1024,512]{1,0:T(8,128)(2,1)}, s32[8,128]{1,0:T(8,128)S(1)}) custom-call(bf16[1024,227]{1,0:T(8,128)(2,1)S(1)} %copy.27.refs_0_, bf16[227,512]{1,0:T(8,128)(2,1)S(1)} %copy-done.17, f32[1,512]{1,0:T(1,128)S(1)} %bitcast.31, s32[32,128]{1,0:T(8,128)S(1)} %copy-done.21), custom_call_target="tpu_custom_call" | custom-call | flops 238026752 | bytes 1747968 | tf_op jit(solution)/shard_map/hidden/pallas_call | solution.py:67
  14.9 1.4 node_pre.1
  17.0 1.2 ask.1
  18.2 5.3 %all-to-all-start.1 = ((bf16[8,48,512]{2,1,0:T(8,128)(2,1)}), bf16[8,48,512]{2,1,0:T(8,128)(2,1)S(1)}, u32[]{:S(2)}, u32[]{:S(2)}) async-start(bf16[8,48,512]{2,1,0:T(8,128)(2,1)} %bitcast.8), calls=%async_computation.1 | async-start | bytes 786432 | tf_op jit(solution)/shard_map/all_to_all | solution.py:428
  23.6 9.7 %grid.1 = (bf16[512,1024]{1,0:T(8,128)(2,1)}, bf16[4096,512]{1,0:T(8,128)(2,1)}) custom-call(s32[32,128]{1,0:T(8,128)} %bitcast.29, bf16[1024,512]{1,0:T(8,128)(2,1)} %get-tuple-element.42.refs_1_, bf16[512,512]{1,0:T(8,128)(2,1)} %refs_2_.3, f32[1,512]{1,0:T(1,128)} %bitcast.37, bf16[512,512]{1,0:T(8,128)(2,1)} %refs_4_.4, ...), custom_call_target="tpu_custom_call" | custom-call | flops 5368709120 | bytes 7358464 | tf_op jit(solution)/shard_map/grid/pallas_call | solution.py:67
  33.3 1.3 all-to-all-done.1
  34.7 9.2 %edge.1 = (bf16[384,512]{1,0:T(8,128)(2,1)}, bf16[384,512]{1,0:T(8,128)(2,1)}, bf16[384,512]{1,0:T(8,128)(2,1)}) custom-call(s32[32,128]{1,0:T(8,128)S(1)} %copy-done.21, bf16[4096,512]{1,0:T(8,128)(2,1)} %get-tuple-element.47.refs_1_, bf16[384,512]{1,0:T(8,128)(2,1)S(1)} %bitcast.24, bf16[512,512]{1,0:T(8,128)(2,1)S(1)} %copy-done.10, ...), custom_call_target="tpu_custom_call" | custom-call | flops 3825205248 | bytes 6834176 | tf_op jit(solution)/shard_map/edge/pallas_call | solution.py:67
  43.9 4.6 %all-to-all-start.2 = ((bf16[8,48,512]{2,1,0:T(8,128)(2,1)}), bf16[8,48,512]{2,1,0:T(8,128)(2,1)S(1)}, u32[]{:S(2)}, u32[]{:S(2)}) async-start(bf16[8,48,512]{2,1,0:T(8,128)(2,1)} %bitcast.11), calls=%async_computation.2 | async-start | bytes 786432 | tf_op jit(solution)/shard_map/all_to_all | solution.py:428
  48.6 9.0 %slope.1 = (bf16[4096,512]{1,0:T(8,128)(2,1)}, f32[384,512]{1,0:T(8,128)}) custom-call(s32[32,128]{1,0:T(8,128)} %get-tuple-element.41.refs_3_.refs_0_, bf16[4096,512]{1,0:T(8,128)(2,1)} %get-tuple-element.47.refs_1_, bf16[384,512]{1,0:T(8,128)(2,1)} %get-tuple-element.52.refs_2_, f32[1,512]{1,0:T(1,128)} %bitcast.32, bf16[384,512]{1,0:T(8,128)(2,1)} %get-tuple-element.48.refs_4_), custom_call_target="tpu_custom_call" | custom-call | flops 3221225472 | bytes 9586688 | tf_op jit(solution)/shard_map/slope/pallas_call | solution.py:67
  57.7 1.4 all-to-all-done.2
  59.1 3.0 %node.1 = (bf16[384,512]{1,0:T(8,128)(2,1)}, bf16[320,512]{1,0:T(8,128)(2,1)}, bf16[320,512]{1,0:T(8,128)(2,1)}) custom-call(bf16[384,512]{1,0:T(8,128)(2,1)S(1)} %bitcast.21, s32[1,384]{1,0:T(1,128)S(1)} %reshape.47.refs_1_, bf16[384,320]{1,0:T(8,128)(2,1)S(1)} %get-tuple-element.49.refs_2_, f32[320,512]{1,0:T(8,128)} %get-tuple-element.50.refs_3_, ...), custom_call_target="tpu_custom_call" | custom-call | flops 587202560 | bytes 3524096 | tf_op jit(solution)/shard_map/node/pallas_call | solution.py:67
  62.1 4.7 %all-to-all-start.3 = ((bf16[8,48,512]{2,1,0:T(8,128)(2,1)}), bf16[8,48,512]{2,1,0:T(8,128)(2,1)S(1)}, u32[]{:S(2)}, u32[]{:S(2)}) async-start(bf16[8,48,512]{2,1,0:T(8,128)(2,1)} %bitcast.13), calls=%async_computation.3 | async-start | bytes 786432 | tf_op jit(solution)/shard_map/all_to_all | solution.py:428
  67.8 7.8 %take_latent.1 = (bf16[512,4096]{1,0:T(8,128)(2,1)}, bf16[512,384]{1,0:T(8,128)(2,1)}, bf16[512,384]{1,0:T(8,128)(2,1)}, s32[8,128]{1,0:T(8,128)S(1)}) custom-call(s32[32,128]{1,0:T(8,128)S(1)} %bitcast.30, bf16[512,1024]{1,0:T(8,128)(2,1)} %get-tuple-element.56.refs_1_, bf16[384,512]{1,0:T(8,128)(2,1)S(1)} %copy-done.22, bf16[384,512]{1,0:T(8,128)(2,1)S(1)} %bitcast.25, ...), custom_call_target="tpu_custom_call" | custom-call | flops 4294967296 | bytes 6832128 | tf_op jit(solution)/shard_map/take_latent/pallas_call | solution.py:67
  76.8 1.3 slot_grad.1
  78.1 4.8 %all-to-all-start.4 = ((bf16[8,48,512]{2,1,0:T(8,128)(2,1)}), bf16[8,48,512]{2,1,0:T(8,128)(2,1)S(1)}, u32[]{:S(2)}, u32[]{:S(2)}) async-start(bf16[8,48,512]{2,1,0:T(8,128)(2,1)} %bitcast.34), calls=%async_computation.4 | async-start | bytes 786432 | tf_op jit(solution)/shard_map/all_to_all | solution.py:428
  82.9 9.6 %edge_back.1 = (bf16[3,256,512]{2,1,0:T(8,128)(2,1)}, bf16[3,256,512]{2,1,0:T(8,128)(2,1)}) custom-call(s32[32,128]{1,0:T(8,128)} %get-tuple-element.41.refs_3_.refs_0_, bf16[4096,512]{1,0:T(8,128)(2,1)} %get-tuple-element.53.refs_6_.refs_1_, bf16[512,4096]{1,0:T(8,128)(2,1)} %get-tuple-element.62.refs_2_, bf16[384,512]{1,0:T(8,128)(2,1)} %get-tuple-element.63.refs_3_, ...), custom_call_target="tpu_custom_call" | custom-call | flops 4160749568 | bytes 11943936 | tf_op jit(solution)/shard_map/edge_back/pallas_call | solution.py:67
  94.6 1.3 collective-permute-done.refs_1_
  96.9 7.0 %all-to-all-start.5 = ((bf16[16,48,512]{2,1,0:T(8,128)(2,1)}), bf16[16,48,512]{2,1,0:T(8,128)(2,1)S(1)}, u32[]{:S(2)}, u32[]{:S(2)}) async-start(bf16[16,48,512]{2,1,0:T(8,128)(2,1)} %parts.1.refs_9_), calls=%async_computation.5 | async-start | bytes 1572864 | tf_op jit(solution)/shard_map/all_to_all | solution.py:606
  103.9 2.9 %node_post.1 = (bf16[320,512]{1,0:T(8,128)(2,1)}, bf16[320,512]{1,0:T(8,128)(2,1)}, s32[8,128]{1,0:T(8,128)S(1)}) custom-call(bf16[384,512]{1,0:T(8,128)(2,1)S(1)} %bitcast.20, s32[1,384]{1,0:T(1,128)S(1)} %reshape.47.refs_1_, bf16[320,512]{1,0:T(8,128)(2,1)S(1)} %copy-done.14, bf16[320,512]{1,0:T(8,128)(2,1)S(1)} %copy-done.15, ...), custom_call_target="tpu_custom_call" | custom-call | flops 629145600 | bytes 3933696 | tf_op jit(solution)/shard_map/node_post/pallas_call | solution.py:67
  106.9 17.0 %all-to-all-done.5.refs_0_ = bf16[16,48,512]{2,1,0:T(8,128)(2,1)S(1)} async-done(((bf16[16,48,512]{2,1,0:T(8,128)(2,1)}), bf16[16,48,512]{2,1,0:T(8,128)(2,1)S(1)}, u32[]{:S(2)}, u32[]{:S(2)}) %all-to-all-start.5) | async-done | bytes 786464 | tf_op jit(solution)/shard_map/all_to_all | solution.py:606
  124.0 25.0 %all_to_all.65.part_ref = bf16[16,48,512]{2,1,0:T(8,128)(2,1)S(1)} all-to-all(bf16[16,48,512]{2,1,0:T(8,128)(2,1)S(1)} %spread.1), channel_id=1, replica_groups=mesh['x'=2,'core'=2,'mesh'=8] {'mesh','x'}, dimensions={0} | all-to-all | bytes 1572864 | tf_op jit(solution)/shard_map/all_to_all | solution.py:629
  (59 shorter events, 10.4 us)
Async XLA Ops:
  0.6 11.2 %copy-start.19 = (f32[512]{0:T(512)S(1)}, f32[512]{0:T(512)}, u32[]{:S(2)}) copy-start(f32[512]{0:T(512)} %param.23) | copy-start | bytes 6148
  0.6 11.2 %copy-start.17 = (bf16[227,512]{1,0:T(8,128)(2,1)S(1)}, bf16[227,512]{1,0:T(8,128)(2,1)}, u32[]{:S(2)}) copy-start(bf16[227,512]{1,0:T(8,128)(2,1)} %refs_1_.4) | copy-start | bytes 697348
  0.7 14.2 %copy-start.16 = (f32[512]{0:T(512)S(1)}, f32[512]{0:T(512)}, u32[]{:S(2)}) copy-start(f32[512]{0:T(512)} %param.32) | copy-start | bytes 6148
  0.7 14.2 %copy-start.5 = (bf16[320,512]{1,0:T(8,128)(2,1)S(1)}, bf16[320,512]{1,0:T(8,128)(2,1)}, u32[]{:S(2)}) copy-start(bf16[320,512]{1,0:T(8,128)(2,1)} %refs_4_.5) | copy-start | bytes 983044
  0.7 14.2 %copy-start.6 = (bf16[320,512]{1,0:T(8,128)(2,1)S(1)}, bf16[320,512]{1,0:T(8,128)(2,1)}, u32[]{:S(2)}) copy-start(bf16[320,512]{1,0:T(8,128)(2,1)} %refs_5_.5) | copy-start | bytes 983044
  0.7 14.2 %copy-start.2 = (bf16[512,512]{1,0:T(8,128)(2,1)S(1)}, bf16[512,512]{1,0:T(8,128)(2,1)}, u32[]{:S(2)}) copy-start(bf16[512,512]{1,0:T(8,128)(2,1)} %refs_7_.1) | copy-start | bytes 1572868
  0.7 14.2 %copy-start.3 = (bf16[512,512]{1,0:T(8,128)(2,1)S(1)}, bf16[512,512]{1,0:T(8,128)(2,1)}, u32[]{:S(2)}) copy-start(bf16[512,512]{1,0:T(8,128)(2,1)} %refs_6_.1) | copy-start | bytes 1572868
  3.3 13.7 %all-to-all-start = ((s32[8,1,128]{2,1,0:T(1,128)}), s32[8,1,128]{2,1,0:T(1,128)S(1)}, u32[]{:S(2)}, u32[]{:S(2)}) async-start(s32[8,1,128]{2,1,0:T(1,128)} %bitcast.35), calls=%async_computation | async-start | bytes 8192 | tf_op jit(solution)/shard_map/all_to_all | solution.py:428
  18.2 16.4 %all-to-all-start.1 = ((bf16[8,48,512]{2,1,0:T(8,128)(2,1)}), bf16[8,48,512]{2,1,0:T(8,128)(2,1)S(1)}, u32[]{:S(2)}, u32[]{:S(2)}) async-start(bf16[8,48,512]{2,1,0:T(8,128)(2,1)} %bitcast.8), calls=%async_computation.1 | async-start | bytes 786432 | tf_op jit(solution)/shard_map/all_to_all | solution.py:428
  23.5 11.1 %copy-start.10 = (bf16[512,512]{1,0:T(8,128)(2,1)S(1)}, bf16[512,512]{1,0:T(8,128)(2,1)}, u32[]{:S(2)}) copy-start(bf16[512,512]{1,0:T(8,128)(2,1)} %refs_8_.1) | copy-start | bytes 1572868
  23.5 11.1 %copy-start.11 = (bf16[512,512]{1,0:T(8,128)(2,1)S(1)}, bf16[512,512]{1,0:T(8,128)(2,1)}, u32[]{:S(2)}) copy-start(bf16[512,512]{1,0:T(8,128)(2,1)} %refs_1_.7) | copy-start | bytes 1572868
  23.6 11.1 %copy-start.20 = (f32[512]{0:T(512)S(1)}, f32[512]{0:T(512)}, u32[]{:S(2)}) copy-start(f32[512]{0:T(512)} %param.28) | copy-start | bytes 6148
  34.6 9.2 %copy-start.12 = (bf16[8,48,512]{2,1,0:T(8,128)(2,1)}, bf16[8,48,512]{2,1,0:T(8,128)(2,1)S(1)}, u32[]{:S(2)}) copy-start(bf16[8,48,512]{2,1,0:T(8,128)(2,1)S(1)} %all-to-all-done.1) | copy-start | bytes 1179652
  43.9 15.2 %all-to-all-start.2 = ((bf16[8,48,512]{2,1,0:T(8,128)(2,1)}), bf16[8,48,512]{2,1,0:T(8,128)(2,1)S(1)}, u32[]{:S(2)}, u32[]{:S(2)}) async-start(bf16[8,48,512]{2,1,0:T(8,128)(2,1)} %bitcast.11), calls=%async_computation.2 | async-start | bytes 786432 | tf_op jit(solution)/shard_map/all_to_all | solution.py:428
  48.6 10.5 %copy-start.9 = (bf16[512,512]{1,0:T(8,128)(2,1)S(1)}, bf16[512,512]{1,0:T(8,128)(2,1)}, u32[]{:S(2)}) copy-start(bf16[512,512]{1,0:T(8,128)(2,1)} %refs_5_.4) | copy-start | bytes 1572868
  57.7 9.1 %copy-start.18 = (s32[4096]{0:T(1024)S(1)}, s32[4096]{0:T(1024)}, u32[]{:S(2)}) copy-start(s32[4096]{0:T(1024)} %param.20) | copy-start | bytes 49156
  62.1 14.7 %all-to-all-start.3 = ((bf16[8,48,512]{2,1,0:T(8,128)(2,1)}), bf16[8,48,512]{2,1,0:T(8,128)(2,1)S(1)}, u32[]{:S(2)}, u32[]{:S(2)}) async-start(bf16[8,48,512]{2,1,0:T(8,128)(2,1)} %bitcast.13), calls=%async_computation.3 | async-start | bytes 786432 | tf_op jit(solution)/shard_map/all_to_all | solution.py:428
  78.1 14.5 %all-to-all-start.4 = ((bf16[8,48,512]{2,1,0:T(8,128)(2,1)}), bf16[8,48,512]{2,1,0:T(8,128)(2,1)S(1)}, u32[]{:S(2)}, u32[]{:S(2)}) async-start(bf16[8,48,512]{2,1,0:T(8,128)(2,1)} %bitcast.34), calls=%async_computation.4 | async-start | bytes 786432 | tf_op jit(solution)/shard_map/all_to_all | solution.py:428
  92.5 11.4 %copy-start.14 = (bf16[320,512]{1,0:T(8,128)(2,1)S(1)}, bf16[320,512]{1,0:T(8,128)(2,1)}, u32[]{:S(2)}) copy-start(bf16[320,512]{1,0:T(8,128)(2,1)} %get-tuple-element.60.refs_2_) | copy-start | bytes 983044
  92.5 11.4 %copy-start.15 = (bf16[320,512]{1,0:T(8,128)(2,1)S(1)}, bf16[320,512]{1,0:T(8,128)(2,1)}, u32[]{:S(2)}) copy-start(bf16[320,512]{1,0:T(8,128)(2,1)} %get-tuple-element.61.refs_3_) | copy-start | bytes 983044
  93.3 10.6 %copy-start.1 = (bf16[8,48,512]{2,1,0:T(8,128)(2,1)S(1)}, bf16[8,48,512]{2,1,0:T(8,128)(2,1)}, u32[]{:S(2)}) copy-start(bf16[8,48,512]{2,1,0:T(8,128)(2,1)} %copy-done) | copy-start | bytes 1179652
  93.3 2.5 %collective-permute-start = (bf16[3,256,512]{2,1,0:T(8,128)(2,1)}, bf16[3,256,512]{2,1,0:T(8,128)(2,1)S(1)}, u32[]{:S(2)}, u32[]{:S(2)}) collective-permute-start(bf16[3,256,512]{2,1,0:T(8,128)(2,1)} %held.1), channel_id=1, source_target_pairs={{0,8},{8,0},{1,9},{9,1},{2,10},{10,2},{3,11},{11,3},{4,12},{12,4},... | collective-permute-start | bytes 2359304 | tf_op jit(solution)/shard_map/ppermute | solution.py:378
  96.9 27.0 %all-to-all-start.5 = ((bf16[16,48,512]{2,1,0:T(8,128)(2,1)}), bf16[16,48,512]{2,1,0:T(8,128)(2,1)S(1)}, u32[]{:S(2)}, u32[]{:S(2)}) async-start(bf16[16,48,512]{2,1,0:T(8,128)(2,1)} %parts.1.refs_9_), calls=%async_computation.5 | async-start | bytes 1572864 | tf_op jit(solution)/shard_map/all_to_all | solution.py:606
  149.0 2.3 %collective-permute-start.1 = (bf16[16,48,512]{2,1,0:T(8,128)(2,1)S(1)}, bf16[16,48,512]{2,1,0:T(8,128)(2,1)S(1)}, u32[]{:S(2)}, u32[]{:S(2)}) collective-permute-start(bf16[16,48,512]{2,1,0:T(8,128)(2,1)S(1)} %all_to_all.65.part_ref), channel_id=1, source_target_pairs={{0,8},{8,0},{1,9},{9,1},{2,10},{10,2},{3,11},{11,3},{4,12},{12,4},... | collective-permute-start | bytes 2359304 | tf_op jit(solution)/shard_map/ppermute | solution.py:378
  (7 other events, 27.9 us)
